TPU v7x, 32 devices: a whole 2x2x4 slice. The times are simulated.
32 devices in a mesh: groups: 2 (over y), dp: 4 (over x, core), fsdp: 4 (over z).
Axes of the slice: x: 2, y: 2, z: 4, core: 2. Of those that a mesh axis runs over, the one named last changes fastest.
Arguments:
- input_rows: bfloat16 [2560, 6144], P(('groups', 'dp'), 'fsdp'), parts along dimension 0, may hold values from -6 to 6
- cotangent: bfloat16 [1280, 16384], P(('groups', 'dp'), 'fsdp'), parts along dimension 0, may hold values from -1.5 to 1.5
- frozen_weight: bfloat16 [6144, 16384], P(None, 'fsdp'), may hold values from -0.078125 to 0.078125
- adapter_down_weight: bfloat16 [64, 6144, 64], P('groups', 'fsdp'), parts along dimension 0, may hold values from -0.078125 to 0.078125
- adapter_up_weight: bfloat16 [64, 64, 16384], P('groups', None, 'fsdp'), parts along dimension 0, may hold values from -0.75 to 0.75
- tenant_row_counts: int32 [8, 32], P('groups'), parts along dimension 0, may hold values from 0 to 160, as said below
- handoff_counts: int32 [8, 4], P('groups'), parts along dimension 0, may hold values from 0 to 160, as said below
- tenant_gradient_slot: int32 [64], P('groups'), parts along dimension 0, may hold values from 0 to 31, each once
Outputs:
- outputs: bfloat16 [1280, 16384], P(('groups', 'dp'), 'fsdp'), parts along dimension 0
- row_grad: bfloat16 [2560, 6144], P(('groups', 'dp'), 'fsdp'), parts along dimension 0
- grad_a: bfloat16 [64, 6144, 64], P(('groups', 'dp'), 'fsdp'), parts along dimension 0
- grad_b: bfloat16 [64, 64, 16384], P(('groups', 'dp'), None, 'fsdp'), parts along dimension 0
There are 2 independent parts, one for each index of `groups`. A program takes and returns all parts, laid end to end along the dimension named above; an argument that names none is the same for every part. Nothing has to cross between parts.
Inputs may be any that keep to these rules, and one draw needn't show every extreme that they name: A group's rows of input_rows are its first (sum of its row of tenant_row_counts) rows, tenant 0's first, then tenant 1's and so on; the other rows are unused. One group holds 320 rows in every draw, and one tenant of that group holds exactly 160 of them. `handoff_counts`: row i sums to group i's rows (the sum of row i of tenant_row_counts); every column sums to 160. Group i hands its rows out in order: the first S[i, 0] to group 0, the next S[i, 1] to group 1, and so on (the diagonal entry counts the rows it keeps). Off the diagonal an entry is at most 80, and some entry reaches it in every draw; some diagonal entry is 160 in every draw. `tenant_gradient_slot`: each slot once; slot s belongs to data group s // 8.
All inputs are finite; a program needn't handle non-finite values.
Results may differ from a plain program's by a relative error of at most 0.01.
Values may be sent and summed in bfloat16 or wider, within the bound.
No kernel may reach another device: no remote copies, remote signals or barrier semaphores. Data moves between devices by JAX's collectives and lax.ppermute only.
A program may use at most 256 MiB of HBM per device.

v0:
```python
import jax
import jax.numpy as jnp
from jax import lax
from jax.sharding import PartitionSpec as P

adapter_scale = 0.25


def before_sums(values, group_axis):
    return jnp.cumsum(values, axis=group_axis) - values


def find_source(starts, counts, length):
    places = jnp.arange(length, dtype=jnp.int32)[:, None]
    inside = (places >= starts[None, :]) & (places < (starts + counts)[None, :])
    numbers = jnp.arange(starts.shape[0], dtype=jnp.int32)[None, :]
    source = jnp.sum(jnp.where(inside, numbers, 0), axis=1)
    offset = places[:, 0] - jnp.sum(jnp.where(inside, starts[None, :], 0), axis=1)
    present = jnp.any(inside, axis=1)
    return (source, offset, present)


def pack_slots(values, starts, counts, width, allowed):
    places = jnp.arange(width, dtype=jnp.int32)[None, :]
    picked = jnp.minimum(starts[:, None] + places, values.shape[0] - 1)
    valid = (places < counts[:, None]) & allowed[:, None]
    taken = jnp.take(values, picked.reshape(-1), axis=0).reshape(
        counts.shape[0], width, values.shape[1]
    )
    return jnp.where(valid[:, :, None], taken, jnp.zeros((), values.dtype))


def body(
    input_rows,
    cotangent,
    frozen_weight,
    adapter_down_weight,
    adapter_up_weight,
    tenant_row_counts,
    handoff_counts,
    tenant_gradient_slot,
):
    groups = lax.axis_size("dp")
    mine = lax.axis_index("dp")
    balanced_rows = cotangent.shape[0]
    capacity = input_rows.shape[0]
    feature_width = input_rows.shape[1]
    column_index = cotangent.shape[1]
    tenant_labels = adapter_up_weight.shape[0]
    group_position = adapter_up_weight.shape[1]
    sent_before = before_sums(handoff_counts, 1)
    recv_before = before_sums(handoff_counts, 0)
    my_sends = handoff_counts[mine]
    my_send_starts = sent_before[mine]
    my_recvs = handoff_counts[:, mine]
    my_recv_starts = recv_before[:, mine]
    others = jnp.arange(groups, dtype=jnp.int32) != mine
    source, offset, present = find_source(my_recv_starts, my_recvs, balanced_rows)
    source_row = sent_before[source, mine] + offset
    tenant_end = jnp.cumsum(tenant_row_counts, axis=1)
    row_tenant = jnp.sum(
        (jnp.take(tenant_end, source, axis=0) <= source_row[:, None]).astype(jnp.int32), axis=1
    )
    tenant_onehot = (
        row_tenant[:, None] == jnp.arange(tenant_labels, dtype=jnp.int32)[None, :]
    ).astype(jnp.bfloat16)
    half_slot = balanced_rows // 2
    outgoing = pack_slots(input_rows, my_send_starts, my_sends, half_slot, others)
    arrived = lax.all_to_all(outgoing, "dp", split_axis=0, concat_axis=0, tiled=True)
    pool = jnp.concatenate([arrived.reshape(groups * half_slot, feature_width), input_rows], axis=0)
    picked = jnp.where(source == mine, groups * half_slot + source_row, source * half_slot + offset)
    group_rows = jnp.take(pool, jnp.minimum(picked, pool.shape[0] - 1), axis=0)
    frozen_output = jnp.dot(
        lax.all_gather(group_rows, "fsdp", axis=1, tiled=True),
        frozen_weight,
        preferred_element_type=jnp.float32,
    )
    lowered_gathered = jnp.einsum(
        "ai,wiv->awv", group_rows, adapter_down_weight, preferred_element_type=jnp.float32
    )
    backward_gathered = jnp.einsum(
        "ku,wxu->kwx", cotangent, adapter_up_weight, preferred_element_type=jnp.float32
    )
    hot_wide = tenant_onehot.astype(jnp.float32)[:, :, None]
    down_part = jnp.sum(lowered_gathered * hot_wide, axis=1)
    back_part = jnp.sum(backward_gathered * hot_wide, axis=1)
    lowered_total, backward_total = lax.psum((down_part, back_part), "fsdp")
    adapter_input = lowered_total.astype(jnp.bfloat16)
    adapter_gradient = (adapter_scale * backward_total).astype(jnp.bfloat16)
    scattered_input = (tenant_onehot[:, :, None] * adapter_input[:, None, :]).reshape(
        balanced_rows, tenant_labels * group_position
    )
    scattered_gradient = (tenant_onehot[:, :, None] * adapter_gradient[:, None, :]).reshape(
        balanced_rows, tenant_labels * group_position
    )
    adapter_output = jnp.dot(
        scattered_input,
        adapter_up_weight.reshape(tenant_labels * group_position, column_index),
        preferred_element_type=jnp.float32,
    )
    adapter_backward = lax.dot_general(
        scattered_gradient,
        adapter_down_weight.transpose(1, 0, 2).reshape(
            feature_width, tenant_labels * group_position
        ),
        (((1,), (1,)), ((), ())),
        preferred_element_type=jnp.float32,
    )
    outputs = (frozen_output + adapter_scale * adapter_output).astype(jnp.bfloat16)
    grad_terms = lax.dot_general(
        cotangent, frozen_weight, (((1,), (1,)), ((), ())), preferred_element_type=jnp.float32
    )
    frozen_gradient = lax.psum_scatter(grad_terms, "fsdp", scatter_dimension=1, tiled=True)
    group_gradient = (frozen_gradient + adapter_backward).astype(jnp.bfloat16)
    part_a = lax.dot_general(
        group_rows, scattered_gradient, (((0,), (0,)), ((), ())), preferred_element_type=jnp.float32
    )
    part_a = part_a.reshape(feature_width, tenant_labels, group_position).transpose(1, 0, 2)
    partial_up = adapter_scale * lax.dot_general(
        scattered_input, cotangent, (((0,), (0,)), ((), ())), preferred_element_type=jnp.float32
    )
    partial_up = partial_up.reshape(tenant_labels, group_position, column_index)
    order = jnp.argsort(tenant_gradient_slot)
    share = tenant_labels // groups
    owner_a = (
        jnp.take(part_a, order, axis=0)
        .astype(jnp.bfloat16)
        .reshape(groups, share, feature_width, group_position)
    )
    owner_b = (
        jnp.take(partial_up, order, axis=0)
        .astype(jnp.bfloat16)
        .reshape(groups, share, group_position, column_index)
    )
    source_home, offset_home, present_home = find_source(my_send_starts, my_sends, capacity)
    half_slot = balanced_rows // 2
    back_slots = pack_slots(group_gradient, my_recv_starts, my_recvs, half_slot, others)
    home, sums_a, sums_b = (
        lax.all_to_all(back_slots, "dp", split_axis=0, concat_axis=0, tiled=True),
        lax.all_to_all(owner_a, "dp", split_axis=0, concat_axis=0, tiled=True),
        lax.all_to_all(owner_b, "dp", split_axis=0, concat_axis=0, tiled=True),
    )
    pool_home = jnp.concatenate(
        [home.reshape(groups * half_slot, feature_width), group_gradient], axis=0
    )
    picked_home = jnp.where(
        source_home == mine,
        groups * half_slot + recv_before[mine, mine] + offset_home,
        source_home * half_slot + offset_home,
    )
    row_grad = jnp.take(pool_home, jnp.minimum(picked_home, pool_home.shape[0] - 1), axis=0)
    row_grad = jnp.where(present_home[:, None], row_grad, jnp.zeros((), jnp.bfloat16))
    grad_a = jnp.sum(sums_a.astype(jnp.float32), axis=0).astype(jnp.bfloat16)
    grad_b = jnp.sum(sums_b.astype(jnp.float32), axis=0).astype(jnp.bfloat16)
    return (outputs, row_grad, grad_a, grad_b)


def solution(mesh):
    placed = (
        P(("groups", "dp"), "fsdp"),
        P(("groups", "dp"), "fsdp"),
        P(None, "fsdp"),
        P("groups", "fsdp", None),
        P("groups", None, "fsdp"),
        P("groups", None),
        P("groups", None),
        P("groups"),
    )
    return jax.shard_map(
        body,
        mesh=mesh,
        in_specs=placed,
        out_specs=(
            P(("groups", "dp"), "fsdp"),
            P(("groups", "dp"), "fsdp"),
            P(("groups", "dp"), "fsdp", None),
            P(("groups", "dp"), None, "fsdp"),
        ),
        check_vma=False,
    )
```

profile of v0, /device:TPU:0, one launch (start us, length us, event | category | flops | bytes accessed | tf_op | source)
XLA Modules:
  0.0 419.9 jit_solution(15626134767676327123)
XLA Ops:
  7.2 0.0 copy-start
  7.2 0.8 reduce_window_sum.33
  8.0 0.9 reduce_window_sum.34
  8.9 0.9 dynamic-slice_reduce_fusion
  9.7 0.7 fusion.37
  10.4 0.7 add_bitcast_fusion
  11.1 0.1 add_minimum_fusion.1
  11.2 0.1 compare_and_fusion.4
  11.2 0.1 min.82
  11.4 5.0 %gather_fusion.1 = bf16[320,1536]{1,0:T(8,128)(2,1)S(1)} fusion(bf16[320,1536]{1,0:T(8,128)(2,1)} %param.8, s32[1024]{0:T(1024)S(1)} %pad_clamp_fusion.5), kind=kCustom, calls=%fused_computation.1 | custom fusion | bytes 1967360 | tf_op jit(solution)/shard_map/jit(_take)/gather | solution.py:27
  16.4 0.1 fusion.26
  16.5 1.1 select_select_fusion.2
  17.6 4.2 %all-to-all-start = ((bf16[4,80,1536]{2,1,0:T(8,128)(2,1)}), bf16[4,80,1536]{2,1,0:T(8,128)(2,1)S(1)}, u32[]{:S(2)}, u32[]{:S(2)}) async-start(bf16[4,80,1536]{2,1,0:T(8,128)(2,1)} %select_select_fusion.2), calls=%async_computation | async-start | bytes 1966080 | tf_op jit(solution)/shard_map/all_to_all | solution.py:69
  21.8 24.1 %fusion.40 = f32[160,6144]{1,0:T(8,128)} fusion(bf16[160,4096]{1,0:T(8,128)(2,1)S(1)} %copy-done, bf16[6144,4096]{1,0:T(8,128)(2,1)} %param.10), kind=kOutput, calls=%fused_computation.109 | convolution fusion | flops 8053063680 | bytes 55574528 | tf_op jit(solution)/shard_map/dot_general | solution.py:110
  45.9 0.0 reduce-scatter.2.cloned.1.call-update
  45.9 0.2 dynamic-slice_reduce_fusion.1
  46.1 0.1 select_reduce_fusion.2
  46.2 2.0 gather_fusion
  48.3 1.6 sort.17
  49.9 0.2 reduce_window_sum.35
  50.1 0.7 gather_fusion.3
  50.8 0.2 convert_reduce_fusion
  51.1 0.1 broadcast_in_dim.175
  51.2 9.1 %multiply_reduce_fusion = f32[160,64]{0,1:T(8,128)S(1)} fusion(bf16[32,64,4096]{2,1,0:T(8,128)(2,1)} %param.12, bf16[160,4096]{1,0:T(8,128)(2,1)S(1)} %copy-done, f32[160,32]{0,1:T(8,128)S(1)} %get-tuple-element.20), kind=kOutput, calls=%fused_computation.21 | convolution fusion | flops 2684999680 | bytes 18149376 | tf_op jit(solution)/shard_map/ku,wxu->kwx/dot_general | solution.py:81
  60.3 1.4 pad_maximum_fusion
  61.7 3.2 gather_fusion.2
  65.0 0.1 broadcast_select_fusion
  65.1 0.0 copy-start.4
  65.1 4.8 %fusion.39 = f32[160,2048]{0,1:S(1)} fusion(bf16[160,1536]{1,0:T(8,128)(2,1)S(1)} %broadcast_select_fusion, bf16[1536,2048]{0,1:T(8,128)(2,1)} %bitcast.75), kind=kOutput, calls=%fused_computation.108 | convolution fusion | flops 1006632960 | bytes 8093696
  69.9 0.3 multiply_reduce_fusion.1
  70.2 27.4 %all-reduce.1 = (bf16[160,64]{0,1:T(8,128)(2,1)S(1)}, f32[160,64]{0,1:T(8,128)S(1)}) all-reduce(f32[160,64]{0,1:T(8,128)S(1)} %multiply_reduce_fusion.1, f32[160,64]{0,1:T(8,128)S(1)} %multiply_reduce_fusion), channel_id=1, replica_groups=mesh['groups'=2,'dp'=4,'fsdp'=4] {'fsdp'}, use_global_device_ids=true, to_apply=%region_7.8 | all-reduce | flops 20480 | bytes 143360 | tf_op jit(solution)/shard_map/psum | solution.py:87
  97.7 4.4 %convolution_bitcast_fusion = bf16[32,1536,64]{1,2,0:T(8,128)(2,1)} fusion(bf16[160,64]{0,1:T(8,128)(2,1)S(1)} %multiply_convert_fusion, bf16[160,32]{0,1:T(8,128)(2,1)S(1)} %get-tuple-element.19, bf16[160,1536]{1,0:T(8,128)(2,1)S(1)} %broadcast_select_fusion), kind=kOutput, calls=%fused_computation.11 | convolution fusion | flops 1007943680 | bytes 6813696 | tf_op jit(solution)/shard_map/dot_general | solution.py:115
  102.1 6.4 %gather_fusion.6 = bf16[32,1536,64]{1,2,0:T(8,128)(2,1)} fusion(bf16[32,1536,64]{1,2,0:T(8,128)(2,1)} %convolution_bitcast_fusion, s32[1024]{0:T(1024)S(1)} %pad_clamp_fusion), kind=kCustom, calls=%fused_computation.6 | custom fusion | bytes 12583040 | tf_op jit(solution)/shard_map/jit(_take)/gather | solution.py:126
  108.5 7.3 %select_convert_fusion.1 = bf16[4,8,1536,64]{2,3,1,0:T(8,128)(2,1)} fusion(bf16[4,8,1536,64]{2,3,1,0:T(8,128)(2,1)} %bitcast.74, pred[4,8]{1,0:T(4,128)(4,1)S(1)} %broadcast_in_dim.175), kind=kLoop, calls=%fused_computation.10 | loop fusion | flops 3145728 | bytes 12582944 | tf_op jit(solution)/shard_map/convert_element_type | solution.py:127
  115.8 5.2 %all-to-all-start.2 = ((bf16[4,8,1536,64]{2,3,1,0:T(8,128)(2,1)}), bf16[4,8,1536,64]{2,3,1,0:T(8,128)(2,1)}, u32[]{:S(2)}, u32[]{:S(2)}) async-start(bf16[4,8,1536,64]{2,3,1,0:T(8,128)(2,1)} %select_convert_fusion.1), calls=%async_computation.3 | async-start | bytes 12582912 | tf_op jit(solution)/shard_map/all_to_all | solution.py:140
  121.1 0.1 add_minimum_fusion
  121.1 0.1 min.89
  121.3 0.1 compare_and_fusion.1
  121.3 0.1 broadcast_multiply_fusion.1
  121.4 8.1 %broadcast_multiply_fusion = bf16[2048,4096]{1,0:T(8,128)(2,1)} fusion(bf16[160,2048]{0,1:T(8,128)(2,1)S(1)} %bitcast.83, bf16[160,4096]{1,0:T(8,128)(2,1)S(1)} %copy-done), kind=kOutput, calls=%fused_computation.9 | convolution fusion | flops 2701131776 | bytes 18743296 | tf_op jit(solution)/shard_map/dot_general | solution.py:119
  129.5 13.0 %gather_fusion.7 = bf16[32,64,4096]{2,1,0:T(8,128)(2,1)} fusion(bf16[32,64,4096]{2,1,0:T(8,128)(2,1)} %bitcast.76, s32[1024]{0:T(1024)S(1)} %pad_clamp_fusion), kind=kCustom, calls=%fused_computation.7 | custom fusion | bytes 33554560 | tf_op jit(solution)/shard_map/jit(_take)/gather | solution.py:131
  142.5 4.2 %fusion.11 = bf16[160,1536]{1,0:T(8,128)(2,1)S(1)} fusion(f32[160,1536]{1,0:T(8,128)} %reduce-scatter.2.cloned.1.call-done, bf16[32,1536,64]{1,2,0:T(8,128)(2,1)} %param.11, bf16[160,64]{0,1:T(8,128)(2,1)S(1)} %multiply_convert_fusion, bf16[160,32]{0,1:T(8,128)(2,1)S(1)} %get-tuple-element.19), kind=kOutput, calls=%fused_computation.20 | convolution fusion | flops 1007452160 | bytes 7796736 | tf_op jit(solution)/shard_map/dot_general | solution.py:101
  146.7 2.2 gather_fusion.4
  149.0 1.1 select_select_fusion.1
  150.1 41.7 %all-to-all-done.2 = bf16[4,8,1536,64]{2,3,1,0:T(8,128)(2,1)} async-done(((bf16[4,8,1536,64]{2,3,1,0:T(8,128)(2,1)}), bf16[4,8,1536,64]{2,3,1,0:T(8,128)(2,1)}, u32[]{:S(2)}, u32[]{:S(2)}) %all-to-all-start.2) | async-done | bytes 6291488 | tf_op jit(solution)/shard_map/all_to_all | solution.py:140
  191.8 3.5 all-to-all-start.1
  195.3 14.9 %select_convert_fusion = bf16[4,8,64,4096]{3,2,1,0:T(8,128)(2,1)} fusion(bf16[4,8,64,4096]{3,2,1,0:T(8,128)(2,1)} %bitcast.73, pred[4,8]{1,0:T(4,128)(4,1)S(1)} %broadcast_in_dim.175), kind=kLoop, calls=%fused_computation.8 | loop fusion | flops 8388608 | bytes 33554464 | tf_op jit(solution)/shard_map/convert_element_type | solution.py:132
  210.2 0.0 all-to-all-done.1
  210.2 0.9 copy-done.3
  211.1 7.0 %all-to-all-start.3 = ((bf16[4,8,64,4096]{3,2,1,0:T(8,128)(2,1)}), bf16[4,8,64,4096]{3,2,1,0:T(8,128)(2,1)}, u32[]{:S(2)}, u32[]{:S(2)}) async-start(bf16[4,8,64,4096]{3,2,1,0:T(8,128)(2,1)} %select_convert_fusion), calls=%async_computation.4 | async-start | bytes 33554432 | tf_op jit(solution)/shard_map/all_to_all | solution.py:141
  218.1 0.3 all-gather.2.cloned.1.call-start
  218.4 0.4 all-gather.2.cloned.1.call-update
  218.9 0.6 dynamic_slice.19
  220.1 0.1 select_reduce_fusion
  220.3 0.1 fusion.36
  220.3 43.4 %all-gather.2.cloned.1.call-done = bf16[160,6144]{1,0:T(8,128)(2,1)} async-done(((bf16[160,1536]{1,0:T(8,128)(2,1)}), bf16[160,6144]{1,0:T(8,128)(2,1)}) %all-gather.2.cloned.1.call-update) | async-done | bytes 1966096 | tf_op jit(solution)/shard_map/all_gather | solution.py:74
  263.8 21.6 %fusion.38 = f32[160,4096]{1,0:T(8,128)} fusion(bf16[160,6144]{1,0:T(8,128)(2,1)} %all-gather.2.cloned.1.call-done, bf16[6144,4096]{1,0:T(8,128)(2,1)} %param.10), kind=kOutput, calls=%fused_computation.107 | convolution fusion | flops 8053063680 | bytes 54919168 | tf_op jit(solution)/shard_map/dot_general | solution.py:73
  285.4 10.6 %fusion.4 = bf16[160,4096]{1,0:T(8,128)(2,1)} fusion(f32[160,4096]{1,0:T(8,128)} %fusion.38, bf16[32,64,4096]{2,1,0:T(8,128)(2,1)} %param.12, bf16[160,64]{0,1:T(8,128)(2,1)S(1)} %get-tuple-element.10, bf16[160,32]{0,1:T(8,128)(2,1)S(1)} %get-tuple-element.19), kind=kOutput, calls=%fused_computation.17 | convolution fusion | flops 2686648320 | bytes 20740096 | tf_op jit(solution)/shard_map/dot_general | solution.py:96
  296.0 5.4 %reduce_sum.103 = bf16[8,1536,64]{1,2,0:T(8,128)(2,1)} reduce(bf16[4,8,1536,64]{2,3,1,0:T(8,128)(2,1)} %all-to-all-done.2, bf16[]{:T(256)} %constant.102.clone.1), dimensions={0}, to_apply=%region_15.16 | reduce | flops 2359296 | bytes 7864322 | tf_op jit(solution)/shard_map/reduce_sum | solution.py:153
  301.4 1.3 pad_maximum_fusion.1
  302.7 2.2 gather_fusion.5
  304.9 1.1 select_select_fusion
  306.1 95.1 %all-to-all-done.3 = bf16[4,8,64,4096]{3,2,1,0:T(8,128)(2,1)} async-done(((bf16[4,8,64,4096]{3,2,1,0:T(8,128)(2,1)}), bf16[4,8,64,4096]{3,2,1,0:T(8,128)(2,1)}, u32[]{:S(2)}, u32[]{:S(2)}) %all-to-all-start.3) | async-done | bytes 16777248 | tf_op jit(solution)/shard_map/all_to_all | solution.py:141
  401.2 11.9 %reduce_sum.104 = bf16[8,64,4096]{2,1,0:T(8,128)(2,1)} reduce(bf16[4,8,64,4096]{3,2,1,0:T(8,128)(2,1)} %all-to-all-done.3, bf16[]{:T(256)} %constant.102.clone.1), dimensions={0}, to_apply=%region_16.17 | reduce | flops 6291456 | bytes 20971522 | tf_op jit(solution)/shard_map/reduce_sum | solution.py:154
  (36 shorter events, 0.3 us)
Async XLA Ops:
  7.2 14.7 %copy-start = (bf16[160,4096]{1,0:T(8,128)(2,1)S(1)}, bf16[160,4096]{1,0:T(8,128)(2,1)}, u32[]{:S(2)}) copy-start(bf16[160,4096]{1,0:T(8,128)(2,1)} %param.9) | copy-start | bytes 3932164
  17.6 42.7 %all-to-all-start = ((bf16[4,80,1536]{2,1,0:T(8,128)(2,1)}), bf16[4,80,1536]{2,1,0:T(8,128)(2,1)S(1)}, u32[]{:S(2)}, u32[]{:S(2)}) async-start(bf16[4,80,1536]{2,1,0:T(8,128)(2,1)} %select_select_fusion.2), calls=%async_computation | async-start | bytes 1966080 | tf_op jit(solution)/shard_map/all_to_all | solution.py:69
  21.8 120.7 %reduce-scatter.2.cloned.1.call-start = ((), (), s32[]{:S(2)}) async-start(), calls=%async_computation.6 | async-start | bytes 4915200 | tf_op jit(solution)/shard_map/reduce_scatter | solution.py:113
  45.9 2.4 copy-start.6
  45.9 4.0 copy-start.5
  51.1 9.2 %copy-start.2 = (bf16[320,1536]{1,0:T(8,128)(2,1)S(1)}, bf16[320,1536]{1,0:T(8,128)(2,1)}, u32[]{:S(2)}) copy-start(bf16[320,1536]{1,0:T(8,128)(2,1)} %param.8) | copy-start | bytes 2949124
  65.1 32.6 %copy-start.4 = (bf16[160,1536]{1,0:T(8,128)(2,1)}, bf16[160,1536]{1,0:T(8,128)(2,1)S(1)}, u32[]{:S(2)}) copy-start(bf16[160,1536]{1,0:T(8,128)(2,1)S(1)} %broadcast_select_fusion) | copy-start | bytes 1474564
  115.8 75.9 %all-to-all-start.2 = ((bf16[4,8,1536,64]{2,3,1,0:T(8,128)(2,1)}), bf16[4,8,1536,64]{2,3,1,0:T(8,128)(2,1)}, u32[]{:S(2)}, u32[]{:S(2)}) async-start(bf16[4,8,1536,64]{2,3,1,0:T(8,128)(2,1)} %select_convert_fusion.1), calls=%async_computation.3 | async-start | bytes 12582912 | tf_op jit(solution)/shard_map/all_to_all | solution.py:140
  191.8 18.4 %all-to-all-start.1 = ((bf16[4,80,1536]{2,1,0:T(8,128)(2,1)}), bf16[4,80,1536]{2,1,0:T(8,128)(2,1)S(1)}, u32[]{:S(2)}, u32[]{:S(2)}) async-start(bf16[4,80,1536]{2,1,0:T(8,128)(2,1)} %select_select_fusion.1), calls=%async_computation.2 | async-start | bytes 1966080 | tf_op jit(solution)/shard_map/all_to_all | solution.py:139
  210.2 0.9 copy-start.3
  211.1 190.0 %all-to-all-start.3 = ((bf16[4,8,64,4096]{3,2,1,0:T(8,128)(2,1)}), bf16[4,8,64,4096]{3,2,1,0:T(8,128)(2,1)}, u32[]{:S(2)}, u32[]{:S(2)}) async-start(bf16[4,8,64,4096]{3,2,1,0:T(8,128)(2,1)} %select_convert_fusion), calls=%async_computation.4 | async-start | bytes 33554432 | tf_op jit(solution)/shard_map/all_to_all | solution.py:141
  218.1 45.7 %all-gather.2.cloned.1.call-start = ((), (), s32[]{:S(2)}) async-start(), calls=%async_computation.5 | async-start | bytes 2457600 | tf_op jit(solution)/shard_map/all_gather | solution.py:74
  401.2 11.9 %copy-start.1 = (bf16[160,4096]{1,0:T(8,128)(2,1)S(1)}, bf16[160,4096]{1,0:T(8,128)(2,1)}, u32[]{:S(2)}) copy-start(bf16[160,4096]{1,0:T(8,128)(2,1)} %param.9) | copy-start | bytes 3932164
Sparse Core Ops, SparseCore 0:
  46.1 79.3 reduce-scatter.1
  221.1 42.6 all-gather.1
where the time goes:
time: 421 us; the launch traced here: 420 us
  waiting for transfers between devices  181 us (43%)
  matrix products  87 us (21%)
  other arithmetic  52 us (12%)
  local copies, waits for them, and re-layouts  37.7 us (9%)
  blocking collectives  27.4 us (7%)
  starting transfers between devices  20.2 us (5%)
  between operations  15 us (4%)
    all_to_all x1, waiting for transfers between devices, body(): lax.all_to_all(owner_b, 'dp', split_axis=0, concat_axis=0, tiled=True)  95.1 us
    all_gather x1, waiting for transfers between devices, body(): lax.all_gather(group_rows, 'fsdp', axis=1, tiled=True)  43.4 us
    all_to_all x1, waiting for transfers between devices, body(): lax.all_to_all(owner_a, 'dp', split_axis=0, concat_axis=0, tiled=True)  41.7 us
    psum x1, blocking collectives, body(): lowered_total, backward_total = lax.psum((down_part, back_part), 'fsdp')  27.4 us
    dot_general x1, matrix products, body(): lax.dot_general(cotangent, frozen_weight, (((1,), (1,)), ((), ())), prefe...  24.1 us
    dot_general x1, matrix products, body(): jnp.dot(lax.all_gather(group_rows, 'fsdp', axis=1, tiled=True), frozen_we...  21.6 us
    convert_element_type x1, other arithmetic, body(): owner_b = jnp.take(partial_up, order, axis=0).astype(jnp.bfloat16).reshap...  14.9 us
    gather x1, local copies, waits for them, and re-layouts, body(): jnp.take(partial_up, order, axis=0).astype(jnp.bfloat16)  13 us
  transfers between devices with their start and end apart: 6, of which 3 were waited for; matrix products, arithmetic and copies ran while one was open for 37% of the time, Pallas kernels for 0%

commit v1 on v0

--- a/solution.py
+++ b/solution.py
@@ -1,9 +1,17 @@
+import functools
+
 import jax
 import jax.numpy as jnp
 from jax import lax
+from jax.experimental import pallas as pl
+from jax.experimental.pallas import tpu as pltpu
 from jax.sharding import PartitionSpec as P
 
 adapter_scale = 0.25
+BF = jnp.bfloat16
+F32 = jnp.float32
+I32 = jnp.int32
+VMEM_LIMIT = 48 * 2**20
 
 
 def before_sums(values, group_axis):
@@ -30,7 +38,7 @@
     return jnp.where(valid[:, :, None], taken, jnp.zeros((), values.dtype))
 
 
-def body(
+def plain_body(
     input_rows,
     cotangent,
     frozen_weight,
@@ -155,6 +163,445 @@
     return (outputs, row_grad, grad_a, grad_b)
 
 
+def params():
+    return pltpu.CompilerParams(vmem_limit_bytes=VMEM_LIMIT)
+
+
+def cost(flops, moved):
+    return pl.CostEstimate(flops=int(flops), bytes_accessed=int(moved), transcendentals=0)
+
+
+SMEM = functools.partial(pl.BlockSpec, memory_space=pltpu.SMEM)
+
+
+def whole(shape):
+    return pl.BlockSpec(shape, lambda *_: (0,) * len(shape))
+
+
+def before(handoff_ref, giver, taker, groups):
+    sent = jnp.int32(0)
+    got = jnp.int32(0)
+    for other in range(groups):
+        sent = sent + jnp.where(other < taker, handoff_ref[giver, other], 0)
+        got = got + jnp.where(other < giver, handoff_ref[other, taker], 0)
+    return sent, got
+
+
+def pack(place, handoff, counts, slots, rows, balanced, half):
+    groups, tenants = counts.shape
+    capacity, width = rows.shape
+
+    def kernel(place_ref, handoff_ref, slots_ref, counts_ref, rows_ref, *outs):
+        out_refs, tenant_ref, slot_ref = outs[: groups - 1], outs[groups - 1], outs[groups]
+        mine = place_ref[0]
+        here = lax.broadcasted_iota(I32, (half, capacity), 1)
+        slot = lax.broadcasted_iota(I32, (half, capacity), 0)
+        for step in range(1, groups):
+            partner = mine ^ step
+            sent, _ = before(handoff_ref, mine, partner, groups)
+            pick = (here == slot + sent) & (slot < handoff_ref[mine, partner])
+            out_refs[step - 1][...] = jnp.dot(
+                pick.astype(F32).astype(BF), rows_ref[...], preferred_element_type=F32
+            ).astype(BF)
+        upto = lax.broadcasted_iota(I32, (tenants, tenants), 1) <= lax.broadcasted_iota(
+            I32, (tenants, tenants), 0
+        )
+        ends = lax.dot_general(
+            upto.astype(F32).astype(BF),
+            counts_ref[...].astype(F32).astype(BF),
+            (((1,), (1,)), ((), ())),
+            preferred_element_type=F32,
+        ).astype(I32)
+        place_of = lax.broadcasted_iota(I32, (1, balanced), 1)
+        for step in range(groups):
+            taker = mine ^ step
+            position = place_of
+            row_ends = jnp.zeros((tenants, balanced), I32)
+            for giver in range(groups):
+                sent, got = before(handoff_ref, giver, taker, groups)
+                inside = (place_of >= got) & (place_of < got + handoff_ref[giver, taker])
+                position = position + jnp.where(inside, sent - got, 0)
+                row_ends = row_ends + jnp.where(inside, ends[:, giver : giver + 1], 0)
+            tenant = jnp.sum((row_ends <= position).astype(I32), axis=0, keepdims=True)
+            target = jnp.zeros((1, balanced), I32)
+            for label in range(tenants):
+                target = target + jnp.where(tenant == label, slots_ref[label], 0)
+            tenant_ref[step : step + 1, :] = tenant
+            slot_ref[step : step + 1, :] = target
+
+    return pl.pallas_call(
+        kernel,
+        in_specs=[SMEM(), SMEM(), SMEM(), pl.BlockSpec(memory_space=pltpu.VMEM), pl.BlockSpec(memory_space=pltpu.VMEM)],
+        out_shape=[jax.ShapeDtypeStruct((half, width), BF)] * (groups - 1)
+        + [jax.ShapeDtypeStruct((groups, balanced), I32)] * 2,
+        compiler_params=params(),
+        cost_estimate=cost(2 * 3 * half * capacity * width, 2 * capacity * width * 2),
+    )(place, handoff, slots, counts, rows)
+
+
+def masked_rank(product, tenant, first, rank):
+    total = jnp.zeros((rank, product.shape[1]), F32)
+    for label in range(product.shape[0] // rank):
+        total = total + jnp.where(tenant == first + label, product[label * rank : (label + 1) * rank], 0.0)
+    return total
+
+
+def unpack(place, handoff, tenant, rows, arrived, down, rank, block):
+    groups, balanced = tenant.shape
+    capacity, width = rows.shape
+    half = arrived[0].shape[0]
+
+    def kernel(place_ref, handoff_ref, tenant_ref, rows_ref, *refs):
+        arrived_refs = refs[: groups - 1]
+        down_ref, gathered_ref, lowered_ref, turned = refs[groups - 1 :]
+        step = pl.program_id(0)
+
+        @pl.when(step == 0)
+        def _():
+            mine = place_ref[0]
+            place_of = lax.broadcasted_iota(I32, (balanced, capacity), 0)
+            here = lax.broadcasted_iota(I32, (balanced, capacity), 1)
+            sent, got = before(handoff_ref, mine, mine, groups)
+            inside = (place_of >= got) & (place_of < got + handoff_ref[mine, mine])
+            pick = inside & (here == place_of - got + sent)
+            total = jnp.dot(pick.astype(F32).astype(BF), rows_ref[...], preferred_element_type=F32)
+            place_of = lax.broadcasted_iota(I32, (balanced, half), 0)
+            here = lax.broadcasted_iota(I32, (balanced, half), 1)
+            for k in range(1, groups):
+                giver = mine ^ k
+                _, got = before(handoff_ref, giver, mine, groups)
+                inside = (place_of >= got) & (place_of < got + handoff_ref[giver, mine])
+                pick = inside & (here == place_of - got)
+                total = total + jnp.dot(
+                    pick.astype(F32).astype(BF), arrived_refs[k - 1][...], preferred_element_type=F32
+                )
+            gathered_ref[...] = total.astype(BF)
+            turned[...] = total.T.astype(BF)
+            lowered_ref[...] = jnp.zeros_like(lowered_ref)
+
+        product = jnp.dot(down_ref[...], turned[...], preferred_element_type=F32)
+        lowered_ref[...] += masked_rank(product, tenant_ref[0:1, :], step * (block // rank), rank)
+
+    return pl.pallas_call(
+        kernel,
+        grid=(down.shape[0] // block,),
+        in_specs=[SMEM(), SMEM(), whole((groups, balanced)), whole((capacity, width))]
+        + [whole((half, width))] * (groups - 1)
+        + [pl.BlockSpec((block, width), lambda i: (i, 0))],
+        out_specs=[whole((balanced, width)), whole((rank, balanced))],
+        out_shape=[
+            jax.ShapeDtypeStruct((balanced, width), BF),
+            jax.ShapeDtypeStruct((rank, balanced), F32),
+        ],
+        scratch_shapes=[pltpu.VMEM((width, balanced), BF)],
+        compiler_params=params(),
+        cost_estimate=cost(2 * balanced * down.size, 2 * down.size + 6 * balanced * width),
+    )(place, handoff, tenant, rows, *arrived, down)
+
+
+def rank_backward(tenant, turned, up, rank, block):
+    balanced = turned.shape[1]
+    hidden = up.shape[1]
+
+    def kernel(tenant_ref, turned_ref, up_ref, out_ref):
+        step = pl.program_id(0)
+        product = jnp.dot(up_ref[...], turned_ref[...], preferred_element_type=F32)
+        mine = masked_rank(product, tenant_ref[0:1, :], step * (block // rank), rank)
+
+        @pl.when(step == 0)
+        def _():
+            out_ref[...] = mine
+
+        @pl.when(step > 0)
+        def _():
+            out_ref[...] += mine
+
+    return pl.pallas_call(
+        kernel,
+        grid=(up.shape[0] // block,),
+        in_specs=[whole(tenant.shape), whole(turned.shape), pl.BlockSpec((block, hidden), lambda i: (i, 0))],
+        out_specs=whole((rank, balanced)),
+        out_shape=jax.ShapeDtypeStruct((rank, balanced), F32),
+        compiler_params=params(),
+        cost_estimate=cost(2 * balanced * up.size, 2 * up.size),
+    )(tenant, turned, up)
+
+
+def base_gradient(owner, turned, weight, width, block, arrived=None):
+    hidden, balanced = turned.shape
+    steps = width // block
+
+    def kernel(owner_ref, turned_ref, weight_ref, *refs):
+        product = jnp.dot(weight_ref[...], turned_ref[...], preferred_element_type=F32).T
+        if arrived is not None:
+            product = product + refs[0][...].astype(F32)
+        refs[-1][...] = product.astype(BF)
+
+    piece = pl.BlockSpec((balanced, block), lambda i, owner_ref: (0, i))
+    return pl.pallas_call(
+        kernel,
+        grid_spec=pltpu.PrefetchScalarGridSpec(
+            num_scalar_prefetch=1,
+            grid=(steps,),
+            in_specs=[
+                whole(turned.shape),
+                pl.BlockSpec((block, hidden), lambda i, owner_ref: (owner_ref[0] * steps + i, 0)),
+            ]
+            + ([] if arrived is None else [piece]),
+            out_specs=piece,
+        ),
+        out_shape=jax.ShapeDtypeStruct((balanced, width), BF),
+        compiler_params=params(),
+        cost_estimate=cost(2 * balanced * width * hidden, 2 * width * hidden),
+    )(owner, turned, weight, *(() if arrived is None else (arrived,)))
+
+
+def spread(wide_ref, column_ref, twice_ref, tenants, rank):
+    lanes = 2 * rank
+    odd = (lax.broadcasted_iota(I32, (column_ref.shape[0], lanes), 1) >= rank).astype(I32)
+    label = column_ref[...] - odd
+    for pair in range(tenants // 2):
+        wide_ref[:, pair * lanes : (pair + 1) * lanes] = jnp.where(
+            label == 2 * pair, twice_ref[...].astype(F32), 0.0
+        ).astype(BF)
+
+
+def forward(owners, parts, weight, block, total=None, column=None, twice=None, up=None, rank=None):
+    balanced, width = parts[0].shape
+    hidden = weight.shape[1]
+    count = len(parts)
+    last = up is not None
+
+    def kernel(owners_ref, *refs):
+        part_refs, weight_refs = refs[:count], refs[count : 2 * count]
+        rest = list(refs[2 * count :])
+        value = jnp.dot(part_refs[0][...], weight_refs[0][...], preferred_element_type=F32)
+        for i in range(1, count):
+            value = value + jnp.dot(part_refs[i][...], weight_refs[i][...], preferred_element_type=F32)
+        if total is not None:
+            value = value + rest.pop(0)[...]
+        if last:
+            column_ref, twice_ref, up_ref = rest.pop(0), rest.pop(0), rest.pop(0)
+            wide_ref = rest.pop()
+
+            @pl.when(pl.program_id(0) == 0)
+            def _():
+                spread(wide_ref, column_ref, twice_ref, up.shape[0] // rank, rank)
+
+            value = value + jnp.dot(wide_ref[...], up_ref[...], preferred_element_type=F32)
+        rest[0][...] = value.astype(rest[0].dtype)
+
+    piece = pl.BlockSpec((balanced, block), lambda i, o: (0, i))
+    in_specs = [whole((balanced, width))] * count
+    for i in range(count):
+        in_specs.append(pl.BlockSpec((width, block), lambda n, o, i=i: (o[i], n)))
+    operands = [*parts, *([weight] * count)]
+    if total is not None:
+        in_specs.append(piece)
+        operands.append(total)
+    if last:
+        in_specs += [whole(column.shape), whole(twice.shape), pl.BlockSpec((up.shape[0], block), lambda i, o: (0, i))]
+        operands += [column, twice, up]
+    return pl.pallas_call(
+        kernel,
+        grid_spec=pltpu.PrefetchScalarGridSpec(
+            num_scalar_prefetch=1,
+            grid=(hidden // block,),
+            in_specs=in_specs,
+            out_specs=piece,
+            scratch_shapes=[pltpu.VMEM((balanced, up.shape[0]), BF)] if last else [],
+        ),
+        out_shape=jax.ShapeDtypeStruct((balanced, hidden), BF if last else F32),
+        compiler_params=params(),
+        cost_estimate=cost(
+            2 * balanced * hidden * (count * width + (up.shape[0] if last else 0)),
+            2 * hidden * (count * width + (up.shape[0] if last else 0)),
+        ),
+    )(owners, *operands)
+
+
+def finish_gradient(terms, column, twice, down, block, rank):
+    balanced, width = terms[0].shape
+
+    def kernel(column_ref, twice_ref, down_ref, *refs):
+        term_refs, out_ref, wide_ref = refs[:-2], refs[-2], refs[-1]
+
+        @pl.when(pl.program_id(0) == 0)
+        def _():
+            spread(wide_ref, column_ref, twice_ref, down.shape[0] // rank, rank)
+
+        value = jnp.dot(wide_ref[...], down_ref[...], preferred_element_type=F32)
+        for term_ref in term_refs:
+            value = value + term_ref[...].astype(F32)
+        out_ref[...] = value.astype(BF)
+
+    piece = pl.BlockSpec((balanced, block), lambda i: (0, i))
+    return pl.pallas_call(
+        kernel,
+        grid=(width // block,),
+        in_specs=[whole(column.shape), whole(twice.shape), pl.BlockSpec((down.shape[0], block), lambda i: (0, i))]
+        + [piece] * len(terms),
+        out_specs=piece,
+        out_shape=jax.ShapeDtypeStruct((balanced, width), BF),
+        scratch_shapes=[pltpu.VMEM((balanced, down.shape[0]), BF)],
+        compiler_params=params(),
+        cost_estimate=cost(2 * balanced * down.size, 2 * down.size),
+    )(column, twice, down, *terms)
+
+
+def owned_gradient(place, slot, ranks, values, share, scale, block):
+    groups, balanced = slot.shape
+    rank = ranks[0].shape[0]
+    width = values[0].shape[1]
+
+    def kernel(place_ref, slot_ref, *refs):
+        rank_refs, value_refs = refs[:groups], refs[groups : 2 * groups]
+        out_ref, wide_ref = refs[2 * groups :]
+
+        @pl.when(pl.program_id(0) == 0)
+        def _():
+            first = place_ref[0] * share
+            for k in range(groups):
+                for s in range(share):
+                    wide_ref[k, s * rank : (s + 1) * rank, :] = jnp.where(
+                        slot_ref[k : k + 1, :] == first + s, rank_refs[k][...].astype(F32), 0.0
+                    ).astype(BF)
+
+        value = jnp.dot(wide_ref[0], value_refs[0][...], preferred_element_type=F32)
+        for k in range(1, groups):
+            value = value + jnp.dot(wide_ref[k], value_refs[k][...], preferred_element_type=F32)
+        out_ref[...] = (scale * value).astype(BF)
+
+    return pl.pallas_call(
+        kernel,
+        grid=(width // block,),
+        in_specs=[SMEM(), whole(slot.shape)]
+        + [whole((rank, balanced))] * groups
+        + [pl.BlockSpec((balanced, block), lambda i: (0, i))] * groups,
+        out_specs=pl.BlockSpec((share * rank, block), lambda i: (0, i)),
+        out_shape=jax.ShapeDtypeStruct((share * rank, width), BF),
+        scratch_shapes=[pltpu.VMEM((groups, share * rank, balanced), BF)],
+        compiler_params=params(),
+        cost_estimate=cost(2 * groups * balanced * share * rank * width, 2 * width * (groups * balanced + share * rank)),
+    )(place, slot, *ranks, *values)
+
+
+def bring_home(place, handoff, gradients, capacity):
+    balanced, width = gradients[0].shape
+    groups = handoff.shape[0]
+
+    def kernel(place_ref, handoff_ref, *refs):
+        out_ref = refs[-1]
+        mine = place_ref[0]
+        row = lax.broadcasted_iota(I32, (capacity, balanced), 0)
+        here = lax.broadcasted_iota(I32, (capacity, balanced), 1)
+        total = jnp.zeros((capacity, width), F32)
+        for k in range(groups):
+            taker = mine ^ k
+            sent, got = before(handoff_ref, mine, taker, groups)
+            inside = (row >= sent) & (row < sent + handoff_ref[mine, taker])
+            pick = inside & (here == row - sent + got)
+            total = total + jnp.dot(pick.astype(F32).astype(BF), refs[k][...], preferred_element_type=F32)
+        out_ref[...] = total.astype(BF)
+
+    return pl.pallas_call(
+        kernel,
+        in_specs=[SMEM(), SMEM()] + [pl.BlockSpec(memory_space=pltpu.VMEM)] * groups,
+        out_shape=jax.ShapeDtypeStruct((capacity, width), BF),
+        compiler_params=params(),
+        cost_estimate=cost(2 * groups * balanced * capacity * width, 4 * groups * balanced * width),
+    )(place, handoff, *gradients)
+
+
+def swap(values, axis, distance):
+    size = lax.axis_size(axis)
+    return lax.ppermute(values, axis, [(i, i ^ distance) for i in range(size)])
+
+
+def after(values, *earlier):
+    return lax.optimization_barrier((values, *earlier))[0]
+
+
+def fast_body(
+    input_rows,
+    cotangent,
+    frozen_weight,
+    adapter_down_weight,
+    adapter_up_weight,
+    tenant_row_counts,
+    handoff_counts,
+    tenant_gradient_slot,
+):
+    mine = lax.axis_index("dp")
+    z = lax.axis_index("fsdp")
+    balanced = cotangent.shape[0]
+    capacity, width = input_rows.shape
+    tenants, rank, hidden = adapter_up_weight.shape
+    share = tenants // lax.axis_size("dp")
+    place = mine.astype(I32).reshape(1)
+    owner = [(z ^ k).astype(I32) for k in range(4)]
+    down = adapter_down_weight.transpose(0, 2, 1).reshape(tenants * rank, width)
+    up = adapter_up_weight.reshape(tenants * rank, hidden)
+    turned = cotangent.T
+
+    *outgoing, tenant, slot = pack(
+        place, handoff_counts, tenant_row_counts, tenant_gradient_slot, input_rows, balanced, balanced // 2
+    )
+    arrived = [None] * 3
+    for k in (2, 3, 1):
+        arrived[k - 1] = swap(outgoing[k - 1], "dp", k)
+
+    far = base_gradient(owner[3].reshape(1), turned, frozen_weight, width, 512)
+    for_far = swap(far, "fsdp", 1)
+    near = base_gradient(owner[1].reshape(1), turned, frozen_weight, width, 512)
+    from_near = swap(near, "fsdp", 1)
+    raised = rank_backward(tenant, turned, up, rank, 512)
+    gathered, lowered = unpack(place, handoff_counts, tenant, input_rows, arrived, down, rank, 512)
+    pair = swap(gathered, "fsdp", 2)
+    beside = swap(gathered, "fsdp", 1)
+    across = base_gradient(owner[2].reshape(1), turned, frozen_weight, width, 512, for_far)
+    from_pair = swap(across, "fsdp", 2)
+    cot_x = swap(after(cotangent, gathered), "dp", 2)
+    diagonal = swap(pair, "fsdp", 1)
+
+    partial = jnp.concatenate([lowered, raised], axis=0)
+    summed = partial + swap(partial, "fsdp", 1)
+    summed = summed + swap(partial, "fsdp", 2) + swap(partial, "fsdp", 3)
+    lora_in = summed[:rank].astype(BF)
+    lora_grad = (adapter_scale * summed[rank:]).astype(BF)
+    ranks = jnp.concatenate([lora_in, lora_grad], axis=0)
+    all_ranks = [ranks] + [swap(ranks, "dp", k) for k in (1, 2, 3)]
+    column = tenant[0].reshape(balanced, 1)
+    twice_in = jnp.concatenate([lora_in * jnp.asarray(adapter_scale, BF)] * 2, axis=0).T
+    twice_grad = jnp.concatenate([lora_grad] * 2, axis=0).T
+
+    own = base_gradient(owner[0].reshape(1), turned, frozen_weight, width, 512)
+    total = forward(jnp.stack([owner[0], owner[1]]), [gathered, beside], frozen_weight, 512)
+    group_gradient = finish_gradient([own, from_near, from_pair], column, twice_grad, down, 512, rank)
+
+    gathered_x = swap(after(gathered, cot_x), "dp", 2)
+    cot_all = [cotangent, swap(cotangent, "dp", 1), cot_x, swap(cot_x, "dp", 1)]
+    gathered_all = [gathered, swap(gathered, "dp", 1), gathered_x, swap(gathered_x, "dp", 1)]
+    back_x = swap(group_gradient, "dp", 2)
+    back = [group_gradient, swap(group_gradient, "dp", 1), back_x, swap(back_x, "dp", 1)]
+
+    outputs = forward(
+        jnp.stack([owner[2], owner[3]]), [pair, diagonal], frozen_weight, 512,
+        total, column, twice_in, up, rank,
+    )
+    grad_b = owned_gradient(
+        place, slot, [r[:rank] for r in all_ranks], cot_all, share, adapter_scale, 1024
+    )
+    grad_a = owned_gradient(place, slot, [r[rank:] for r in all_ranks], gathered_all, share, 1.0, 512)
+    row_grad = bring_home(place, handoff_counts, back, capacity)
+    return (
+        outputs,
+        row_grad,
+        grad_a.reshape(share, rank, width).transpose(0, 2, 1),
+        grad_b.reshape(share, rank, hidden),
+    )
+
+
 def solution(mesh):
     placed = (
         P(("groups", "dp"), "fsdp"),
@@ -166,8 +613,9 @@
         P("groups", None),
         P("groups"),
     )
+    four_by_four = mesh.shape["dp"] == 4 and mesh.shape["fsdp"] == 4
     return jax.shard_map(
-        body,
+        fast_body if four_by_four else plain_body,
         mesh=mesh,
         in_specs=placed,
         out_specs=(

time: 421 us -> 188 us (0.45)
  waiting for transfers between devices: 181 us -> 57.7 us
  Pallas kernels: 0 us -> 95.9 us
  matrix products: 87 us -> 0 us
  other arithmetic: 52 us -> 0.24 us
  blocking collectives: 27.4 us -> 0 us
  local copies, waits for them, and re-layouts: 37.7 us -> 10.7 us
  between operations: 15 us -> 0.87 us
    all_to_all x4 -> x0, waiting for transfers between devices: 137 us -> none  [the longest x1 95.1 us: body(): lax.all_to_all(owner_b, 'dp', split_axis=0, concat_axis=0, tiled=True)]
    pallas_call x0 -> x13, Pallas kernels: none -> 95.9 us  [the longest x2 31.1 us: forward(): pl.pallas_call(kernel, grid_spec=pltpu.PrefetchScalarGridSpec(num_scalar_...]
    dot_general x7 -> x0, matrix products: 82.2 us -> none  [the longest x1 24.1 us: body(): lax.dot_general(cotangent, frozen_weight, (((1,), (1,)), ((), ())), prefe...]
    ppermute x0 -> x24, waiting for transfers between devices: none -> 57.7 us  [swap(): return lax.ppermute(values, axis, [(i, i ^ distance) for i in range(size)])]
    all_gather x1 -> x0, waiting for transfers between devices: 43.4 us -> none  [body(): lax.all_gather(group_rows, 'fsdp', axis=1, tiled=True)]
    gather x8 -> x0, local copies, waits for them, and re-layouts: 34.8 us -> none  [the longest x1 13 us: body(): jnp.take(partial_up, order, axis=0).astype(jnp.bfloat16)]
    psum x1 -> x0, blocking collectives: 27.4 us -> none  [body(): lowered_total, backward_total = lax.psum((down_part, back_part), 'fsdp')]
    convert_element_type x4 -> x1, other arithmetic: 22.2 us -> 0.01 us  [fast_body(): lora_grad = (adapter_scale * summed[rank:]).astype(BF)]
  transfers between devices with their start and end apart: 6 -> 24, of which waited for: 3 -> 7; matrix products, arithmetic and copies ran while one was open for 37% -> 2% of each run, Pallas kernels for 0% -> 47%
where the time goes in v1:
time: 188 us; the launch traced here: 185 us
  Pallas kernels  95.9 us (51%)
  waiting for transfers between devices  57.7 us (31%)
  starting transfers between devices  19.4 us (10%)
  local copies, waits for them, and re-layouts  10.7 us (6%)
    ppermute x24, waiting for transfers between devices, swap(): return lax.ppermute(values, axis, [(i, i ^ distance) for i in range(size)])  57.7 us
    pallas_call x2, Pallas kernels, forward(): pl.pallas_call(kernel, grid_spec=pltpu.PrefetchScalarGridSpec(num_scalar_...  31.1 us
    pallas_call x4, Pallas kernels, base_gradient(): pl.pallas_call(kernel, grid_spec=pltpu.PrefetchScalarGridSpec(num_scalar_...  30.4 us
    ppermute x24, starting transfers between devices, swap(): return lax.ppermute(values, axis, [(i, i ^ distance) for i in range(size)])  19.4 us
    pallas_call x2, Pallas kernels, owned_gradient(): pl.pallas_call(kernel, grid=(width // block,), in_specs=[SMEM(), whole(sl...  10.7 us
    unnamed x21, local copies, waits for them, and re-layouts  9.58 us
    pallas_call x1, Pallas kernels, rank_backward(): pl.pallas_call(kernel, grid=(up.shape[0] // block,), in_specs=[whole(tena...  8.5 us
    pallas_call x1, Pallas kernels, unpack(): pl.pallas_call(kernel, grid=(down.shape[0] // block,), in_specs=[SMEM(),...  5.69 us
  transfers between devices with their start and end apart: 24, of which 7 were waited for; matrix products, arithmetic and copies ran while one was open for 2% of the time, Pallas kernels for 47%

profile of v1, /device:TPU:0, one launch (start us, length us, event | category | flops | bytes accessed | tf_op | source)
XLA Modules:
  0.0 184.8 jit_solution(6534532461428751156)
XLA Ops:
  0.6 0.0 copy-start
  0.6 1.2 copy-done
  1.8 0.7 copy-done.6
  2.5 0.7 copy-done.8
  3.2 0.7 copy-done.9
  3.9 2.2 %shard_map.111 = (bf16[80,1536]{1,0:T(8,128)(2,1)}, bf16[80,1536]{1,0:T(8,128)(2,1)}, bf16[80,1536]{1,0:T(8,128)(2,1)}, s32[4,160]{1,0:T(4,128)S(1)}, s32[4,160]{1,0:T(4,128)S(1)}) custom-call(s32[1]{0:T(128)} %bitcast.2.place_ref, s32[4,4]{1,0:T(4,128)S(1)} %copy-done.6, s32[32]{0:T(128)S(1)} %copy-done.9, s32[4,32]{1,0:T(4,128)S(1)} %copy-done.8, ...), custom_call_target="tpu_custom_call" | custom-call | flops 235929600 | bytes 1966080 | tf_op jit(solution)/shard_map/pallas_call | solution.py:232
  6.0 0.5 collective-permute-start
  6.5 2.5 %collective-permute-start.1 = (bf16[80,1536]{1,0:T(8,128)(2,1)}, bf16[80,1536]{1,0:T(8,128)(2,1)S(1)}, u32[]{:S(2)}, u32[]{:S(2)}) collective-permute-start(bf16[80,1536]{1,0:T(8,128)(2,1)} %get-tuple-element.15), channel_id=1, source_target_pairs={{0,8},{4,12},{8,0},{12,4},{1,9},{5,13},{9,1},{13,5},{2,10},{6,14},... | collective-permute-start | bytes 737288 | tf_op jit(solution)/shard_map/ppermute | solution.py:518
  9.0 0.1 collective-permute-start.2
  9.1 3.1 %copy.15 = bf16[160,4096]{0,1:T(8,128)(2,1)S(1)} copy(bf16[160,4096]{1,0:T(8,128)(2,1)} %refs_4_.1) | data formatting | bytes 2621440 | tf_op args[1]
  12.2 7.8 %shard_map.118 = bf16[160,1536]{1,0:T(8,128)(2,1)} custom-call(s32[1]{0:T(128)} %bitcast.1.owner_ref, bf16[4096,160]{1,0:T(8,128)(2,1)S(1)} %bitcast.20, bf16[6144,4096]{1,0:T(8,128)(2,1)} %weight_ref.7), custom_call_target="tpu_custom_call" | custom-call | flops 2013265920 | bytes 12582912 | tf_op jit(solution)/shard_map/pallas_call | solution.py:341
  20.0 1.8 collective-permute-start.10
  21.8 7.8 %shard_map.117 = bf16[160,1536]{1,0:T(8,128)(2,1)} custom-call(s32[1]{0:T(128)} %bitcast.6.owner_ref, bf16[4096,160]{1,0:T(8,128)(2,1)S(1)} %bitcast.21, bf16[6144,4096]{1,0:T(8,128)(2,1)} %weight_ref.7), custom_call_target="tpu_custom_call" | custom-call | flops 2013265920 | bytes 12582912 | tf_op jit(solution)/shard_map/pallas_call | solution.py:341
  29.5 0.2 collective-permute-start.9
  29.8 7.1 %shard_map.116.refs_0_ = bf16[160,1536]{1,0:T(8,128)(2,1)S(1)} custom-call(s32[1]{0:T(128)} %bitcast.5.owner_ref, bf16[4096,160]{1,0:T(8,128)(2,1)S(1)} %bitcast.22, bf16[6144,4096]{1,0:T(8,128)(2,1)} %weight_ref.7), custom_call_target="tpu_custom_call" | custom-call | flops 2013265920 | bytes 12582912 | tf_op jit(solution)/shard_map/pallas_call | solution.py:341
  36.9 0.1 pad_add_fusion.1.owners_ref
  36.9 0.1 copy.16.refs_5_.column_ref
  37.1 0.0 copy-start.1
  37.1 0.0 copy-start.7
  37.1 8.5 %shard_map.114 = f32[64,160]{1,0:T(8,128)S(1)} custom-call(s32[4,160]{1,0:T(4,128)S(1)} %get-tuple-element.13.tenant_ref, bf16[4096,160]{1,0:T(8,128)(2,1)S(1)} %bitcast.23, bf16[2048,4096]{1,0:T(8,128)(2,1)} %bitcast.25), custom_call_target="tpu_custom_call" | custom-call | flops 2684354560 | bytes 16777216 | tf_op jit(solution)/shard_map/pallas_call | solution.py:319
  45.6 0.0 collective-permute-done.refs_0_
  45.6 0.0 copy-start.2
  45.6 0.7 copy-done.2
  46.3 0.7 copy-done.4
  47.0 0.9 copy-done.3
  48.0 0.9 copy-done.5
  48.9 5.7 %shard_map.112 = (bf16[160,1536]{1,0:T(8,128)(2,1)S(1)}, f32[64,160]{1,0:T(8,128)S(1)}) custom-call(s32[1]{0:T(128)} %bitcast.2.place_ref, s32[4,4]{1,0:T(4,128)S(1)} %copy-done.7, s32[4,160]{1,0:T(4,128)S(1)} %get-tuple-element.13.tenant_ref, bf16[320,1536]{1,0:T(8,128)(2,1)S(1)} %copy-done.1, bf16[80,1536]{1,0:T(8,128)(2,1)S(1)} %collective-permute-done.refs_0_, ...), custom_call_target="tpu_custom_call" | custom-call | flops 1006632960 | bytes 7766016 | tf_op jit(solution)/shard_map/pallas_call | solution.py:285
  54.6 1.9 %collective-permute-start.6 = (f32[128,160]{1,0:T(8,128)S(1)}, f32[128,160]{1,0:T(8,128)S(1)}, u32[]{:S(2)}, u32[]{:S(2)}) collective-permute-start(f32[128,160]{1,0:T(8,128)S(1)} %pad_maximum_fusion), channel_id=1, source_target_pairs={{0,1},{1,0},{2,3},{3,2},{4,5},{5,4},{6,7},{7,6},{8,9},{9,8},{10,11... | collective-permute-start | bytes 245768 | tf_op jit(solution)/shard_map/ppermute | solution.py:518
  56.5 2.6 %collective-permute-start.7 = (f32[128,160]{1,0:T(8,128)S(1)}, f32[128,160]{1,0:T(8,128)S(1)}, u32[]{:S(2)}, u32[]{:S(2)}) collective-permute-start(f32[128,160]{1,0:T(8,128)S(1)} %pad_maximum_fusion), channel_id=1, source_target_pairs={{0,2},{1,3},{2,0},{3,1},{4,6},{5,7},{6,4},{7,5},{8,10},{9,11},{10,... | collective-permute-start | bytes 245768 | tf_op jit(solution)/shard_map/ppermute | solution.py:518
  59.1 0.0 collective-permute-start.8
  59.1 0.1 pad_add_fusion.owners_ref
  59.2 2.2 %collective-permute-done.6 = f32[128,160]{1,0:T(8,128)S(1)} collective-permute-done((f32[128,160]{1,0:T(8,128)S(1)}, f32[128,160]{1,0:T(8,128)S(1)}, u32[]{:S(2)}, u32[]{:S(2)}) %collective-permute-start.6) | collective-permute-done | bytes 81952 | tf_op jit(solution)/shard_map/ppermute | solution.py:518
  61.3 2.6 %collective-permute-start.3 = (bf16[160,1536]{1,0:T(8,128)(2,1)S(1)}, bf16[160,1536]{1,0:T(8,128)(2,1)}, u32[]{:S(2)}, u32[]{:S(2)}) collective-permute-start(bf16[160,1536]{1,0:T(8,128)(2,1)S(1)} %get-tuple-element.21.refs_0_.refs_4_), channel_id=1, source_target_pairs={{0,2},{1,3},{2,0},{3,1},{4,6},{5,7},{6,4},{7,5},{8,10},{9,11},{10,... | collective-permute-start | bytes 1474568 | tf_op jit(solution)/shard_map/ppermute | solution.py:518
  63.9 16.0 %collective-permute-done.7 = f32[128,160]{1,0:T(8,128)S(1)} collective-permute-done((f32[128,160]{1,0:T(8,128)S(1)}, f32[128,160]{1,0:T(8,128)S(1)}, u32[]{:S(2)}, u32[]{:S(2)}) %collective-permute-start.7) | collective-permute-done | bytes 81952 | tf_op jit(solution)/shard_map/ppermute | solution.py:518
  79.9 1.5 collective-permute-start.19
  81.5 0.1 collective-permute-start.17
  81.6 0.0 collective-permute-done.10.refs_0_
  81.6 0.6 collective-permute-start.16
  82.2 7.8 %shard_map.119 = bf16[160,1536]{1,0:T(8,128)(2,1)} custom-call(s32[1]{0:T(128)} %bitcast.owner_ref, bf16[4096,160]{1,0:T(8,128)(2,1)S(1)} %bitcast.24, bf16[6144,4096]{1,0:T(8,128)(2,1)} %weight_ref.7, bf16[160,1536]{1,0:T(8,128)(2,1)} %collective-permute-done.10.refs_0_), custom_call_target="tpu_custom_call" | custom-call | flops 2013265920 | bytes 12582912 | tf_op jit(solution)/shard_map/pallas_call | solution.py:341
  90.0 8.8 %collective-permute-done.17 = bf16[128,160]{1,0:T(8,128)(2,1)S(1)} collective-permute-done((bf16[128,160]{1,0:T(8,128)(2,1)S(1)}, bf16[128,160]{1,0:T(8,128)(2,1)S(1)}, u32[]{:S(2)}, u32[]{:S(2)}) %collective-permute-start.17) | collective-permute-done | bytes 40992 | tf_op jit(solution)/shard_map/ppermute | solution.py:518
  98.7 0.0 collective-permute-start.11
  98.7 0.1 copy.19.twice_ref
  98.9 0.1 copy.17.refs_6_
  99.0 1.6 collective-permute-done.16
  100.6 1.3 collective-permute-start.5
  101.9 0.0 collective-permute-done.3.refs_0_
  101.9 0.7 collective-permute-start.4
  102.7 0.8 fusion.3
  103.4 0.1 collective-permute-start.22
  103.5 20.4 %collective-permute-done.11.refs_2_ = bf16[160,1536]{1,0:T(8,128)(2,1)S(1)} collective-permute-done((bf16[160,1536]{1,0:T(8,128)(2,1)}, bf16[160,1536]{1,0:T(8,128)(2,1)S(1)}, u32[]{:S(2)}, u32[]{:S(2)}) %collective-permute-start.11) | collective-permute-done | bytes 491552 | tf_op jit(solution)/shard_map/ppermute | solution.py:518
  124.0 0.0 collective-permute-start.15
  124.0 4.5 %shard_map.120.refs_0_ = bf16[160,1536]{1,0:T(8,128)(2,1)S(1)} custom-call(s32[160,1]{1,0:T(8,128)S(1)} %copy.16.refs_5_.column_ref, bf16[160,128]{1,0:T(8,128)(2,1)S(1)} %copy.19.twice_ref, bf16[2048,1536]{1,0:T(8,128)(2,1)} %bitcast.28, bf16[160,1536]{1,0:T(8,128)(2,1)S(1)} %shard_map.116.refs_0_, bf16[160,1536]{1,0:T(8,128)(2,1)} %collective-permute-done.9.refs_1_, ...), custom_call_target="tpu_custom_call" | custom-call | flops 1006632960 | bytes 6291456 | tf_op jit(solution)/shard_map/pallas_call | solution.py:439
  128.6 0.6 collective-permute-start.13
  129.2 0.2 collective-permute-start.12
  129.4 1.5 collective-permute-start.20
  130.9 4.1 %collective-permute-done.4.refs_1_ = bf16[160,1536]{1,0:T(8,128)(2,1)S(1)} collective-permute-done((bf16[160,1536]{1,0:T(8,128)(2,1)}, bf16[160,1536]{1,0:T(8,128)(2,1)S(1)}, u32[]{:S(2)}, u32[]{:S(2)}) %collective-permute-start.4) | collective-permute-done | bytes 491552 | tf_op jit(solution)/shard_map/ppermute | solution.py:518
  135.0 12.6 %shard_map.113.refs_4_ = f32[160,4096]{1,0:T(8,128)S(1)} custom-call(s32[2]{0:T(128)S(1)} %pad_add_fusion.1.owners_ref, bf16[160,1536]{1,0:T(8,128)(2,1)S(1)} %get-tuple-element.21.refs_0_.refs_4_, bf16[160,1536]{1,0:T(8,128)(2,1)S(1)} %collective-permute-done.5.refs_1_, bf16[6144,4096]{1,0:T(8,128)(2,1)} %weight_ref.7, bf16[6144,4096]{1,0:T(8,128)(2,1)} %weight_ref.7), custom_call_target="tpu_custom_call" | custom-call | flops 4026531840 | bytes 25165824 | tf_op jit(solution)/shard_map/pallas_call | solution.py:405
  147.6 0.6 collective-permute-start.18
  148.1 0.1 collective-permute-start.14
  148.2 4.5 %collective-permute-done.20.refs_6_ = bf16[160,1536]{1,0:T(8,128)(2,1)S(1)} collective-permute-done((bf16[160,1536]{1,0:T(8,128)(2,1)S(1)}, bf16[160,1536]{1,0:T(8,128)(2,1)S(1)}, u32[]{:S(2)}, u32[]{:S(2)}) %collective-permute-start.20) | collective-permute-done | bytes 491552 | tf_op jit(solution)/shard_map/ppermute | solution.py:518
  152.8 18.6 %shard_map.115 = bf16[160,4096]{1,0:T(8,128)(2,1)} custom-call(s32[2]{0:T(128)S(1)} %pad_add_fusion.owners_ref, bf16[160,1536]{1,0:T(8,128)(2,1)} %collective-permute-done.3.refs_0_, bf16[160,1536]{1,0:T(8,128)(2,1)S(1)} %collective-permute-done.4.refs_1_, bf16[6144,4096]{1,0:T(8,128)(2,1)} %weight_ref.7, bf16[6144,4096]{1,0:T(8,128)(2,1)} %weight_ref.7, ...), custom_call_target="tpu_custom_call" | custom-call | flops 6710886400 | bytes 41943040 | tf_op jit(solution)/shard_map/pallas_call | solution.py:405
  171.4 2.7 %shard_map.121 = bf16[320,1536]{1,0:T(8,128)(2,1)} custom-call(s32[1]{0:T(128)} %bitcast.2.place_ref, s32[4,4]{1,0:T(4,128)S(1)} %copy-done.7, bf16[160,1536]{1,0:T(8,128)(2,1)S(1)} %shard_map.120.refs_0_, bf16[160,1536]{1,0:T(8,128)(2,1)S(1)} %collective-permute-done.12.refs_1_, bf16[160,1536]{1,0:T(8,128)(2,1)S(1)} %collective-permute-done.13.refs_2_, ...), custom_call_target="tpu_custom_call" | custom-call | flops 629145600 | bytes 3932160 | tf_op jit(solution)/shard_map/pallas_call | solution.py:507
  174.1 3.3 %shard_map.122 = bf16[512,1536]{1,0:T(8,128)(2,1)} custom-call(s32[1]{0:T(128)} %bitcast.2.place_ref, s32[4,160]{1,0:T(4,128)S(1)} %get-tuple-element.19.slot_ref, bf16[64,160]{1,0:T(8,128)(2,1)S(1)} %fusion.1.refs_0_, bf16[64,160]{1,0:T(8,128)(2,1)S(1)} %get-tuple-element.29.refs_1_, bf16[64,160]{1,0:T(8,128)(2,1)S(1)} %get-tuple-element.27.refs_2_, ...), custom_call_target="tpu_custom_call" | custom-call | flops 1006632960 | bytes 3538944 | tf_op jit(solution)/shard_map/pallas_call | solution.py:475
  177.3 7.5 %shard_map.123 = bf16[512,4096]{1,0:T(8,128)(2,1)} custom-call(s32[1]{0:T(128)} %bitcast.2.place_ref, s32[4,160]{1,0:T(4,128)S(1)} %get-tuple-element.19.slot_ref, bf16[64,160]{1,0:T(8,128)(2,1)S(1)} %get-tuple-element.23.refs_0_, bf16[64,160]{1,0:T(8,128)(2,1)S(1)} %get-tuple-element.28.refs_1_, bf16[64,160]{1,0:T(8,128)(2,1)S(1)} %get-tuple-element.26.refs_2_, ...), custom_call_target="tpu_custom_call" | custom-call | flops 2684354560 | bytes 9437184 | tf_op jit(solution)/shard_map/pallas_call | solution.py:475
  (33 shorter events, 0.2 us)
Async XLA Ops:
  0.6 1.2 copy-start
  1.8 0.7 copy-start.6
  2.5 0.7 copy-start.8
  3.2 0.7 copy-start.9
  6.0 39.6 %collective-permute-start = (bf16[80,1536]{1,0:T(8,128)(2,1)}, bf16[80,1536]{1,0:T(8,128)(2,1)S(1)}, u32[]{:S(2)}, u32[]{:S(2)}) collective-permute-start(bf16[80,1536]{1,0:T(8,128)(2,1)} %get-tuple-element.14), channel_id=1, source_target_pairs={{0,4},{4,0},{8,12},{12,8},{1,5},{5,1},{9,13},{13,9},{2,6},{6,2},{1... | collective-permute-start | bytes 737288 | tf_op jit(solution)/shard_map/ppermute | solution.py:518
  6.5 39.1 %collective-permute-start.1 = (bf16[80,1536]{1,0:T(8,128)(2,1)}, bf16[80,1536]{1,0:T(8,128)(2,1)S(1)}, u32[]{:S(2)}, u32[]{:S(2)}) collective-permute-start(bf16[80,1536]{1,0:T(8,128)(2,1)} %get-tuple-element.15), channel_id=1, source_target_pairs={{0,8},{4,12},{8,0},{12,4},{1,9},{5,13},{9,1},{13,5},{2,10},{6,14},... | collective-permute-start | bytes 737288 | tf_op jit(solution)/shard_map/ppermute | solution.py:518
  9.0 37.3 %collective-permute-start.2 = (bf16[80,1536]{1,0:T(8,128)(2,1)}, bf16[80,1536]{1,0:T(8,128)(2,1)S(1)}, u32[]{:S(2)}, u32[]{:S(2)}) collective-permute-start(bf16[80,1536]{1,0:T(8,128)(2,1)} %get-tuple-element.16), channel_id=1, source_target_pairs={{0,12},{4,8},{8,4},{12,0},{1,13},{5,9},{9,5},{13,1},{2,14},{6,10},... | collective-permute-start | bytes 737288 | tf_op jit(solution)/shard_map/ppermute | solution.py:518
  20.0 61.6 %collective-permute-start.10 = (bf16[160,1536]{1,0:T(8,128)(2,1)}, bf16[160,1536]{1,0:T(8,128)(2,1)}, u32[]{:S(2)}, u32[]{:S(2)}) collective-permute-start(bf16[160,1536]{1,0:T(8,128)(2,1)} %shard_map.118), channel_id=1, source_target_pairs={{0,1},{1,0},{2,3},{3,2},{4,5},{5,4},{6,7},{7,6},{8,9},{9,8},{10,11... | collective-permute-start | bytes 1474568 | tf_op jit(solution)/shard_map/ppermute | solution.py:518
  29.5 73.9 %collective-permute-start.9 = (bf16[160,1536]{1,0:T(8,128)(2,1)}, bf16[160,1536]{1,0:T(8,128)(2,1)}, u32[]{:S(2)}, u32[]{:S(2)}) collective-permute-start(bf16[160,1536]{1,0:T(8,128)(2,1)} %shard_map.117), channel_id=1, source_target_pairs={{0,1},{1,0},{2,3},{3,2},{4,5},{5,4},{6,7},{7,6},{8,9},{9,8},{10,11... | collective-permute-start | bytes 1474568 | tf_op jit(solution)/shard_map/ppermute | solution.py:518
  37.1 10.0 %copy-start.1 = (bf16[320,1536]{1,0:T(8,128)(2,1)S(1)}, bf16[320,1536]{1,0:T(8,128)(2,1)}, u32[]{:S(2)}) copy-start(bf16[320,1536]{1,0:T(8,128)(2,1)} %rows_ref.3) | copy-start | bytes 2949124
  37.1 9.9 %copy-start.7 = (s32[4,4]{1,0:T(4,128)S(1)}, s32[4,4]{1,0:T(4,128)}, u32[]{:S(2)}) copy-start(s32[4,4]{1,0:T(4,128)} %handoff_ref.5) | copy-start | bytes 196
  45.6 0.7 copy-start.2
  46.3 0.7 copy-start.4
  47.0 0.9 copy-start.3
  48.0 0.9 copy-start.5
  54.6 6.7 %collective-permute-start.6 = (f32[128,160]{1,0:T(8,128)S(1)}, f32[128,160]{1,0:T(8,128)S(1)}, u32[]{:S(2)}, u32[]{:S(2)}) collective-permute-start(f32[128,160]{1,0:T(8,128)S(1)} %pad_maximum_fusion), channel_id=1, source_target_pairs={{0,1},{1,0},{2,3},{3,2},{4,5},{5,4},{6,7},{7,6},{8,9},{9,8},{10,11... | collective-permute-start | bytes 245768 | tf_op jit(solution)/shard_map/ppermute | solution.py:518
  56.5 23.4 %collective-permute-start.7 = (f32[128,160]{1,0:T(8,128)S(1)}, f32[128,160]{1,0:T(8,128)S(1)}, u32[]{:S(2)}, u32[]{:S(2)}) collective-permute-start(f32[128,160]{1,0:T(8,128)S(1)} %pad_maximum_fusion), channel_id=1, source_target_pairs={{0,2},{1,3},{2,0},{3,1},{4,6},{5,7},{6,4},{7,5},{8,10},{9,11},{10,... | collective-permute-start | bytes 245768 | tf_op jit(solution)/shard_map/ppermute | solution.py:518
  59.1 22.3 %collective-permute-start.8 = (f32[128,160]{1,0:T(8,128)S(1)}, f32[128,160]{1,0:T(8,128)S(1)}, u32[]{:S(2)}, u32[]{:S(2)}) collective-permute-start(f32[128,160]{1,0:T(8,128)S(1)} %pad_maximum_fusion), channel_id=1, source_target_pairs={{0,3},{1,2},{2,1},{3,0},{4,7},{5,6},{6,5},{7,4},{8,11},{9,10},{10,... | collective-permute-start | bytes 245768 | tf_op jit(solution)/shard_map/ppermute | solution.py:518
  61.3 40.6 %collective-permute-start.3 = (bf16[160,1536]{1,0:T(8,128)(2,1)S(1)}, bf16[160,1536]{1,0:T(8,128)(2,1)}, u32[]{:S(2)}, u32[]{:S(2)}) collective-permute-start(bf16[160,1536]{1,0:T(8,128)(2,1)S(1)} %get-tuple-element.21.refs_0_.refs_4_), channel_id=1, source_target_pairs={{0,2},{1,3},{2,0},{3,1},{4,6},{5,7},{6,4},{7,5},{8,10},{9,11},{10,... | collective-permute-start | bytes 1474568 | tf_op jit(solution)/shard_map/ppermute | solution.py:518
  79.9 48.7 %collective-permute-start.19 = (bf16[160,4096]{1,0:T(8,128)(2,1)}, bf16[160,4096]{1,0:T(8,128)(2,1)}, u32[]{:S(2)}, u32[]{:S(2)}) collective-permute-start(bf16[160,4096]{1,0:T(8,128)(2,1)} %refs_4_.1), channel_id=1, source_target_pairs={{0,8},{4,12},{8,0},{12,4},{1,9},{5,13},{9,1},{13,5},{2,10},{6,14},... | collective-permute-start | bytes 3932168 | tf_op jit(solution)/shard_map/ppermute | solution.py:518
  81.5 17.2 %collective-permute-start.17 = (bf16[128,160]{1,0:T(8,128)(2,1)S(1)}, bf16[128,160]{1,0:T(8,128)(2,1)S(1)}, u32[]{:S(2)}, u32[]{:S(2)}) collective-permute-start(bf16[128,160]{1,0:T(8,128)(2,1)S(1)} %get-tuple-element.30), channel_id=1, source_target_pairs={{0,12},{4,8},{8,4},{12,0},{1,13},{5,9},{9,5},{13,1},{2,14},{6,10},... | collective-permute-start | bytes 122888 | tf_op jit(solution)/shard_map/ppermute | solution.py:518
  81.6 19.0 %collective-permute-start.16 = (bf16[128,160]{1,0:T(8,128)(2,1)S(1)}, bf16[128,160]{1,0:T(8,128)(2,1)}, u32[]{:S(2)}, u32[]{:S(2)}) collective-permute-start(bf16[128,160]{1,0:T(8,128)(2,1)S(1)} %get-tuple-element.30), channel_id=1, source_target_pairs={{0,8},{4,12},{8,0},{12,4},{1,9},{5,13},{9,1},{13,5},{2,10},{6,14},... | collective-permute-start | bytes 122888 | tf_op jit(solution)/shard_map/ppermute | solution.py:518
  98.7 25.2 %collective-permute-start.11 = (bf16[160,1536]{1,0:T(8,128)(2,1)}, bf16[160,1536]{1,0:T(8,128)(2,1)S(1)}, u32[]{:S(2)}, u32[]{:S(2)}) collective-permute-start(bf16[160,1536]{1,0:T(8,128)(2,1)} %shard_map.119), channel_id=1, source_target_pairs={{0,2},{1,3},{2,0},{3,1},{4,6},{5,7},{6,4},{7,5},{8,10},{9,11},{10,... | collective-permute-start | bytes 1474568 | tf_op jit(solution)/shard_map/ppermute | solution.py:518
  100.6 28.8 %collective-permute-start.5 = (bf16[160,1536]{1,0:T(8,128)(2,1)S(1)}, bf16[160,1536]{1,0:T(8,128)(2,1)S(1)}, u32[]{:S(2)}, u32[]{:S(2)}) collective-permute-start(bf16[160,1536]{1,0:T(8,128)(2,1)S(1)} %get-tuple-element.21.refs_0_.refs_4_), channel_id=1, source_target_pairs={{0,1},{1,0},{2,3},{3,2},{4,5},{5,4},{6,7},{7,6},{8,9},{9,8},{10,11... | collective-permute-start | bytes 1474568 | tf_op jit(solution)/shard_map/ppermute | solution.py:518
  101.9 33.1 %collective-permute-start.4 = (bf16[160,1536]{1,0:T(8,128)(2,1)}, bf16[160,1536]{1,0:T(8,128)(2,1)S(1)}, u32[]{:S(2)}, u32[]{:S(2)}) collective-permute-start(bf16[160,1536]{1,0:T(8,128)(2,1)} %collective-permute-done.3.refs_0_), channel_id=1, source_target_pairs={{0,1},{1,0},{2,3},{3,2},{4,5},{5,4},{6,7},{7,6},{8,9},{9,8},{10,11... | collective-permute-start | bytes 1474568 | tf_op jit(solution)/shard_map/ppermute | solution.py:518
  103.4 73.9 %collective-permute-start.22 = (bf16[160,4096]{1,0:T(8,128)(2,1)}, bf16[160,4096]{1,0:T(8,128)(2,1)S(1)}, u32[]{:S(2)}, u32[]{:S(2)}) collective-permute-start(bf16[160,4096]{1,0:T(8,128)(2,1)} %refs_4_.1), channel_id=1, source_target_pairs={{0,4},{4,0},{8,12},{12,8},{1,5},{5,1},{9,13},{13,9},{2,6},{6,2},{1... | collective-permute-start | bytes 3932168 | tf_op jit(solution)/shard_map/ppermute | solution.py:518
  124.0 5.2 %collective-permute-start.15 = (bf16[128,160]{1,0:T(8,128)(2,1)S(1)}, bf16[128,160]{1,0:T(8,128)(2,1)S(1)}, u32[]{:S(2)}, u32[]{:S(2)}) collective-permute-start(bf16[128,160]{1,0:T(8,128)(2,1)S(1)} %get-tuple-element.30), channel_id=1, source_target_pairs={{0,4},{4,0},{8,12},{12,8},{1,5},{5,1},{9,13},{13,9},{2,6},{6,2},{1... | collective-permute-start | bytes 122888 | tf_op jit(solution)/shard_map/ppermute | solution.py:518
  128.6 19.0 %collective-permute-start.13 = (bf16[160,1536]{1,0:T(8,128)(2,1)S(1)}, bf16[160,1536]{1,0:T(8,128)(2,1)S(1)}, u32[]{:S(2)}, u32[]{:S(2)}) collective-permute-start(bf16[160,1536]{1,0:T(8,128)(2,1)S(1)} %shard_map.120.refs_0_), channel_id=1, source_target_pairs={{0,8},{4,12},{8,0},{12,4},{1,9},{5,13},{9,1},{13,5},{2,10},{6,14},... | collective-permute-start | bytes 1474568 | tf_op jit(solution)/shard_map/ppermute | solution.py:518
  129.2 18.9 %collective-permute-start.12 = (bf16[160,1536]{1,0:T(8,128)(2,1)S(1)}, bf16[160,1536]{1,0:T(8,128)(2,1)S(1)}, u32[]{:S(2)}, u32[]{:S(2)}) collective-permute-start(bf16[160,1536]{1,0:T(8,128)(2,1)S(1)} %shard_map.120.refs_0_), channel_id=1, source_target_pairs={{0,4},{4,0},{8,12},{12,8},{1,5},{5,1},{9,13},{13,9},{2,6},{6,2},{1... | collective-permute-start | bytes 1474568 | tf_op jit(solution)/shard_map/ppermute | solution.py:518
  129.4 23.4 %collective-permute-start.20 = (bf16[160,1536]{1,0:T(8,128)(2,1)S(1)}, bf16[160,1536]{1,0:T(8,128)(2,1)S(1)}, u32[]{:S(2)}, u32[]{:S(2)}) collective-permute-start(bf16[160,1536]{1,0:T(8,128)(2,1)S(1)} %get-tuple-element.21.refs_0_.refs_4_), channel_id=1, source_target_pairs={{0,8},{4,12},{8,0},{12,4},{1,9},{5,13},{9,1},{13,5},{2,10},{6,14},... | collective-permute-start | bytes 1474568 | tf_op jit(solution)/shard_map/ppermute | solution.py:518
  135.0 42.4 %collective-permute-start.23 = (bf16[160,4096]{1,0:T(8,128)(2,1)}, bf16[160,4096]{1,0:T(8,128)(2,1)S(1)}, u32[]{:S(2)}, u32[]{:S(2)}) collective-permute-start(bf16[160,4096]{1,0:T(8,128)(2,1)} %collective-permute-done.19.refs_6_), channel_id=1, source_target_pairs={{0,4},{4,0},{8,12},{12,8},{1,5},{5,1},{9,13},{13,9},{2,6},{6,2},{1... | collective-permute-start | bytes 3932168 | tf_op jit(solution)/shard_map/ppermute | solution.py:518
  147.6 26.5 %collective-permute-start.18 = (bf16[160,1536]{1,0:T(8,128)(2,1)S(1)}, bf16[160,1536]{1,0:T(8,128)(2,1)S(1)}, u32[]{:S(2)}, u32[]{:S(2)}) collective-permute-start(bf16[160,1536]{1,0:T(8,128)(2,1)S(1)} %get-tuple-element.21.refs_0_.refs_4_), channel_id=1, source_target_pairs={{0,4},{4,0},{8,12},{12,8},{1,5},{5,1},{9,13},{13,9},{2,6},{6,2},{1... | collective-permute-start | bytes 1474568 | tf_op jit(solution)/shard_map/ppermute | solution.py:518
  148.1 23.2 %collective-permute-start.14 = (bf16[160,1536]{1,0:T(8,128)(2,1)S(1)}, bf16[160,1536]{1,0:T(8,128)(2,1)S(1)}, u32[]{:S(2)}, u32[]{:S(2)}) collective-permute-start(bf16[160,1536]{1,0:T(8,128)(2,1)S(1)} %collective-permute-done.13.refs_2_), channel_id=1, source_target_pairs={{0,4},{4,0},{8,12},{12,8},{1,5},{5,1},{9,13},{13,9},{2,6},{6,2},{1... | collective-permute-start | bytes 1474568 | tf_op jit(solution)/shard_map/ppermute | solution.py:518
  152.8 21.3 %collective-permute-start.21 = (bf16[160,1536]{1,0:T(8,128)(2,1)S(1)}, bf16[160,1536]{1,0:T(8,128)(2,1)S(1)}, u32[]{:S(2)}, u32[]{:S(2)}) collective-permute-start(bf16[160,1536]{1,0:T(8,128)(2,1)S(1)} %collective-permute-done.20.refs_6_), channel_id=1, source_target_pairs={{0,4},{4,0},{8,12},{12,8},{1,5},{5,1},{9,13},{13,9},{2,6},{6,2},{1... | collective-permute-start | bytes 1474568 | tf_op jit(solution)/shard_map/ppermute | solution.py:518

commit v2 on v1

--- a/solution.py
+++ b/solution.py
@@ -163,12 +163,12 @@
     return (outputs, row_grad, grad_a, grad_b)
 
 
-def params():
-    return pltpu.CompilerParams(vmem_limit_bytes=VMEM_LIMIT)
+def params(limit=VMEM_LIMIT):
+    return pltpu.CompilerParams(vmem_limit_bytes=limit)
 
 
 def cost(flops, moved):
-    return pl.CostEstimate(flops=int(flops), bytes_accessed=int(moved), transcendentals=0)
+    return pl.CostEstimate(flops=int(flops) // 1000, bytes_accessed=int(moved) // 1000, transcendentals=0)
 
 
 SMEM = functools.partial(pl.BlockSpec, memory_space=pltpu.SMEM)
@@ -234,7 +234,7 @@
         in_specs=[SMEM(), SMEM(), SMEM(), pl.BlockSpec(memory_space=pltpu.VMEM), pl.BlockSpec(memory_space=pltpu.VMEM)],
         out_shape=[jax.ShapeDtypeStruct((half, width), BF)] * (groups - 1)
         + [jax.ShapeDtypeStruct((groups, balanced), I32)] * 2,
-        compiler_params=params(),
+        compiler_params=params(60 * 2**20),
         cost_estimate=cost(2 * 3 * half * capacity * width, 2 * capacity * width * 2),
     )(place, handoff, slots, counts, rows)
 
@@ -299,32 +299,39 @@
     )(place, handoff, tenant, rows, *arrived, down)
 
 
-def rank_backward(tenant, turned, up, rank, block):
-    balanced = turned.shape[1]
+def rank_backward(tenant, turned, up, lowered, block):
+    rank, balanced = lowered.shape
     hidden = up.shape[1]
-
-    def kernel(tenant_ref, turned_ref, up_ref, out_ref):
+    steps = up.shape[0] // block
+
+    def kernel(tenant_ref, turned_ref, lowered_ref, up_ref, out_ref, total_ref):
         step = pl.program_id(0)
-        product = jnp.dot(up_ref[...], turned_ref[...], preferred_element_type=F32)
-        mine = masked_rank(product, tenant_ref[0:1, :], step * (block // rank), rank)
 
         @pl.when(step == 0)
         def _():
-            out_ref[...] = mine
-
-        @pl.when(step > 0)
+            total_ref[:rank, :] = lowered_ref[...]
+            total_ref[rank:, :] = jnp.zeros((rank, balanced), F32)
+
+        product = jnp.dot(up_ref[...], turned_ref[...], preferred_element_type=F32)
+        total_ref[rank:, :] += masked_rank(product, tenant_ref[0:1, :], step * (block // rank), rank)
+
+        @pl.when(step == steps - 1)
         def _():
-            out_ref[...] += mine
-
-    return pl.pallas_call(
-        kernel,
-        grid=(up.shape[0] // block,),
-        in_specs=[whole(tenant.shape), whole(turned.shape), pl.BlockSpec((block, hidden), lambda i: (i, 0))],
-        out_specs=whole((rank, balanced)),
-        out_shape=jax.ShapeDtypeStruct((rank, balanced), F32),
+            out_ref[...] = total_ref[...].T
+
+    return pl.pallas_call(
+        kernel,
+        grid=(steps,),
+        in_specs=[
+            whole(tenant.shape), whole(turned.shape), whole(lowered.shape),
+            pl.BlockSpec((block, hidden), lambda i: (i, 0)),
+        ],
+        out_specs=whole((balanced, 2 * rank)),
+        out_shape=jax.ShapeDtypeStruct((balanced, 2 * rank), F32),
+        scratch_shapes=[pltpu.VMEM((2 * rank, balanced), F32)],
         compiler_params=params(),
         cost_estimate=cost(2 * balanced * up.size, 2 * up.size),
-    )(tenant, turned, up)
+    )(tenant, turned, lowered, up)
 
 
 def base_gradient(owner, turned, weight, width, block, arrived=None):
@@ -356,17 +363,68 @@
     )(owner, turned, weight, *(() if arrived is None else (arrived,)))
 
 
-def spread(wide_ref, column_ref, twice_ref, tenants, rank):
-    lanes = 2 * rank
-    odd = (lax.broadcasted_iota(I32, (column_ref.shape[0], lanes), 1) >= rank).astype(I32)
-    label = column_ref[...] - odd
+def spread(wide_ref, tenant_ref, ranks_ref, second, scale, tenants, rank):
+    balanced, lanes = ranks_ref.shape
+    vectors = scale * ranks_ref[...].astype(F32)
+    turned = pltpu.roll(vectors, rank, 1)
+    high = lax.broadcasted_iota(I32, (balanced, lanes), 1) >= rank
+    twice = jnp.where(high, vectors, turned) if second else jnp.where(high, turned, vectors)
+    half = (lax.broadcasted_iota(I32, (lanes, balanced), 0) >= rank).astype(F32)
+    label = (tenant_ref[0:1, :].astype(F32) - half).T
     for pair in range(tenants // 2):
-        wide_ref[:, pair * lanes : (pair + 1) * lanes] = jnp.where(
-            label == 2 * pair, twice_ref[...].astype(F32), 0.0
-        ).astype(BF)
-
-
-def forward(owners, parts, weight, block, total=None, column=None, twice=None, up=None, rank=None):
+        wide_ref[:, pair * lanes : (pair + 1) * lanes] = jnp.where(label == 2.0 * pair, twice, 0.0).astype(BF)
+
+
+def own_and_forward(owners, parts, turned, weight, block):
+    balanced, width = parts[0].shape
+    hidden = weight.shape[1]
+    steps = hidden // block
+
+    def kernel(owners_ref, first_ref, second_ref, turned_ref, mine_ref, other_ref, total_ref, own_ref, sum_ref):
+        step = pl.program_id(0)
+        piece = jnp.dot(mine_ref[...], turned_ref[...], preferred_element_type=F32)
+
+        @pl.when(step == 0)
+        def _():
+            sum_ref[...] = piece
+
+        @pl.when(step > 0)
+        def _():
+            sum_ref[...] += piece
+
+        total_ref[...] = jnp.dot(
+            first_ref[...], mine_ref[...], preferred_element_type=F32
+        ) + jnp.dot(second_ref[...], other_ref[...], preferred_element_type=F32)
+
+        @pl.when(step == steps - 1)
+        def _():
+            own_ref[...] = sum_ref[...].T.astype(BF)
+
+    return pl.pallas_call(
+        kernel,
+        grid_spec=pltpu.PrefetchScalarGridSpec(
+            num_scalar_prefetch=1,
+            grid=(steps,),
+            in_specs=[
+                whole((balanced, width)),
+                whole((balanced, width)),
+                pl.BlockSpec((block, balanced), lambda n, o: (n, 0)),
+                pl.BlockSpec((width, block), lambda n, o: (o[0], n)),
+                pl.BlockSpec((width, block), lambda n, o: (o[1], n)),
+            ],
+            out_specs=[pl.BlockSpec((balanced, block), lambda n, o: (0, n)), whole((balanced, width))],
+            scratch_shapes=[pltpu.VMEM((width, balanced), F32)],
+        ),
+        out_shape=[
+            jax.ShapeDtypeStruct((balanced, hidden), F32),
+            jax.ShapeDtypeStruct((balanced, width), BF),
+        ],
+        compiler_params=params(),
+        cost_estimate=cost(6 * balanced * width * hidden, 4 * width * hidden),
+    )(owners, *parts, turned, weight, weight)
+
+
+def forward(owners, parts, weight, block, total=None, tenant=None, ranks=None, up=None):
     balanced, width = parts[0].shape
     hidden = weight.shape[1]
     count = len(parts)
@@ -381,12 +439,13 @@
         if total is not None:
             value = value + rest.pop(0)[...]
         if last:
-            column_ref, twice_ref, up_ref = rest.pop(0), rest.pop(0), rest.pop(0)
+            tenant_ref, ranks_ref, up_ref = rest.pop(0), rest.pop(0), rest.pop(0)
             wide_ref = rest.pop()
 
             @pl.when(pl.program_id(0) == 0)
             def _():
-                spread(wide_ref, column_ref, twice_ref, up.shape[0] // rank, rank)
+                rank = ranks.shape[1] // 2
+                spread(wide_ref, tenant_ref, ranks_ref, False, adapter_scale, up.shape[0] // rank, rank)
 
             value = value + jnp.dot(wide_ref[...], up_ref[...], preferred_element_type=F32)
         rest[0][...] = value.astype(rest[0].dtype)
@@ -400,8 +459,8 @@
         in_specs.append(piece)
         operands.append(total)
     if last:
-        in_specs += [whole(column.shape), whole(twice.shape), pl.BlockSpec((up.shape[0], block), lambda i, o: (0, i))]
-        operands += [column, twice, up]
+        in_specs += [whole(tenant.shape), whole(ranks.shape), pl.BlockSpec((up.shape[0], block), lambda i, o: (0, i))]
+        operands += [tenant, ranks, up]
     return pl.pallas_call(
         kernel,
         grid_spec=pltpu.PrefetchScalarGridSpec(
@@ -420,39 +479,40 @@
     )(owners, *operands)
 
 
-def finish_gradient(terms, column, twice, down, block, rank):
+def finish_gradient(terms, tenant, ranks, down, block):
     balanced, width = terms[0].shape
 
-    def kernel(column_ref, twice_ref, down_ref, *refs):
+    lanes = ranks.shape[1]
+    rank = lanes // 2
+
+    def kernel(tenant_ref, ranks_ref, down_ref, *refs):
         term_refs, out_ref, wide_ref = refs[:-2], refs[-2], refs[-1]
-
-        @pl.when(pl.program_id(0) == 0)
-        def _():
-            spread(wide_ref, column_ref, twice_ref, down.shape[0] // rank, rank)
-
-        value = jnp.dot(wide_ref[...], down_ref[...], preferred_element_type=F32)
-        for term_ref in term_refs:
-            value = value + term_ref[...].astype(F32)
-        out_ref[...] = value.astype(BF)
-
-    piece = pl.BlockSpec((balanced, block), lambda i: (0, i))
-    return pl.pallas_call(
-        kernel,
-        grid=(width // block,),
-        in_specs=[whole(column.shape), whole(twice.shape), pl.BlockSpec((down.shape[0], block), lambda i: (0, i))]
-        + [piece] * len(terms),
-        out_specs=piece,
-        out_shape=jax.ShapeDtypeStruct((balanced, width), BF),
+        spread(wide_ref, tenant_ref, ranks_ref, True, 1.0, down.shape[0] // rank, rank)
+        for start in range(0, width, block):
+            at = pl.ds(start, block)
+            value = jnp.dot(wide_ref[...], down_ref[:, at], preferred_element_type=F32)
+            for term_ref in term_refs:
+                value = value + term_ref[:, at].astype(F32)
+            out_ref[:, at] = value.astype(BF)
+        out_ref[:, pl.ds(width, lanes)] = ranks_ref[...]
+
+    return pl.pallas_call(
+        kernel,
+        grid=(1,),
+        in_specs=[whole(tenant.shape), whole(ranks.shape), whole(down.shape)] + [whole((balanced, width))] * len(terms),
+        out_specs=whole((balanced, width + lanes)),
+        out_shape=jax.ShapeDtypeStruct((balanced, width + lanes), BF),
         scratch_shapes=[pltpu.VMEM((balanced, down.shape[0]), BF)],
         compiler_params=params(),
         cost_estimate=cost(2 * balanced * down.size, 2 * down.size),
-    )(column, twice, down, *terms)
-
-
-def owned_gradient(place, slot, ranks, values, share, scale, block):
+    )(tenant, ranks, down, *terms)
+
+
+def owned_gradient(place, slot, bundles, second, values, share, lanes, scale, block):
     groups, balanced = slot.shape
-    rank = ranks[0].shape[0]
+    rank = lanes // 2
     width = values[0].shape[1]
+    column = bundles[0].shape[1] // lanes - 1
 
     def kernel(place_ref, slot_ref, *refs):
         rank_refs, value_refs = refs[:groups], refs[groups : 2 * groups]
@@ -462,9 +522,11 @@
         def _():
             first = place_ref[0] * share
             for k in range(groups):
+                turned = rank_refs[k][...].astype(F32).T
+                mine = turned[rank:, :] if second else turned[:rank, :]
                 for s in range(share):
                     wide_ref[k, s * rank : (s + 1) * rank, :] = jnp.where(
-                        slot_ref[k : k + 1, :] == first + s, rank_refs[k][...].astype(F32), 0.0
+                        slot_ref[k : k + 1, :] == first + s, mine, 0.0
                     ).astype(BF)
 
         value = jnp.dot(wide_ref[0], value_refs[0][...], preferred_element_type=F32)
@@ -476,18 +538,18 @@
         kernel,
         grid=(width // block,),
         in_specs=[SMEM(), whole(slot.shape)]
-        + [whole((rank, balanced))] * groups
+        + [pl.BlockSpec((balanced, lanes), lambda i: (0, column))] * groups
         + [pl.BlockSpec((balanced, block), lambda i: (0, i))] * groups,
         out_specs=pl.BlockSpec((share * rank, block), lambda i: (0, i)),
         out_shape=jax.ShapeDtypeStruct((share * rank, width), BF),
         scratch_shapes=[pltpu.VMEM((groups, share * rank, balanced), BF)],
         compiler_params=params(),
         cost_estimate=cost(2 * groups * balanced * share * rank * width, 2 * width * (groups * balanced + share * rank)),
-    )(place, slot, *ranks, *values)
-
-
-def bring_home(place, handoff, gradients, capacity):
-    balanced, width = gradients[0].shape
+    )(place, slot, *bundles, *values)
+
+
+def bring_home(place, handoff, bundles, capacity, width):
+    balanced = bundles[0].shape[0]
     groups = handoff.shape[0]
 
     def kernel(place_ref, handoff_ref, *refs):
@@ -506,11 +568,13 @@
 
     return pl.pallas_call(
         kernel,
-        in_specs=[SMEM(), SMEM()] + [pl.BlockSpec(memory_space=pltpu.VMEM)] * groups,
+        grid=(1,),
+        in_specs=[SMEM(), SMEM()] + [whole((balanced, width))] * groups,
+        out_specs=whole((capacity, width)),
         out_shape=jax.ShapeDtypeStruct((capacity, width), BF),
         compiler_params=params(),
         cost_estimate=cost(2 * groups * balanced * capacity * width, 4 * groups * balanced * width),
-    )(place, handoff, *gradients)
+    )(place, handoff, *bundles)
 
 
 def swap(values, axis, distance):
@@ -550,50 +614,63 @@
     arrived = [None] * 3
     for k in (2, 3, 1):
         arrived[k - 1] = swap(outgoing[k - 1], "dp", k)
-
-    far = base_gradient(owner[3].reshape(1), turned, frozen_weight, width, 512)
+    far = base_gradient(owner[3].reshape(1), after(turned, *outgoing), frozen_weight, width, 512)
     for_far = swap(far, "fsdp", 1)
-    near = base_gradient(owner[1].reshape(1), turned, frozen_weight, width, 512)
+    near = base_gradient(owner[1].reshape(1), turned, after(frozen_weight, far), width, 512)
     from_near = swap(near, "fsdp", 1)
-    raised = rank_backward(tenant, turned, up, rank, 512)
-    gathered, lowered = unpack(place, handoff_counts, tenant, input_rows, arrived, down, rank, 512)
+    gathered, lowered = unpack(
+        place, handoff_counts, tenant, input_rows, arrived, after(down, near, *arrived), rank, 512
+    )
+    beside = swap(gathered, "fsdp", 1)
     pair = swap(gathered, "fsdp", 2)
-    beside = swap(gathered, "fsdp", 1)
-    across = base_gradient(owner[2].reshape(1), turned, frozen_weight, width, 512, for_far)
-    from_pair = swap(across, "fsdp", 2)
-    cot_x = swap(after(cotangent, gathered), "dp", 2)
-    diagonal = swap(pair, "fsdp", 1)
-
-    partial = jnp.concatenate([lowered, raised], axis=0)
-    summed = partial + swap(partial, "fsdp", 1)
-    summed = summed + swap(partial, "fsdp", 2) + swap(partial, "fsdp", 3)
-    lora_in = summed[:rank].astype(BF)
-    lora_grad = (adapter_scale * summed[rank:]).astype(BF)
-    ranks = jnp.concatenate([lora_in, lora_grad], axis=0)
-    all_ranks = [ranks] + [swap(ranks, "dp", k) for k in (1, 2, 3)]
-    column = tenant[0].reshape(balanced, 1)
-    twice_in = jnp.concatenate([lora_in * jnp.asarray(adapter_scale, BF)] * 2, axis=0).T
-    twice_grad = jnp.concatenate([lora_grad] * 2, axis=0).T
-
-    own = base_gradient(owner[0].reshape(1), turned, frozen_weight, width, 512)
-    total = forward(jnp.stack([owner[0], owner[1]]), [gathered, beside], frozen_weight, 512)
-    group_gradient = finish_gradient([own, from_near, from_pair], column, twice_grad, down, 512, rank)
-
-    gathered_x = swap(after(gathered, cot_x), "dp", 2)
-    cot_all = [cotangent, swap(cotangent, "dp", 1), cot_x, swap(cot_x, "dp", 1)]
-    gathered_all = [gathered, swap(gathered, "dp", 1), gathered_x, swap(gathered_x, "dp", 1)]
-    back_x = swap(group_gradient, "dp", 2)
-    back = [group_gradient, swap(group_gradient, "dp", 1), back_x, swap(back_x, "dp", 1)]
-
+    cot_x = swap(after(cotangent, *arrived, far), "dp", 2)
+    partial = rank_backward(tenant, turned, after(up, gathered, for_far), lowered, 512)
+    across = base_gradient(
+        owner[2].reshape(1), turned, after(frozen_weight, partial), width, 512, for_far
+    )
+    late = after(partial, across, cot_x, from_near)
+    sums = [swap(late, "fsdp", k) for k in (1, 2, 3)]
+    from_pair = swap(after(across, from_near, cot_x), "fsdp", 2)
+    total, own = own_and_forward(
+        jnp.stack([owner[0], owner[1]]), [gathered, beside], turned, after(frozen_weight, across), 512
+    )
+    diagonal = swap(after(pair, total), "fsdp", 1)
+    gathered_x = swap(after(gathered, total), "dp", 2)
+    scale = jnp.where(jnp.arange(2 * rank) < rank, 1.0, adapter_scale).astype(F32)
+    ranks = ((after(partial, total, from_pair) + sums[0] + (sums[1] + sums[2])) * scale).astype(BF)
+    bundle = finish_gradient([own, from_near, from_pair], tenant, ranks, after(down, total), 512)
+    bundle_x = swap(bundle, "dp", 2)
+    bundle_c = swap(bundle, "dp", 1)
+    cot_all = [
+        cotangent,
+        swap(after(cotangent, bundle), "dp", 1),
+        cot_x,
+        swap(after(cot_x, bundle), "dp", 1),
+    ]
     outputs = forward(
-        jnp.stack([owner[2], owner[3]]), [pair, diagonal], frozen_weight, 512,
-        total, column, twice_in, up, rank,
-    )
+        jnp.stack([owner[2], owner[3]]),
+        [pair, diagonal],
+        after(frozen_weight, bundle, diagonal),
+        512,
+        total,
+        tenant,
+        ranks,
+        up,
+    )
+    bundles = [bundle, bundle_c, bundle_x, swap(after(bundle_x, outputs), "dp", 1)]
+    gathered_all = [
+        gathered,
+        swap(after(gathered, outputs), "dp", 1),
+        gathered_x,
+        swap(after(gathered_x, outputs), "dp", 1),
+    ]
     grad_b = owned_gradient(
-        place, slot, [r[:rank] for r in all_ranks], cot_all, share, adapter_scale, 1024
-    )
-    grad_a = owned_gradient(place, slot, [r[rank:] for r in all_ranks], gathered_all, share, 1.0, 512)
-    row_grad = bring_home(place, handoff_counts, back, capacity)
+        place, slot, after(bundles, outputs), False, cot_all, share, 2 * rank, adapter_scale, 1024
+    )
+    grad_a = owned_gradient(
+        place, slot, after(bundles, grad_b), True, gathered_all, share, 2 * rank, 1.0, 512
+    )
+    row_grad = bring_home(place, handoff_counts, after(bundles, grad_a), capacity, width)
     return (
         outputs,
         row_grad,

time: 188 us -> 141 us (0.75); the launches traced: 185 us -> 141 us
  waiting for transfers between devices: 57.7 us -> 16.3 us
  local copies, waits for them, and re-layouts: 10.7 us -> 4.16 us
  Pallas kernels: 95.9 us -> 98.7 us
    ppermute x24 -> x21, waiting for transfers between devices: 57.7 us -> 16.3 us  [swap(): return lax.ppermute(values, axis, [(i, i ^ distance) for i in range(size)])]
    pallas_call x3 -> x4, Pallas kernels: 15.8 us -> 36.3 us  [the longest x1 20.8 us: own_and_forward(): pl.pallas_call(kernel, grid_spec=pltpu.PrefetchScalarGridSpec(num_scalar_...]
    pallas_call x2 -> x1, Pallas kernels: 31.1 us -> 18.5 us  [forward(): pl.pallas_call(kernel, grid_spec=pltpu.PrefetchScalarGridSpec(num_scalar_...]
    pallas_call x4 -> x3, Pallas kernels: 30.4 us -> 22.8 us  [base_gradient(): pl.pallas_call(kernel, grid_spec=pltpu.PrefetchScalarGridSpec(num_scalar_...]
    unnamed x21 -> x13, local copies, waits for them, and re-layouts: 9.58 us -> 4.16 us
    ppermute x24 -> x21, starting transfers between devices: 19.4 us -> 20.7 us  [swap(): return lax.ppermute(values, axis, [(i, i ^ distance) for i in range(size)])]
  transfers between devices with their start and end apart: 24 -> 21, of which waited for: 7 -> 6; matrix products, arithmetic and copies ran while one was open for 2% -> 2% of each run, Pallas kernels for 47% -> 63%
where the time goes in v2:
time: 141 us
  Pallas kernels  98.7 us (70%)
  starting transfers between devices  20.7 us (15%)
  waiting for transfers between devices  16.3 us (12%)
  local copies, waits for them, and re-layouts  4.16 us (3%)
    pallas_call x3, Pallas kernels, base_gradient(): pl.pallas_call(kernel, grid_spec=pltpu.PrefetchScalarGridSpec(num_scalar_...  22.8 us
    pallas_call x1, Pallas kernels, own_and_forward(): pl.pallas_call(kernel, grid_spec=pltpu.PrefetchScalarGridSpec(num_scalar_...  20.8 us
    ppermute x21, starting transfers between devices, swap(): return lax.ppermute(values, axis, [(i, i ^ distance) for i in range(size)])  20.7 us
    pallas_call x1, Pallas kernels, forward(): pl.pallas_call(kernel, grid_spec=pltpu.PrefetchScalarGridSpec(num_scalar_...  18.5 us
    ppermute x21, waiting for transfers between devices, swap(): return lax.ppermute(values, axis, [(i, i ^ distance) for i in range(size)])  16.3 us
    pallas_call x2, Pallas kernels, owned_gradient(): pl.pallas_call(kernel, grid=(width // block,), in_specs=[SMEM(), whole(sl...  12.2 us
    pallas_call x1, Pallas kernels, rank_backward(): pl.pallas_call(kernel, grid=(steps,), in_specs=[whole(tenant.shape), whol...  8.51 us
    pallas_call x1, Pallas kernels, unpack(): pl.pallas_call(kernel, grid=(down.shape[0] // block,), in_specs=[SMEM(),...  6.08 us
  transfers between devices with their start and end apart: 21, of which 6 were waited for; matrix products, arithmetic and copies ran while one was open for 2% of the time, Pallas kernels for 63%

profile of v2, /device:TPU:0, one launch (start us, length us, event | category | flops | bytes accessed | tf_op | source)
XLA Modules:
  0.0 140.8 jit_solution(3059797829904731311)
XLA Ops:
  0.6 2.8 %shard_map.111 = (bf16[80,1536]{1,0:T(8,128)(2,1)}, bf16[80,1536]{1,0:T(8,128)(2,1)}, bf16[80,1536]{1,0:T(8,128)(2,1)}, s32[4,160]{1,0:T(4,128)}, s32[4,160]{1,0:T(4,128)}) custom-call(s32[1]{0:T(128)} %bitcast.2.place_ref, s32[4,4]{1,0:T(4,128)} %handoff_ref.5, s32[32]{0:T(128)} %slots_ref.1, s32[4,32]{1,0:T(4,128)} %counts_ref.1, bf16[320,1536]{1,0:T(8,128)(2,1)} %rows_ref.3), custom_call_target="tpu_custom_call" | custom-call | flops 235929 | bytes 1966 | tf_op jit(solution)/shard_map/pallas_call | solution.py:232
  3.5 0.4 collective-permute-start
  3.9 2.5 %collective-permute-start.1 = (bf16[80,1536]{1,0:T(8,128)(2,1)}, bf16[80,1536]{1,0:T(8,128)(2,1)}, u32[]{:S(2)}, u32[]{:S(2)}) collective-permute-start(bf16[80,1536]{1,0:T(8,128)(2,1)} %get-tuple-element.46), channel_id=1, source_target_pairs={{0,8},{4,12},{8,0},{12,4},{1,9},{5,13},{9,1},{13,5},{2,10},{6,14},... | collective-permute-start | bytes 737288 | tf_op jit(solution)/shard_map/ppermute | solution.py:582
  6.4 0.1 collective-permute-start.2
  6.5 3.1 %copy.12 = bf16[160,4096]{0,1:T(8,128)(2,1)S(1)} copy(bf16[160,4096]{1,0:T(8,128)(2,1)} %refs_4_.1) | data formatting | bytes 2621440 | tf_op args[1]
  9.6 0.0 copy-start
  9.6 7.9 %shard_map.112 = bf16[160,1536]{1,0:T(8,128)(2,1)} custom-call(s32[1]{0:T(128)} %bitcast.1.owner_ref, bf16[4096,160]{1,0:T(8,128)(2,1)S(1)} %bitcast.14, bf16[6144,4096]{1,0:T(8,128)(2,1)} %refs_3_), custom_call_target="tpu_custom_call" | custom-call | flops 2013265 | bytes 12582 | tf_op jit(solution)/shard_map/pallas_call | solution.py:348
  17.5 0.0 collective-permute-done.refs_0_
  17.5 0.0 collective-permute-done.1.refs_1_
  17.5 0.8 collective-permute-done.2.refs_2_
  18.4 0.0 copy-done
  18.4 1.5 %collective-permute-start.8 = (bf16[160,4096]{1,0:T(8,128)(2,1)S(1)}, bf16[160,4096]{1,0:T(8,128)(2,1)}, u32[]{:S(2)}, u32[]{:S(2)}) collective-permute-start(bf16[160,4096]{1,0:T(8,128)(2,1)S(1)} %copy-done), channel_id=1, source_target_pairs={{0,8},{4,12},{8,0},{12,4},{1,9},{5,13},{9,1},{13,5},{2,10},{6,14},... | collective-permute-start | bytes 3932168 | tf_op jit(solution)/shard_map/ppermute | solution.py:582
  19.9 1.6 %collective-permute-start.5 = (bf16[160,1536]{1,0:T(8,128)(2,1)}, bf16[160,1536]{1,0:T(8,128)(2,1)}, u32[]{:S(2)}, u32[]{:S(2)}) collective-permute-start(bf16[160,1536]{1,0:T(8,128)(2,1)} %shard_map.112), channel_id=1, source_target_pairs={{0,1},{1,0},{2,3},{3,2},{4,5},{5,4},{6,7},{7,6},{8,9},{9,8},{10,11... | collective-permute-start | bytes 1474568 | tf_op jit(solution)/shard_map/ppermute | solution.py:582
  21.5 7.8 %shard_map.113 = bf16[160,1536]{1,0:T(8,128)(2,1)} custom-call(s32[1]{0:T(128)} %bitcast.5.owner_ref, bf16[4096,160]{1,0:T(8,128)(2,1)S(1)} %bitcast.15, bf16[6144,4096]{1,0:T(8,128)(2,1)} %refs_3_), custom_call_target="tpu_custom_call" | custom-call | flops 2013265 | bytes 12582 | tf_op jit(solution)/shard_map/pallas_call | solution.py:348
  29.4 0.4 collective-permute-start.7
  29.8 0.0 copy-done.1
  29.8 0.0 copy-done.2
  29.8 0.0 copy-done.3
  29.8 6.1 %shard_map.114 = (bf16[160,1536]{1,0:T(8,128)(2,1)}, f32[64,160]{1,0:T(8,128)S(1)}) custom-call(s32[1]{0:T(128)} %bitcast.2.place_ref, s32[4,4]{1,0:T(4,128)S(1)} %copy-done.3, s32[4,160]{1,0:T(4,128)S(1)} %copy-done.2, bf16[320,1536]{1,0:T(8,128)(2,1)S(1)} %copy-done.1, bf16[80,1536]{1,0:T(8,128)(2,1)} %collective-permute-done.refs_0_, ...), custom_call_target="tpu_custom_call" | custom-call | flops 1006632 | bytes 7766 | tf_op jit(solution)/shard_map/pallas_call | solution.py:285
  35.9 1.6 %collective-permute-start.4 = (bf16[160,1536]{1,0:T(8,128)(2,1)}, bf16[160,1536]{1,0:T(8,128)(2,1)}, u32[]{:S(2)}, u32[]{:S(2)}) collective-permute-start(bf16[160,1536]{1,0:T(8,128)(2,1)} %get-tuple-element.78.first_ref.refs_4_), channel_id=1, source_target_pairs={{0,1},{1,0},{2,3},{3,2},{4,5},{5,4},{6,7},{7,6},{8,9},{9,8},{10,11... | collective-permute-start | bytes 1474568 | tf_op jit(solution)/shard_map/ppermute | solution.py:582
  37.5 2.6 %collective-permute-start.3 = (bf16[160,1536]{1,0:T(8,128)(2,1)}, bf16[160,1536]{1,0:T(8,128)(2,1)S(1)}, u32[]{:S(2)}, u32[]{:S(2)}) collective-permute-start(bf16[160,1536]{1,0:T(8,128)(2,1)} %get-tuple-element.78.first_ref.refs_4_), channel_id=1, source_target_pairs={{0,2},{1,3},{2,0},{3,1},{4,6},{5,7},{6,4},{7,5},{8,10},{9,11},{10,... | collective-permute-start | bytes 1474568 | tf_op jit(solution)/shard_map/ppermute | solution.py:582
  40.1 0.0 collective-permute-done.5.refs_0_
  40.1 8.5 %shard_map.115 = f32[160,128]{1,0:T(8,128)S(1)} custom-call(s32[4,160]{1,0:T(4,128)S(1)} %copy-done.2, bf16[4096,160]{1,0:T(8,128)(2,1)S(1)} %bitcast.16, f32[64,160]{1,0:T(8,128)S(1)} %get-tuple-element.52.lowered_ref, bf16[2048,4096]{1,0:T(8,128)(2,1)} %bitcast.19), custom_call_target="tpu_custom_call" | custom-call | flops 2684354 | bytes 16777 | tf_op jit(solution)/shard_map/pallas_call | solution.py:322
  48.6 7.1 %shard_map.116 = bf16[160,1536]{1,0:T(8,128)(2,1)S(1)} custom-call(s32[1]{0:T(128)} %bitcast.owner_ref, bf16[4096,160]{1,0:T(8,128)(2,1)S(1)} %bitcast.17, bf16[6144,4096]{1,0:T(8,128)(2,1)} %refs_3_, bf16[160,1536]{1,0:T(8,128)(2,1)} %collective-permute-done.5.refs_0_), custom_call_target="tpu_custom_call" | custom-call | flops 2013265 | bytes 12582 | tf_op jit(solution)/shard_map/pallas_call | solution.py:348
  55.7 0.0 collective-permute-done.7.refs_1_
  55.7 0.0 collective-permute-done.8.refs_6_
  55.7 1.4 collective-permute-start.9
  57.1 2.5 %collective-permute-start.10 = (f32[160,128]{1,0:T(8,128)S(1)}, f32[160,128]{1,0:T(8,128)S(1)}, u32[]{:S(2)}, u32[]{:S(2)}) collective-permute-start(f32[160,128]{1,0:T(8,128)S(1)} %shard_map.115), channel_id=1, source_target_pairs={{0,1},{1,0},{2,3},{3,2},{4,5},{5,4},{6,7},{7,6},{8,9},{9,8},{10,11... | collective-permute-start | bytes 245768 | tf_op jit(solution)/shard_map/ppermute | solution.py:582
  59.6 0.1 collective-permute-start.11
  59.6 6.3 %collective-permute-done.4.second_ref = bf16[160,1536]{1,0:T(8,128)(2,1)} collective-permute-done((bf16[160,1536]{1,0:T(8,128)(2,1)}, bf16[160,1536]{1,0:T(8,128)(2,1)}, u32[]{:S(2)}, u32[]{:S(2)}) %collective-permute-start.4) | collective-permute-done | bytes 491552 | tf_op jit(solution)/shard_map/ppermute | solution.py:582
  65.9 3.6 %collective-permute-start.12 = (f32[160,128]{1,0:T(8,128)S(1)}, f32[160,128]{1,0:T(8,128)S(1)}, u32[]{:S(2)}, u32[]{:S(2)}) collective-permute-start(f32[160,128]{1,0:T(8,128)S(1)} %shard_map.115), channel_id=1, source_target_pairs={{0,3},{1,2},{2,1},{3,0},{4,7},{5,6},{6,5},{7,4},{8,11},{9,10},{10,... | collective-permute-start | bytes 245768 | tf_op jit(solution)/shard_map/ppermute | solution.py:582
  69.5 0.1 pad_add_fusion.1.owners_ref
  69.6 20.8 %shard_map.117 = (f32[160,4096]{1,0:T(8,128)S(1)}, bf16[160,1536]{1,0:T(8,128)(2,1)S(1)}) custom-call(s32[2]{0:T(128)S(1)} %pad_add_fusion.1.owners_ref, bf16[160,1536]{1,0:T(8,128)(2,1)} %get-tuple-element.78.first_ref.refs_4_, bf16[160,1536]{1,0:T(8,128)(2,1)} %collective-permute-done.4.second_ref, bf16[4096,160]{1,0:T(8,128)(2,1)S(1)} %bitcast.18, ...), custom_call_target="tpu_custom_call" | custom-call | flops 6039797 | bytes 25165 | tf_op jit(solution)/shard_map/pallas_call | solution.py:403
  90.4 0.0 collective-permute-done.3.refs_0_
  90.4 0.1 collective-permute-start.6
  90.5 1.1 collective-permute-done.9.refs_2_
  91.6 0.0 collective-permute-done.10
  91.6 1.7 %collective-permute-done.11 = f32[160,128]{1,0:T(8,128)S(1)} collective-permute-done((f32[160,128]{1,0:T(8,128)S(1)}, f32[160,128]{1,0:T(8,128)S(1)}, u32[]{:S(2)}, u32[]{:S(2)}) %collective-permute-start.11) | collective-permute-done | bytes 81952 | tf_op jit(solution)/shard_map/ppermute | solution.py:582
  93.3 0.0 collective-permute-done.12
  93.4 4.2 %shard_map.118.refs_0_ = bf16[160,1664]{1,0:T(8,128)(2,1)S(1)} custom-call(s32[4,160]{1,0:T(4,128)S(1)} %copy-done.2, bf16[160,128]{1,0:T(8,128)(2,1)S(1)} %multiply_convert_fusion.ranks_ref.refs_6_, bf16[2048,1536]{1,0:T(8,128)(2,1)} %bitcast.22, bf16[160,1536]{1,0:T(8,128)(2,1)S(1)} %get-tuple-element.63.refs_0_, ...), custom_call_target="tpu_custom_call" | custom-call | flops 1006632 | bytes 6291 | tf_op jit(solution)/shard_map/pallas_call | solution.py:499
  97.6 0.1 collective-permute-start.17
  97.7 0.5 collective-permute-start.16
  98.2 0.5 collective-permute-start.14
  98.7 0.0 collective-permute-start.13
  98.7 5.0 %collective-permute-done.6.refs_1_ = bf16[160,1536]{1,0:T(8,128)(2,1)S(1)} collective-permute-done((bf16[160,1536]{1,0:T(8,128)(2,1)S(1)}, bf16[160,1536]{1,0:T(8,128)(2,1)S(1)}, u32[]{:S(2)}, u32[]{:S(2)}) %collective-permute-start.6) | collective-permute-done | bytes 491552 | tf_op jit(solution)/shard_map/ppermute | solution.py:582
  103.7 0.5 collective-permute-start.19
  104.3 0.1 pad_add_fusion.owners_ref
  104.3 18.5 %shard_map.119 = bf16[160,4096]{1,0:T(8,128)(2,1)} custom-call(s32[2]{0:T(128)S(1)} %pad_add_fusion.owners_ref, bf16[160,1536]{1,0:T(8,128)(2,1)S(1)} %collective-permute-done.3.refs_0_, bf16[160,1536]{1,0:T(8,128)(2,1)S(1)} %collective-permute-done.6.refs_1_, bf16[6144,4096]{1,0:T(8,128)(2,1)} %refs_3_, bf16[6144,4096]{1,0:T(8,128)(2,1)} %refs_3_, ...), custom_call_target="tpu_custom_call" | custom-call | flops 6710886 | bytes 41943 | tf_op jit(solution)/shard_map/pallas_call | solution.py:464
  122.9 0.0 collective-permute-done.14.refs_2_
  122.9 0.0 collective-permute-start.15
  122.9 0.0 collective-permute-done.19.refs_6_
  122.9 0.5 collective-permute-start.20
  123.4 0.0 collective-permute-done.13.refs_1_
  123.4 0.1 collective-permute-start.18
  123.5 1.3 collective-permute-done.15.refs_3_
  124.8 0.0 collective-permute-done.17.refs_7_
  124.8 0.0 collective-permute-done.16.refs_5_
  124.8 1.0 copy-done.5
  125.9 0.0 copy-done.4
  125.9 7.6 %shard_map.120 = bf16[512,4096]{1,0:T(8,128)(2,1)} custom-call(s32[1]{0:T(128)} %bitcast.2.place_ref, s32[4,160]{1,0:T(4,128)S(1)} %copy-done.4, bf16[160,1664]{1,0:T(8,128)(2,1)S(1)} %shard_map.118.refs_0_, bf16[160,1664]{1,0:T(8,128)(2,1)S(1)} %collective-permute-done.13.refs_1_, bf16[160,1664]{1,0:T(8,128)(2,1)S(1)} %collective-permute-done.14.refs_2_, ...), custom_call_target="tpu_custom_call" | custom-call | flops 2684354 | bytes 9437 | tf_op jit(solution)/shard_map/pallas_call | solution.py:537
  133.5 0.0 collective-permute-done.20.refs_7_
  133.5 0.0 collective-permute-done.18.refs_5_
  133.5 4.5 %shard_map.121 = bf16[512,1536]{1,0:T(8,128)(2,1)} custom-call(s32[1]{0:T(128)} %bitcast.2.place_ref, s32[4,160]{1,0:T(4,128)S(1)} %copy-done.4, bf16[160,1664]{1,0:T(8,128)(2,1)S(1)} %shard_map.118.refs_0_, bf16[160,1664]{1,0:T(8,128)(2,1)S(1)} %collective-permute-done.13.refs_1_, bf16[160,1664]{1,0:T(8,128)(2,1)S(1)} %collective-permute-done.14.refs_2_, ...), custom_call_target="tpu_custom_call" | custom-call | flops 1006632 | bytes 3538 | tf_op jit(solution)/shard_map/pallas_call | solution.py:537
  138.1 2.7 %shard_map.122 = bf16[320,1536]{1,0:T(8,128)(2,1)} custom-call(s32[1]{0:T(128)} %bitcast.2.place_ref, s32[4,4]{1,0:T(4,128)S(1)} %copy-done.3, bf16[160,1664]{1,0:T(8,128)(2,1)S(1)} %shard_map.118.refs_0_, bf16[160,1664]{1,0:T(8,128)(2,1)S(1)} %collective-permute-done.13.refs_1_, bf16[160,1664]{1,0:T(8,128)(2,1)S(1)} %collective-permute-done.14.refs_2_, ...), custom_call_target="tpu_custom_call" | custom-call | flops 629145 | bytes 3932 | tf_op jit(solution)/shard_map/pallas_call | solution.py:569
  (7 shorter events, 0.0 us)
Async XLA Ops:
  3.5 14.1 %collective-permute-start = (bf16[80,1536]{1,0:T(8,128)(2,1)}, bf16[80,1536]{1,0:T(8,128)(2,1)}, u32[]{:S(2)}, u32[]{:S(2)}) collective-permute-start(bf16[80,1536]{1,0:T(8,128)(2,1)} %get-tuple-element.45), channel_id=1, source_target_pairs={{0,4},{4,0},{8,12},{12,8},{1,5},{5,1},{9,13},{13,9},{2,6},{6,2},{1... | collective-permute-start | bytes 737288 | tf_op jit(solution)/shard_map/ppermute | solution.py:582
  3.9 13.6 %collective-permute-start.1 = (bf16[80,1536]{1,0:T(8,128)(2,1)}, bf16[80,1536]{1,0:T(8,128)(2,1)}, u32[]{:S(2)}, u32[]{:S(2)}) collective-permute-start(bf16[80,1536]{1,0:T(8,128)(2,1)} %get-tuple-element.46), channel_id=1, source_target_pairs={{0,8},{4,12},{8,0},{12,4},{1,9},{5,13},{9,1},{13,5},{2,10},{6,14},... | collective-permute-start | bytes 737288 | tf_op jit(solution)/shard_map/ppermute | solution.py:582
  6.4 11.9 %collective-permute-start.2 = (bf16[80,1536]{1,0:T(8,128)(2,1)}, bf16[80,1536]{1,0:T(8,128)(2,1)}, u32[]{:S(2)}, u32[]{:S(2)}) collective-permute-start(bf16[80,1536]{1,0:T(8,128)(2,1)} %get-tuple-element.47), channel_id=1, source_target_pairs={{0,12},{4,8},{8,4},{12,0},{1,13},{5,9},{9,5},{13,1},{2,14},{6,10},... | collective-permute-start | bytes 737288 | tf_op jit(solution)/shard_map/ppermute | solution.py:582
  9.6 8.7 %copy-start = (bf16[160,4096]{1,0:T(8,128)(2,1)S(1)}, bf16[160,4096]{1,0:T(8,128)(2,1)}, u32[]{:S(2)}) copy-start(bf16[160,4096]{1,0:T(8,128)(2,1)} %refs_4_.1) | copy-start | bytes 3932164
  18.4 37.3 %collective-permute-start.8 = (bf16[160,4096]{1,0:T(8,128)(2,1)S(1)}, bf16[160,4096]{1,0:T(8,128)(2,1)}, u32[]{:S(2)}, u32[]{:S(2)}) collective-permute-start(bf16[160,4096]{1,0:T(8,128)(2,1)S(1)} %copy-done), channel_id=1, source_target_pairs={{0,8},{4,12},{8,0},{12,4},{1,9},{5,13},{9,1},{13,5},{2,10},{6,14},... | collective-permute-start | bytes 3932168 | tf_op jit(solution)/shard_map/ppermute | solution.py:582
  19.9 20.2 %collective-permute-start.5 = (bf16[160,1536]{1,0:T(8,128)(2,1)}, bf16[160,1536]{1,0:T(8,128)(2,1)}, u32[]{:S(2)}, u32[]{:S(2)}) collective-permute-start(bf16[160,1536]{1,0:T(8,128)(2,1)} %shard_map.112), channel_id=1, source_target_pairs={{0,1},{1,0},{2,3},{3,2},{4,5},{5,4},{6,7},{7,6},{8,9},{9,8},{10,11... | collective-permute-start | bytes 1474568 | tf_op jit(solution)/shard_map/ppermute | solution.py:582
  21.5 8.3 %copy-start.1 = (bf16[320,1536]{1,0:T(8,128)(2,1)S(1)}, bf16[320,1536]{1,0:T(8,128)(2,1)}, u32[]{:S(2)}) copy-start(bf16[320,1536]{1,0:T(8,128)(2,1)} %rows_ref.3) | copy-start | bytes 2949124
  21.5 8.3 %copy-start.2 = (s32[4,160]{1,0:T(4,128)S(1)}, s32[4,160]{1,0:T(4,128)}, u32[]{:S(2)}) copy-start(s32[4,160]{1,0:T(4,128)} %get-tuple-element.44.tenant_ref.refs_5_) | copy-start | bytes 7684
  21.5 8.3 %copy-start.3 = (s32[4,4]{1,0:T(4,128)S(1)}, s32[4,4]{1,0:T(4,128)}, u32[]{:S(2)}) copy-start(s32[4,4]{1,0:T(4,128)} %handoff_ref.5) | copy-start | bytes 196
  29.4 26.3 %collective-permute-start.7 = (bf16[160,1536]{1,0:T(8,128)(2,1)}, bf16[160,1536]{1,0:T(8,128)(2,1)}, u32[]{:S(2)}, u32[]{:S(2)}) collective-permute-start(bf16[160,1536]{1,0:T(8,128)(2,1)} %shard_map.113), channel_id=1, source_target_pairs={{0,1},{1,0},{2,3},{3,2},{4,5},{5,4},{6,7},{7,6},{8,9},{9,8},{10,11... | collective-permute-start | bytes 1474568 | tf_op jit(solution)/shard_map/ppermute | solution.py:582
  35.9 30.0 %collective-permute-start.4 = (bf16[160,1536]{1,0:T(8,128)(2,1)}, bf16[160,1536]{1,0:T(8,128)(2,1)}, u32[]{:S(2)}, u32[]{:S(2)}) collective-permute-start(bf16[160,1536]{1,0:T(8,128)(2,1)} %get-tuple-element.78.first_ref.refs_4_), channel_id=1, source_target_pairs={{0,1},{1,0},{2,3},{3,2},{4,5},{5,4},{6,7},{7,6},{8,9},{9,8},{10,11... | collective-permute-start | bytes 1474568 | tf_op jit(solution)/shard_map/ppermute | solution.py:582
  37.5 52.9 %collective-permute-start.3 = (bf16[160,1536]{1,0:T(8,128)(2,1)}, bf16[160,1536]{1,0:T(8,128)(2,1)S(1)}, u32[]{:S(2)}, u32[]{:S(2)}) collective-permute-start(bf16[160,1536]{1,0:T(8,128)(2,1)} %get-tuple-element.78.first_ref.refs_4_), channel_id=1, source_target_pairs={{0,2},{1,3},{2,0},{3,1},{4,6},{5,7},{6,4},{7,5},{8,10},{9,11},{10,... | collective-permute-start | bytes 1474568 | tf_op jit(solution)/shard_map/ppermute | solution.py:582
  55.7 35.9 %collective-permute-start.9 = (bf16[160,1536]{1,0:T(8,128)(2,1)S(1)}, bf16[160,1536]{1,0:T(8,128)(2,1)S(1)}, u32[]{:S(2)}, u32[]{:S(2)}) collective-permute-start(bf16[160,1536]{1,0:T(8,128)(2,1)S(1)} %shard_map.116), channel_id=1, source_target_pairs={{0,2},{1,3},{2,0},{3,1},{4,6},{5,7},{6,4},{7,5},{8,10},{9,11},{10,... | collective-permute-start | bytes 1474568 | tf_op jit(solution)/shard_map/ppermute | solution.py:582
  57.1 34.5 %collective-permute-start.10 = (f32[160,128]{1,0:T(8,128)S(1)}, f32[160,128]{1,0:T(8,128)S(1)}, u32[]{:S(2)}, u32[]{:S(2)}) collective-permute-start(f32[160,128]{1,0:T(8,128)S(1)} %shard_map.115), channel_id=1, source_target_pairs={{0,1},{1,0},{2,3},{3,2},{4,5},{5,4},{6,7},{7,6},{8,9},{9,8},{10,11... | collective-permute-start | bytes 245768 | tf_op jit(solution)/shard_map/ppermute | solution.py:582
  59.6 33.8 %collective-permute-start.11 = (f32[160,128]{1,0:T(8,128)S(1)}, f32[160,128]{1,0:T(8,128)S(1)}, u32[]{:S(2)}, u32[]{:S(2)}) collective-permute-start(f32[160,128]{1,0:T(8,128)S(1)} %shard_map.115), channel_id=1, source_target_pairs={{0,2},{1,3},{2,0},{3,1},{4,6},{5,7},{6,4},{7,5},{8,10},{9,11},{10,... | collective-permute-start | bytes 245768 | tf_op jit(solution)/shard_map/ppermute | solution.py:582
  65.9 27.4 %collective-permute-start.12 = (f32[160,128]{1,0:T(8,128)S(1)}, f32[160,128]{1,0:T(8,128)S(1)}, u32[]{:S(2)}, u32[]{:S(2)}) collective-permute-start(f32[160,128]{1,0:T(8,128)S(1)} %shard_map.115), channel_id=1, source_target_pairs={{0,3},{1,2},{2,1},{3,0},{4,7},{5,6},{6,5},{7,4},{8,11},{9,10},{10,... | collective-permute-start | bytes 245768 | tf_op jit(solution)/shard_map/ppermute | solution.py:582
  90.4 13.3 %collective-permute-start.6 = (bf16[160,1536]{1,0:T(8,128)(2,1)S(1)}, bf16[160,1536]{1,0:T(8,128)(2,1)S(1)}, u32[]{:S(2)}, u32[]{:S(2)}) collective-permute-start(bf16[160,1536]{1,0:T(8,128)(2,1)S(1)} %collective-permute-done.3.refs_0_), channel_id=1, source_target_pairs={{0,1},{1,0},{2,3},{3,2},{4,5},{5,4},{6,7},{7,6},{8,9},{9,8},{10,11... | collective-permute-start | bytes 1474568 | tf_op jit(solution)/shard_map/ppermute | solution.py:582
  97.6 27.2 %collective-permute-start.17 = (bf16[160,4096]{1,0:T(8,128)(2,1)}, bf16[160,4096]{1,0:T(8,128)(2,1)S(1)}, u32[]{:S(2)}, u32[]{:S(2)}) collective-permute-start(bf16[160,4096]{1,0:T(8,128)(2,1)} %collective-permute-done.8.refs_6_), channel_id=1, source_target_pairs={{0,4},{4,0},{8,12},{12,8},{1,5},{5,1},{9,13},{13,9},{2,6},{6,2},{1... | collective-permute-start | bytes 3932168 | tf_op jit(solution)/shard_map/ppermute | solution.py:582
  97.7 27.1 %collective-permute-start.16 = (bf16[160,4096]{1,0:T(8,128)(2,1)S(1)}, bf16[160,4096]{1,0:T(8,128)(2,1)S(1)}, u32[]{:S(2)}, u32[]{:S(2)}) collective-permute-start(bf16[160,4096]{1,0:T(8,128)(2,1)S(1)} %copy-done), channel_id=1, source_target_pairs={{0,4},{4,0},{8,12},{12,8},{1,5},{5,1},{9,13},{13,9},{2,6},{6,2},{1... | collective-permute-start | bytes 3932168 | tf_op jit(solution)/shard_map/ppermute | solution.py:582
  98.2 24.7 %collective-permute-start.14 = (bf16[160,1664]{1,0:T(8,128)(2,1)S(1)}, bf16[160,1664]{1,0:T(8,128)(2,1)S(1)}, u32[]{:S(2)}, u32[]{:S(2)}) collective-permute-start(bf16[160,1664]{1,0:T(8,128)(2,1)S(1)} %shard_map.118.refs_0_), channel_id=1, source_target_pairs={{0,8},{4,12},{8,0},{12,4},{1,9},{5,13},{9,1},{13,5},{2,10},{6,14},... | collective-permute-start | bytes 1597448 | tf_op jit(solution)/shard_map/ppermute | solution.py:582
  98.7 24.7 %collective-permute-start.13 = (bf16[160,1664]{1,0:T(8,128)(2,1)S(1)}, bf16[160,1664]{1,0:T(8,128)(2,1)S(1)}, u32[]{:S(2)}, u32[]{:S(2)}) collective-permute-start(bf16[160,1664]{1,0:T(8,128)(2,1)S(1)} %shard_map.118.refs_0_), channel_id=1, source_target_pairs={{0,4},{4,0},{8,12},{12,8},{1,5},{5,1},{9,13},{13,9},{2,6},{6,2},{1... | collective-permute-start | bytes 1597448 | tf_op jit(solution)/shard_map/ppermute | solution.py:582
  103.7 19.2 %collective-permute-start.19 = (bf16[160,1536]{1,0:T(8,128)(2,1)}, bf16[160,1536]{1,0:T(8,128)(2,1)S(1)}, u32[]{:S(2)}, u32[]{:S(2)}) collective-permute-start(bf16[160,1536]{1,0:T(8,128)(2,1)} %get-tuple-element.78.first_ref.refs_4_), channel_id=1, source_target_pairs={{0,8},{4,12},{8,0},{12,4},{1,9},{5,13},{9,1},{13,5},{2,10},{6,14},... | collective-permute-start | bytes 1474568 | tf_op jit(solution)/shard_map/ppermute | solution.py:582
  104.3 21.5 %copy-start.4 = (s32[4,160]{1,0:T(4,128)S(1)}, s32[4,160]{1,0:T(4,128)}, u32[]{:S(2)}) copy-start(s32[4,160]{1,0:T(4,128)} %get-tuple-element.66.slot_ref) | copy-start | bytes 7684
  122.9 1.9 %collective-permute-start.15 = (bf16[160,1664]{1,0:T(8,128)(2,1)S(1)}, bf16[160,1664]{1,0:T(8,128)(2,1)S(1)}, u32[]{:S(2)}, u32[]{:S(2)}) collective-permute-start(bf16[160,1664]{1,0:T(8,128)(2,1)S(1)} %collective-permute-done.14.refs_2_), channel_id=1, source_target_pairs={{0,4},{4,0},{8,12},{12,8},{1,5},{5,1},{9,13},{13,9},{2,6},{6,2},{1... | collective-permute-start | bytes 1597448 | tf_op jit(solution)/shard_map/ppermute | solution.py:582
  122.9 10.6 %collective-permute-start.20 = (bf16[160,1536]{1,0:T(8,128)(2,1)S(1)}, bf16[160,1536]{1,0:T(8,128)(2,1)S(1)}, u32[]{:S(2)}, u32[]{:S(2)}) collective-permute-start(bf16[160,1536]{1,0:T(8,128)(2,1)S(1)} %collective-permute-done.19.refs_6_), channel_id=1, source_target_pairs={{0,4},{4,0},{8,12},{12,8},{1,5},{5,1},{9,13},{13,9},{2,6},{6,2},{1... | collective-permute-start | bytes 1474568 | tf_op jit(solution)/shard_map/ppermute | solution.py:582
  123.4 10.1 %collective-permute-start.18 = (bf16[160,1536]{1,0:T(8,128)(2,1)}, bf16[160,1536]{1,0:T(8,128)(2,1)S(1)}, u32[]{:S(2)}, u32[]{:S(2)}) collective-permute-start(bf16[160,1536]{1,0:T(8,128)(2,1)} %get-tuple-element.78.first_ref.refs_4_), channel_id=1, source_target_pairs={{0,4},{4,0},{8,12},{12,8},{1,5},{5,1},{9,13},{13,9},{2,6},{6,2},{1... | collective-permute-start | bytes 1474568 | tf_op jit(solution)/shard_map/ppermute | solution.py:582
  124.8 1.1 copy-start.5

commit v3 on v2

--- a/solution.py
+++ b/solution.py
@@ -11,7 +11,7 @@
 BF = jnp.bfloat16
 F32 = jnp.float32
 I32 = jnp.int32
-VMEM_LIMIT = 48 * 2**20
+VMEM_LIMIT = 32 * 2**20
 
 
 def before_sums(values, group_axis):
@@ -329,7 +329,7 @@
         out_specs=whole((balanced, 2 * rank)),
         out_shape=jax.ShapeDtypeStruct((balanced, 2 * rank), F32),
         scratch_shapes=[pltpu.VMEM((2 * rank, balanced), F32)],
-        compiler_params=params(),
+        compiler_params=params(50 * 2**20),
         cost_estimate=cost(2 * balanced * up.size, 2 * up.size),
     )(tenant, turned, lowered, up)
 
@@ -363,6 +363,37 @@
     )(owner, turned, weight, *(() if arrived is None else (arrived,)))
 
 
+def turn_and_far(owner, cotangent, weight, width, block):
+    balanced, hidden = cotangent.shape
+    steps = width // block
+
+    def kernel(owner_ref, cotangent_ref, weight_ref, far_ref, turned_ref):
+        @pl.when(pl.program_id(0) == 0)
+        def _():
+            turned_ref[...] = cotangent_ref[...].astype(F32).T.astype(BF)
+
+        far_ref[...] = jnp.dot(weight_ref[...], turned_ref[...], preferred_element_type=F32).T.astype(BF)
+
+    return pl.pallas_call(
+        kernel,
+        grid_spec=pltpu.PrefetchScalarGridSpec(
+            num_scalar_prefetch=1,
+            grid=(steps,),
+            in_specs=[
+                whole(cotangent.shape),
+                pl.BlockSpec((block, hidden), lambda i, o: (o[0] * steps + i, 0)),
+            ],
+            out_specs=[pl.BlockSpec((balanced, block), lambda i, o: (0, i)), whole((hidden, balanced))],
+        ),
+        out_shape=[
+            jax.ShapeDtypeStruct((balanced, width), BF),
+            jax.ShapeDtypeStruct((hidden, balanced), BF),
+        ],
+        compiler_params=params(),
+        cost_estimate=cost(2 * balanced * width * hidden, 2 * width * hidden),
+    )(owner, cotangent, weight)
+
+
 def spread(wide_ref, tenant_ref, ranks_ref, second, scale, tenants, rank):
     balanced, lanes = ranks_ref.shape
     vectors = scale * ranks_ref[...].astype(F32)
@@ -375,53 +406,43 @@
         wide_ref[:, pair * lanes : (pair + 1) * lanes] = jnp.where(label == 2.0 * pair, twice, 0.0).astype(BF)
 
 
-def own_and_forward(owners, parts, turned, weight, block):
-    balanced, width = parts[0].shape
+def own_and_forward(owner, part, turned, weight, block):
+    balanced, width = part.shape
     hidden = weight.shape[1]
-    steps = hidden // block
-
-    def kernel(owners_ref, first_ref, second_ref, turned_ref, mine_ref, other_ref, total_ref, own_ref, sum_ref):
-        step = pl.program_id(0)
-        piece = jnp.dot(mine_ref[...], turned_ref[...], preferred_element_type=F32)
-
-        @pl.when(step == 0)
+    steps = width // block
+
+    def kernel(owner_ref, part_ref, turned_ref, weight_ref, total_ref, own_ref):
+        own_ref[...] = jnp.dot(weight_ref[...], turned_ref[...], preferred_element_type=F32).T.astype(BF)
+        piece = jnp.dot(part_ref[...], weight_ref[...], preferred_element_type=F32)
+
+        @pl.when(pl.program_id(0) == 0)
         def _():
-            sum_ref[...] = piece
-
-        @pl.when(step > 0)
+            total_ref[...] = piece
+
+        @pl.when(pl.program_id(0) > 0)
         def _():
-            sum_ref[...] += piece
-
-        total_ref[...] = jnp.dot(
-            first_ref[...], mine_ref[...], preferred_element_type=F32
-        ) + jnp.dot(second_ref[...], other_ref[...], preferred_element_type=F32)
-
-        @pl.when(step == steps - 1)
-        def _():
-            own_ref[...] = sum_ref[...].T.astype(BF)
-
+            total_ref[...] += piece
+
+    columns = pl.BlockSpec((balanced, block), lambda i, o: (0, i))
     return pl.pallas_call(
         kernel,
         grid_spec=pltpu.PrefetchScalarGridSpec(
             num_scalar_prefetch=1,
             grid=(steps,),
             in_specs=[
-                whole((balanced, width)),
-                whole((balanced, width)),
-                pl.BlockSpec((block, balanced), lambda n, o: (n, 0)),
-                pl.BlockSpec((width, block), lambda n, o: (o[0], n)),
-                pl.BlockSpec((width, block), lambda n, o: (o[1], n)),
+                columns,
+                whole(turned.shape),
+                pl.BlockSpec((block, hidden), lambda i, o: (o[0] * steps + i, 0)),
             ],
-            out_specs=[pl.BlockSpec((balanced, block), lambda n, o: (0, n)), whole((balanced, width))],
-            scratch_shapes=[pltpu.VMEM((width, balanced), F32)],
+            out_specs=[whole((balanced, hidden)), columns],
         ),
         out_shape=[
             jax.ShapeDtypeStruct((balanced, hidden), F32),
             jax.ShapeDtypeStruct((balanced, width), BF),
         ],
         compiler_params=params(),
-        cost_estimate=cost(6 * balanced * width * hidden, 4 * width * hidden),
-    )(owners, *parts, turned, weight, weight)
+        cost_estimate=cost(4 * balanced * width * hidden, 2 * width * hidden),
+    )(owner, part, turned, weight)
 
 
 def forward(owners, parts, weight, block, total=None, tenant=None, ranks=None, up=None):
@@ -471,7 +492,7 @@
             scratch_shapes=[pltpu.VMEM((balanced, up.shape[0]), BF)] if last else [],
         ),
         out_shape=jax.ShapeDtypeStruct((balanced, hidden), BF if last else F32),
-        compiler_params=params(),
+        compiler_params=params(50 * 2**20 if last else VMEM_LIMIT),
         cost_estimate=cost(
             2 * balanced * hidden * (count * width + (up.shape[0] if last else 0)),
             2 * hidden * (count * width + (up.shape[0] if last else 0)),
@@ -606,7 +627,6 @@
     owner = [(z ^ k).astype(I32) for k in range(4)]
     down = adapter_down_weight.transpose(0, 2, 1).reshape(tenants * rank, width)
     up = adapter_up_weight.reshape(tenants * rank, hidden)
-    turned = cotangent.T
 
     *outgoing, tenant, slot = pack(
         place, handoff_counts, tenant_row_counts, tenant_gradient_slot, input_rows, balanced, balanced // 2
@@ -614,7 +634,9 @@
     arrived = [None] * 3
     for k in (2, 3, 1):
         arrived[k - 1] = swap(outgoing[k - 1], "dp", k)
-    far = base_gradient(owner[3].reshape(1), after(turned, *outgoing), frozen_weight, width, 512)
+    far, turned = turn_and_far(
+        owner[3].reshape(1), cotangent, after(frozen_weight, tenant), width, 512
+    )
     for_far = swap(far, "fsdp", 1)
     near = base_gradient(owner[1].reshape(1), turned, after(frozen_weight, far), width, 512)
     from_near = swap(near, "fsdp", 1)
@@ -625,20 +647,23 @@
     pair = swap(gathered, "fsdp", 2)
     cot_x = swap(after(cotangent, *arrived, far), "dp", 2)
     partial = rank_backward(tenant, turned, after(up, gathered, for_far), lowered, 512)
+    first, own = own_and_forward(
+        owner[0].reshape(1), gathered, turned, after(frozen_weight, partial), 512
+    )
+    late = after(partial, first, cot_x)
+    sums = [swap(late, "fsdp", k) for k in (1, 2, 3)]
     across = base_gradient(
-        owner[2].reshape(1), turned, after(frozen_weight, partial), width, 512, for_far
-    )
-    late = after(partial, across, cot_x, from_near)
-    sums = [swap(late, "fsdp", k) for k in (1, 2, 3)]
-    from_pair = swap(after(across, from_near, cot_x), "fsdp", 2)
-    total, own = own_and_forward(
-        jnp.stack([owner[0], owner[1]]), [gathered, beside], turned, after(frozen_weight, across), 512
-    )
-    diagonal = swap(after(pair, total), "fsdp", 1)
-    gathered_x = swap(after(gathered, total), "dp", 2)
+        owner[2].reshape(1), turned, after(frozen_weight, first, from_near), width, 512, for_far
+    )
+    from_pair = swap(across, "fsdp", 2)
+    diagonal = swap(after(pair, across), "fsdp", 1)
+    gathered_x = swap(after(gathered, across, cot_x), "dp", 2)
+    second = forward(
+        jnp.stack([owner[1], owner[2]]), [beside, pair], after(frozen_weight, across), 512, first
+    )
     scale = jnp.where(jnp.arange(2 * rank) < rank, 1.0, adapter_scale).astype(F32)
-    ranks = ((after(partial, total, from_pair) + sums[0] + (sums[1] + sums[2])) * scale).astype(BF)
-    bundle = finish_gradient([own, from_near, from_pair], tenant, ranks, after(down, total), 512)
+    ranks = ((after(partial, second, from_pair) + sums[0] + (sums[1] + sums[2])) * scale).astype(BF)
+    bundle = finish_gradient([own, from_near, from_pair], tenant, ranks, after(down, second, diagonal), 512)
     bundle_x = swap(bundle, "dp", 2)
     bundle_c = swap(bundle, "dp", 1)
     cot_all = [
@@ -648,29 +673,22 @@
         swap(after(cot_x, bundle), "dp", 1),
     ]
     outputs = forward(
-        jnp.stack([owner[2], owner[3]]),
-        [pair, diagonal],
-        after(frozen_weight, bundle, diagonal),
-        512,
-        total,
-        tenant,
-        ranks,
-        up,
+        owner[3].reshape(1), [diagonal], after(frozen_weight, bundle), 512, second, tenant, ranks, up
     )
     bundles = [bundle, bundle_c, bundle_x, swap(after(bundle_x, outputs), "dp", 1)]
+    grad_b = owned_gradient(
+        place, slot, after(bundles, outputs), False, cot_all, share, 2 * rank, adapter_scale, 1024
+    )
+    row_grad = bring_home(place, handoff_counts, after(bundles, grad_b), capacity, width)
     gathered_all = [
         gathered,
         swap(after(gathered, outputs), "dp", 1),
         gathered_x,
-        swap(after(gathered_x, outputs), "dp", 1),
+        swap(after(gathered_x, row_grad), "dp", 1),
     ]
-    grad_b = owned_gradient(
-        place, slot, after(bundles, outputs), False, cot_all, share, 2 * rank, adapter_scale, 1024
-    )
     grad_a = owned_gradient(
-        place, slot, after(bundles, grad_b), True, gathered_all, share, 2 * rank, 1.0, 512
-    )
-    row_grad = bring_home(place, handoff_counts, after(bundles, grad_a), capacity, width)
+        place, slot, after(bundles, row_grad), True, gathered_all, share, 2 * rank, 1.0, 512
+    )
     return (
         outputs,
         row_grad,

time: 141 us -> 131 us (0.929)
  Pallas kernels: 98.7 us -> 92.9 us
  local copies, waits for them, and re-layouts: 4.16 us -> 1.93 us
    pallas_call x1, Pallas kernels: 20.8 us -> 9.21 us  [own_and_forward(): pl.pallas_call(kernel, grid_spec=pltpu.PrefetchScalarGridSpec(num_scalar_...]
    pallas_call x1 -> x2, Pallas kernels: 18.5 us -> 28.1 us  [forward(): pl.pallas_call(kernel, grid_spec=pltpu.PrefetchScalarGridSpec(num_scalar_...]
    pallas_call x0 -> x1, Pallas kernels: none -> 8.77 us  [turn_and_far(): pl.pallas_call(kernel, grid_spec=pltpu.PrefetchScalarGridSpec(num_scalar_...]
    pallas_call x3 -> x2, Pallas kernels: 22.8 us -> 15.1 us  [base_gradient(): pl.pallas_call(kernel, grid_spec=pltpu.PrefetchScalarGridSpec(num_scalar_...]
    unnamed x13 -> x24, local copies, waits for them, and re-layouts: 4.16 us -> 1.93 us
    pallas_call x1, Pallas kernels: 6.08 us -> 3.9 us  [unpack(): pl.pallas_call(kernel, grid=(down.shape[0] // block,), in_specs=[SMEM(),...]
    pallas_call x1, Pallas kernels: 4.23 us -> 2.53 us  [finish_gradient(): pl.pallas_call(kernel, grid=(1,), in_specs=[whole(tenant.shape), whole(ra...]
  transfers between devices with their start and end apart: 21 -> 21, of which waited for: 6 -> 7; matrix products, arithmetic and copies ran while one was open for 2% -> 0% of each run, Pallas kernels for 63% -> 64%
where the time goes in v3:
time: 131 us
  Pallas kernels  92.9 us (71%)
  starting transfers between devices  19.3 us (15%)
  waiting for transfers between devices  16 us (12%)
  local copies, waits for them, and re-layouts  1.93 us (1%)
    pallas_call x2, Pallas kernels, forward(): pl.pallas_call(kernel, grid_spec=pltpu.PrefetchScalarGridSpec(num_scalar_...  28.1 us
    ppermute x21, starting transfers between devices, swap(): return lax.ppermute(values, axis, [(i, i ^ distance) for i in range(size)])  19.3 us
    ppermute x21, waiting for transfers between devices, swap(): return lax.ppermute(values, axis, [(i, i ^ distance) for i in range(size)])  16 us
    pallas_call x2, Pallas kernels, base_gradient(): pl.pallas_call(kernel, grid_spec=pltpu.PrefetchScalarGridSpec(num_scalar_...  15.1 us
    pallas_call x2, Pallas kernels, owned_gradient(): pl.pallas_call(kernel, grid=(width // block,), in_specs=[SMEM(), whole(sl...  11.2 us
    pallas_call x1, Pallas kernels, own_and_forward(): pl.pallas_call(kernel, grid_spec=pltpu.PrefetchScalarGridSpec(num_scalar_...  9.21 us
    pallas_call x1, Pallas kernels, turn_and_far(): pl.pallas_call(kernel, grid_spec=pltpu.PrefetchScalarGridSpec(num_scalar_...  8.77 us
    pallas_call x1, Pallas kernels, rank_backward(): pl.pallas_call(kernel, grid=(steps,), in_specs=[whole(tenant.shape), whol...  8.51 us
  transfers between devices with their start and end apart: 21, of which 7 were waited for; matrix products, arithmetic and copies ran while one was open for 0% of the time, Pallas kernels for 64%

profile of v3, /device:TPU:0, one launch (start us, length us, event | category | flops | bytes accessed | tf_op | source)
XLA Modules:
  0.0 131.0 jit_solution(8667252642008931414)
XLA Ops:
  0.6 2.8 %shard_map.111 = (bf16[80,1536]{1,0:T(8,128)(2,1)}, bf16[80,1536]{1,0:T(8,128)(2,1)}, bf16[80,1536]{1,0:T(8,128)(2,1)}, s32[4,160]{1,0:T(4,128)}, s32[4,160]{1,0:T(4,128)}) custom-call(s32[1]{0:T(128)} %bitcast.1.place_ref, s32[4,4]{1,0:T(4,128)} %handoff_ref.5, s32[32]{0:T(128)} %slots_ref.1, s32[4,32]{1,0:T(4,128)} %counts_ref.1, bf16[320,1536]{1,0:T(8,128)(2,1)} %rows_ref.3), custom_call_target="tpu_custom_call" | custom-call | flops 235929 | bytes 1966 | tf_op jit(solution)/shard_map/pallas_call | solution.py:232
  3.5 0.5 collective-permute-start
  3.9 2.5 %collective-permute-start.1 = (bf16[80,1536]{1,0:T(8,128)(2,1)}, bf16[80,1536]{1,0:T(8,128)(2,1)S(1)}, u32[]{:S(2)}, u32[]{:S(2)}) collective-permute-start(bf16[80,1536]{1,0:T(8,128)(2,1)} %get-tuple-element.48), channel_id=1, source_target_pairs={{0,8},{4,12},{8,0},{12,4},{1,9},{5,13},{9,1},{13,5},{2,10},{6,14},... | collective-permute-start | bytes 737288 | tf_op jit(solution)/shard_map/ppermute | solution.py:603
  6.4 0.1 collective-permute-start.2
  6.5 8.8 %shard_map.112 = (bf16[160,1536]{1,0:T(8,128)(2,1)}, bf16[4096,160]{1,0:T(8,128)(2,1)S(1)}) custom-call(s32[1]{0:T(128)} %bitcast.owner_ref.owners_ref, bf16[160,4096]{1,0:T(8,128)(2,1)} %refs_4_.1, bf16[6144,4096]{1,0:T(8,128)(2,1)} %refs_1_), custom_call_target="tpu_custom_call" | custom-call | flops 2013265 | bytes 12582 | tf_op jit(solution)/shard_map/pallas_call | solution.py:377
  15.3 0.0 collective-permute-done.refs_0_
  15.3 0.0 collective-permute-done.1.refs_1_
  15.3 0.0 copy-start.1
  15.3 2.9 %collective-permute-done.2.refs_2_ = bf16[80,1536]{1,0:T(8,128)(2,1)S(1)} collective-permute-done((bf16[80,1536]{1,0:T(8,128)(2,1)}, bf16[80,1536]{1,0:T(8,128)(2,1)S(1)}, u32[]{:S(2)}, u32[]{:S(2)}) %collective-permute-start.2) | collective-permute-done | bytes 245792 | tf_op jit(solution)/shard_map/ppermute | solution.py:603
  18.3 1.5 %collective-permute-start.9 = (bf16[160,4096]{1,0:T(8,128)(2,1)}, bf16[160,4096]{1,0:T(8,128)(2,1)}, u32[]{:S(2)}, u32[]{:S(2)}) collective-permute-start(bf16[160,4096]{1,0:T(8,128)(2,1)} %refs_4_.1), channel_id=1, source_target_pairs={{0,8},{4,12},{8,0},{12,4},{1,9},{5,13},{9,1},{13,5},{2,10},{6,14},... | collective-permute-start | bytes 3932168 | tf_op jit(solution)/shard_map/ppermute | solution.py:603
  19.8 1.6 %collective-permute-start.4 = (bf16[160,1536]{1,0:T(8,128)(2,1)}, bf16[160,1536]{1,0:T(8,128)(2,1)}, u32[]{:S(2)}, u32[]{:S(2)}) collective-permute-start(bf16[160,1536]{1,0:T(8,128)(2,1)} %get-tuple-element.52), channel_id=1, source_target_pairs={{0,1},{1,0},{2,3},{3,2},{4,5},{5,4},{6,7},{7,6},{8,9},{9,8},{10,11... | collective-permute-start | bytes 1474568 | tf_op jit(solution)/shard_map/ppermute | solution.py:603
  21.4 0.0 copy-start.6
  21.4 8.0 %shard_map.113 = bf16[160,1536]{1,0:T(8,128)(2,1)S(1)} custom-call(s32[1]{0:T(128)} %bitcast.4.owner_ref, bf16[4096,160]{1,0:T(8,128)(2,1)S(1)} %get-tuple-element.51.turned_ref, bf16[6144,4096]{1,0:T(8,128)(2,1)} %refs_1_), custom_call_target="tpu_custom_call" | custom-call | flops 2013265 | bytes 12582 | tf_op jit(solution)/shard_map/pallas_call | solution.py:348
  29.5 0.0 copy-done.1
  29.5 0.0 copy-done.3
  29.5 0.5 collective-permute-start.5
  30.0 0.0 slice-done.1
  30.0 0.0 copy-start.2
  30.0 0.9 copy-done.2
  31.0 0.9 copy-done.4
  31.9 3.9 %shard_map.114 = (bf16[160,1536]{1,0:T(8,128)(2,1)S(1)}, f32[64,160]{1,0:T(8,128)S(1)}) custom-call(s32[1]{0:T(128)} %bitcast.1.place_ref, s32[4,4]{1,0:T(4,128)S(1)} %copy-done.6, s32[4,160]{1,0:T(4,128)S(1)} %copy-done.5, bf16[320,1536]{1,0:T(8,128)(2,1)S(1)} %copy-done, bf16[80,1536]{1,0:T(8,128)(2,1)S(1)} %collective-permute-done.refs_0_, ...), custom_call_target="tpu_custom_call" | custom-call | flops 1006632 | bytes 7766 | tf_op jit(solution)/shard_map/pallas_call | solution.py:285
  35.8 2.6 %collective-permute-start.3 = (bf16[160,1536]{1,0:T(8,128)(2,1)S(1)}, bf16[160,1536]{1,0:T(8,128)(2,1)}, u32[]{:S(2)}, u32[]{:S(2)}) collective-permute-start(bf16[160,1536]{1,0:T(8,128)(2,1)S(1)} %get-tuple-element.86.part_ref.refs_4_), channel_id=1, source_target_pairs={{0,2},{1,3},{2,0},{3,1},{4,6},{5,7},{6,4},{7,5},{8,10},{9,11},{10,... | collective-permute-start | bytes 1474568 | tf_op jit(solution)/shard_map/ppermute | solution.py:603
  38.5 1.6 %collective-permute-start.7 = (bf16[160,1536]{1,0:T(8,128)(2,1)S(1)}, bf16[160,1536]{1,0:T(8,128)(2,1)}, u32[]{:S(2)}, u32[]{:S(2)}) collective-permute-start(bf16[160,1536]{1,0:T(8,128)(2,1)S(1)} %get-tuple-element.86.part_ref.refs_4_), channel_id=1, source_target_pairs={{0,1},{1,0},{2,3},{3,2},{4,5},{5,4},{6,7},{7,6},{8,9},{9,8},{10,11... | collective-permute-start | bytes 1474568 | tf_op jit(solution)/shard_map/ppermute | solution.py:603
  40.0 0.0 collective-permute-done.4.refs_0_
  40.0 8.5 %shard_map.115 = f32[160,128]{1,0:T(8,128)S(1)} custom-call(s32[4,160]{1,0:T(4,128)S(1)} %copy-done.5, bf16[4096,160]{1,0:T(8,128)(2,1)S(1)} %get-tuple-element.51.turned_ref, f32[64,160]{1,0:T(8,128)S(1)} %get-tuple-element.56.lowered_ref, bf16[2048,4096]{1,0:T(8,128)(2,1)} %bitcast.19), custom_call_target="tpu_custom_call" | custom-call | flops 2684354 | bytes 16777 | tf_op jit(solution)/shard_map/pallas_call | solution.py:322
  48.6 9.2 %shard_map.116 = (f32[160,4096]{1,0:T(8,128)S(1)}, bf16[160,1536]{1,0:T(8,128)(2,1)S(1)}) custom-call(s32[1]{0:T(128)} %bitcast.6.owner_ref, bf16[160,1536]{1,0:T(8,128)(2,1)S(1)} %get-tuple-element.86.part_ref.refs_4_, bf16[4096,160]{1,0:T(8,128)(2,1)S(1)} %get-tuple-element.51.turned_ref, bf16[6144,4096]{1,0:T(8,128)(2,1)} %refs_1_), custom_call_target="tpu_custom_call" | custom-call | flops 4026531 | bytes 12582 | tf_op jit(solution)/shard_map/pallas_call | solution.py:427
  57.8 0.0 collective-permute-done.5.refs_1_
  57.8 7.1 %shard_map.117 = bf16[160,1536]{1,0:T(8,128)(2,1)S(1)} custom-call(s32[1]{0:T(128)} %bitcast.5.owner_ref, bf16[4096,160]{1,0:T(8,128)(2,1)S(1)} %get-tuple-element.51.turned_ref, bf16[6144,4096]{1,0:T(8,128)(2,1)} %refs_1_, bf16[160,1536]{1,0:T(8,128)(2,1)} %collective-permute-done.4.refs_0_), custom_call_target="tpu_custom_call" | custom-call | flops 2013265 | bytes 12582 | tf_op jit(solution)/shard_map/pallas_call | solution.py:348
  64.9 0.4 collective-permute-start.8
  65.3 0.0 collective-permute-done.3.refs_1_
  65.3 0.4 collective-permute-start.6
  65.7 0.1 pad_add_fusion.owners_ref
  65.8 0.0 collective-permute-done.9.refs_6_
  65.8 1.6 %collective-permute-start.10 = (f32[160,128]{1,0:T(8,128)S(1)}, f32[160,128]{1,0:T(8,128)S(1)}, u32[]{:S(2)}, u32[]{:S(2)}) collective-permute-start(f32[160,128]{1,0:T(8,128)S(1)} %shard_map.115), channel_id=1, source_target_pairs={{0,1},{1,0},{2,3},{3,2},{4,5},{5,4},{6,7},{7,6},{8,9},{9,8},{10,11... | collective-permute-start | bytes 245768 | tf_op jit(solution)/shard_map/ppermute | solution.py:603
  67.4 2.6 %collective-permute-start.11 = (f32[160,128]{1,0:T(8,128)S(1)}, f32[160,128]{1,0:T(8,128)S(1)}, u32[]{:S(2)}, u32[]{:S(2)}) collective-permute-start(f32[160,128]{1,0:T(8,128)S(1)} %shard_map.115), channel_id=1, source_target_pairs={{0,2},{1,3},{2,0},{3,1},{4,6},{5,7},{6,4},{7,5},{8,10},{9,11},{10,... | collective-permute-start | bytes 245768 | tf_op jit(solution)/shard_map/ppermute | solution.py:603
  70.0 0.0 collective-permute-done.7.refs_0_
  70.0 0.2 collective-permute-start.12
  70.2 13.4 %shard_map.118.refs_2_ = f32[160,4096]{1,0:T(8,128)S(1)} custom-call(s32[2]{0:T(128)S(1)} %pad_add_fusion.owners_ref, bf16[160,1536]{1,0:T(8,128)(2,1)} %collective-permute-done.7.refs_0_, bf16[160,1536]{1,0:T(8,128)(2,1)} %collective-permute-done.3.refs_1_, bf16[6144,4096]{1,0:T(8,128)(2,1)} %refs_1_, bf16[6144,4096]{1,0:T(8,128)(2,1)} %refs_1_, ...), custom_call_target="tpu_custom_call" | custom-call | flops 4026531 | bytes 25165 | tf_op jit(solution)/shard_map/pallas_call | solution.py:485
  83.7 5.2 %collective-permute-done.8.refs_2_ = bf16[160,1536]{1,0:T(8,128)(2,1)S(1)} collective-permute-done((bf16[160,1536]{1,0:T(8,128)(2,1)S(1)}, bf16[160,1536]{1,0:T(8,128)(2,1)S(1)}, u32[]{:S(2)}, u32[]{:S(2)}) %collective-permute-start.8) | collective-permute-done | bytes 491552 | tf_op jit(solution)/shard_map/ppermute | solution.py:603
  88.9 0.0 collective-permute-done.6.refs_0_
  88.9 3.3 %collective-permute-done.10 = f32[160,128]{1,0:T(8,128)S(1)} collective-permute-done((f32[160,128]{1,0:T(8,128)S(1)}, f32[160,128]{1,0:T(8,128)S(1)}, u32[]{:S(2)}, u32[]{:S(2)}) %collective-permute-start.10) | collective-permute-done | bytes 81952 | tf_op jit(solution)/shard_map/ppermute | solution.py:603
  92.2 0.0 collective-permute-done.11
  92.2 1.5 %collective-permute-done.12 = f32[160,128]{1,0:T(8,128)S(1)} collective-permute-done((f32[160,128]{1,0:T(8,128)S(1)}, f32[160,128]{1,0:T(8,128)S(1)}, u32[]{:S(2)}, u32[]{:S(2)}) %collective-permute-start.12) | collective-permute-done | bytes 81952 | tf_op jit(solution)/shard_map/ppermute | solution.py:603
  93.7 2.5 %shard_map.119.refs_0_ = bf16[160,1664]{1,0:T(8,128)(2,1)S(1)} custom-call(s32[4,160]{1,0:T(4,128)S(1)} %copy-done.5, bf16[160,128]{1,0:T(8,128)(2,1)S(1)} %multiply_convert_fusion.ranks_ref.refs_4_, bf16[2048,1536]{1,0:T(8,128)(2,1)S(1)} %bitcast.18, bf16[160,1536]{1,0:T(8,128)(2,1)S(1)} %get-tuple-element.67.refs_0_, ...), custom_call_target="tpu_custom_call" | custom-call | flops 1006632 | bytes 6291 | tf_op jit(solution)/shard_map/pallas_call | solution.py:520
  96.3 0.1 collective-permute-start.17
  96.3 0.5 collective-permute-start.16
  96.8 0.5 collective-permute-start.14
  97.4 0.0 collective-permute-start.13
  97.4 14.6 %shard_map.120 = bf16[160,4096]{1,0:T(8,128)(2,1)} custom-call(s32[1]{0:T(128)} %bitcast.owner_ref.owners_ref, bf16[160,1536]{1,0:T(8,128)(2,1)S(1)} %collective-permute-done.6.refs_0_, bf16[6144,4096]{1,0:T(8,128)(2,1)} %refs_1_, f32[160,4096]{1,0:T(8,128)S(1)} %shard_map.118.refs_2_, s32[4,160]{1,0:T(4,128)S(1)} %copy-done.5, ...), custom_call_target="tpu_custom_call" | custom-call | flops 4697620 | bytes 29360 | tf_op jit(solution)/shard_map/pallas_call | solution.py:485
  112.0 0.0 collective-permute-done.14.refs_2_
  112.0 0.5 collective-permute-start.15
  112.5 1.5 %collective-permute-start.19 = (bf16[160,1536]{1,0:T(8,128)(2,1)S(1)}, bf16[160,1536]{1,0:T(8,128)(2,1)S(1)}, u32[]{:S(2)}, u32[]{:S(2)}) collective-permute-start(bf16[160,1536]{1,0:T(8,128)(2,1)S(1)} %get-tuple-element.86.part_ref.refs_4_), channel_id=1, source_target_pairs={{0,8},{4,12},{8,0},{12,4},{1,9},{5,13},{9,1},{13,5},{2,10},{6,14},... | collective-permute-start | bytes 1474568 | tf_op jit(solution)/shard_map/ppermute | solution.py:603
  114.0 0.0 collective-permute-done.13.refs_1_
  114.0 0.0 collective-permute-start.18
  114.0 0.1 collective-permute-done.15.refs_3_
  114.1 0.0 collective-permute-done.17.refs_7_
  114.1 0.0 collective-permute-done.16.refs_5_
  114.1 7.8 %shard_map.121 = bf16[512,4096]{1,0:T(8,128)(2,1)} custom-call(s32[1]{0:T(128)} %bitcast.1.place_ref, s32[4,160]{1,0:T(4,128)S(1)} %copy-done.7, bf16[160,1664]{1,0:T(8,128)(2,1)S(1)} %shard_map.119.refs_0_, bf16[160,1664]{1,0:T(8,128)(2,1)S(1)} %collective-permute-done.13.refs_1_, bf16[160,1664]{1,0:T(8,128)(2,1)S(1)} %collective-permute-done.14.refs_2_, ...), custom_call_target="tpu_custom_call" | custom-call | flops 2684354 | bytes 9437 | tf_op jit(solution)/shard_map/pallas_call | solution.py:558
  121.9 2.7 %shard_map.122 = bf16[320,1536]{1,0:T(8,128)(2,1)} custom-call(s32[1]{0:T(128)} %bitcast.1.place_ref, s32[4,4]{1,0:T(4,128)S(1)} %copy-done.6, bf16[160,1664]{1,0:T(8,128)(2,1)S(1)} %shard_map.119.refs_0_, bf16[160,1664]{1,0:T(8,128)(2,1)S(1)} %collective-permute-done.13.refs_1_, bf16[160,1664]{1,0:T(8,128)(2,1)S(1)} %collective-permute-done.14.refs_2_, ...), custom_call_target="tpu_custom_call" | custom-call | flops 629145 | bytes 3932 | tf_op jit(solution)/shard_map/pallas_call | solution.py:590
  124.6 1.1 collective-permute-done.19.refs_6_
  125.7 0.0 collective-permute-start.20
  125.7 0.0 collective-permute-done.18.refs_5_
  125.7 1.9 %collective-permute-done.20.refs_7_ = bf16[160,1536]{1,0:T(8,128)(2,1)S(1)} collective-permute-done((bf16[160,1536]{1,0:T(8,128)(2,1)S(1)}, bf16[160,1536]{1,0:T(8,128)(2,1)S(1)}, u32[]{:S(2)}, u32[]{:S(2)}) %collective-permute-start.20) | collective-permute-done | bytes 491552 | tf_op jit(solution)/shard_map/ppermute | solution.py:603
  127.6 3.4 %shard_map.123 = bf16[512,1536]{1,0:T(8,128)(2,1)} custom-call(s32[1]{0:T(128)} %bitcast.1.place_ref, s32[4,160]{1,0:T(4,128)S(1)} %copy-done.7, bf16[160,1664]{1,0:T(8,128)(2,1)S(1)} %shard_map.119.refs_0_, bf16[160,1664]{1,0:T(8,128)(2,1)S(1)} %collective-permute-done.13.refs_1_, bf16[160,1664]{1,0:T(8,128)(2,1)S(1)} %collective-permute-done.14.refs_2_, ...), custom_call_target="tpu_custom_call" | custom-call | flops 1006632 | bytes 3538 | tf_op jit(solution)/shard_map/pallas_call | solution.py:558
  (20 shorter events, 0.1 us)
Async XLA Ops:
  3.5 11.8 %collective-permute-start = (bf16[80,1536]{1,0:T(8,128)(2,1)}, bf16[80,1536]{1,0:T(8,128)(2,1)S(1)}, u32[]{:S(2)}, u32[]{:S(2)}) collective-permute-start(bf16[80,1536]{1,0:T(8,128)(2,1)} %get-tuple-element.47), channel_id=1, source_target_pairs={{0,4},{4,0},{8,12},{12,8},{1,5},{5,1},{9,13},{13,9},{2,6},{6,2},{1... | collective-permute-start | bytes 737288 | tf_op jit(solution)/shard_map/ppermute | solution.py:603
  3.9 11.4 %collective-permute-start.1 = (bf16[80,1536]{1,0:T(8,128)(2,1)}, bf16[80,1536]{1,0:T(8,128)(2,1)S(1)}, u32[]{:S(2)}, u32[]{:S(2)}) collective-permute-start(bf16[80,1536]{1,0:T(8,128)(2,1)} %get-tuple-element.48), channel_id=1, source_target_pairs={{0,8},{4,12},{8,0},{12,4},{1,9},{5,13},{9,1},{13,5},{2,10},{6,14},... | collective-permute-start | bytes 737288 | tf_op jit(solution)/shard_map/ppermute | solution.py:603
  6.4 11.8 %collective-permute-start.2 = (bf16[80,1536]{1,0:T(8,128)(2,1)}, bf16[80,1536]{1,0:T(8,128)(2,1)S(1)}, u32[]{:S(2)}, u32[]{:S(2)}) collective-permute-start(bf16[80,1536]{1,0:T(8,128)(2,1)} %get-tuple-element.49), channel_id=1, source_target_pairs={{0,12},{4,8},{8,4},{12,0},{1,13},{5,9},{9,5},{13,1},{2,14},{6,10},... | collective-permute-start | bytes 737288 | tf_op jit(solution)/shard_map/ppermute | solution.py:603
  15.3 14.1 %copy-start.1 = (bf16[80,1536]{1,0:T(8,128)(2,1)}, bf16[80,1536]{1,0:T(8,128)(2,1)S(1)}, u32[]{:S(2)}) copy-start(bf16[80,1536]{1,0:T(8,128)(2,1)S(1)} %collective-permute-done.1.refs_1_) | copy-start | bytes 737284
  18.3 11.2 %copy-start.3 = (bf16[80,1536]{1,0:T(8,128)(2,1)}, bf16[80,1536]{1,0:T(8,128)(2,1)S(1)}, u32[]{:S(2)}) copy-start(bf16[80,1536]{1,0:T(8,128)(2,1)S(1)} %collective-permute-done.2.refs_2_) | copy-start | bytes 737284
  18.3 47.6 %collective-permute-start.9 = (bf16[160,4096]{1,0:T(8,128)(2,1)}, bf16[160,4096]{1,0:T(8,128)(2,1)}, u32[]{:S(2)}, u32[]{:S(2)}) collective-permute-start(bf16[160,4096]{1,0:T(8,128)(2,1)} %refs_4_.1), channel_id=1, source_target_pairs={{0,8},{4,12},{8,0},{12,4},{1,9},{5,13},{9,1},{13,5},{2,10},{6,14},... | collective-permute-start | bytes 3932168 | tf_op jit(solution)/shard_map/ppermute | solution.py:603
  19.8 20.2 %collective-permute-start.4 = (bf16[160,1536]{1,0:T(8,128)(2,1)}, bf16[160,1536]{1,0:T(8,128)(2,1)}, u32[]{:S(2)}, u32[]{:S(2)}) collective-permute-start(bf16[160,1536]{1,0:T(8,128)(2,1)} %get-tuple-element.52), channel_id=1, source_target_pairs={{0,1},{1,0},{2,3},{3,2},{4,5},{5,4},{6,7},{7,6},{8,9},{9,8},{10,11... | collective-permute-start | bytes 1474568 | tf_op jit(solution)/shard_map/ppermute | solution.py:603
  21.4 8.6 %slice-start = ((s8[6291456]{0:T(1024)(128)(4,1)}), s8[4194304]{0:T(1024)(128)(4,1)S(1)}, s32[]{:S(2)}) async-start(s8[6291456]{0:T(1024)(128)(4,1)} %bitcast.13), calls=%async_computation | async-start | bytes 8388608
  21.4 8.6 %slice-start.1 = ((s8[6291456]{0:T(1024)(128)(4,1)}), s8[2097152]{0:T(1024)(128)(4,1)S(1)}, s32[]{:S(2)}) async-start(s8[6291456]{0:T(1024)(128)(4,1)} %bitcast.13), calls=%async_computation.1 | async-start | bytes 4194304
  21.4 8.6 %copy-start = (bf16[320,1536]{1,0:T(8,128)(2,1)S(1)}, bf16[320,1536]{1,0:T(8,128)(2,1)}, u32[]{:S(2)}) copy-start(bf16[320,1536]{1,0:T(8,128)(2,1)} %rows_ref.3) | copy-start | bytes 2949124
  21.4 8.6 %copy-start.5 = (s32[4,160]{1,0:T(4,128)S(1)}, s32[4,160]{1,0:T(4,128)}, u32[]{:S(2)}) copy-start(s32[4,160]{1,0:T(4,128)} %get-tuple-element.46.tenant_ref.refs_3_) | copy-start | bytes 7684
  21.4 8.6 %copy-start.6 = (s32[4,4]{1,0:T(4,128)S(1)}, s32[4,4]{1,0:T(4,128)}, u32[]{:S(2)}) copy-start(s32[4,4]{1,0:T(4,128)} %handoff_ref.5) | copy-start | bytes 196
  29.5 28.3 %collective-permute-start.5 = (bf16[160,1536]{1,0:T(8,128)(2,1)S(1)}, bf16[160,1536]{1,0:T(8,128)(2,1)}, u32[]{:S(2)}, u32[]{:S(2)}) collective-permute-start(bf16[160,1536]{1,0:T(8,128)(2,1)S(1)} %shard_map.113), channel_id=1, source_target_pairs={{0,1},{1,0},{2,3},{3,2},{4,5},{5,4},{6,7},{7,6},{8,9},{9,8},{10,11... | collective-permute-start | bytes 1474568 | tf_op jit(solution)/shard_map/ppermute | solution.py:603
  30.0 0.9 copy-start.2
  31.0 0.9 copy-start.4
  35.8 29.5 %collective-permute-start.3 = (bf16[160,1536]{1,0:T(8,128)(2,1)S(1)}, bf16[160,1536]{1,0:T(8,128)(2,1)}, u32[]{:S(2)}, u32[]{:S(2)}) collective-permute-start(bf16[160,1536]{1,0:T(8,128)(2,1)S(1)} %get-tuple-element.86.part_ref.refs_4_), channel_id=1, source_target_pairs={{0,2},{1,3},{2,0},{3,1},{4,6},{5,7},{6,4},{7,5},{8,10},{9,11},{10,... | collective-permute-start | bytes 1474568 | tf_op jit(solution)/shard_map/ppermute | solution.py:603
  38.5 31.5 %collective-permute-start.7 = (bf16[160,1536]{1,0:T(8,128)(2,1)S(1)}, bf16[160,1536]{1,0:T(8,128)(2,1)}, u32[]{:S(2)}, u32[]{:S(2)}) collective-permute-start(bf16[160,1536]{1,0:T(8,128)(2,1)S(1)} %get-tuple-element.86.part_ref.refs_4_), channel_id=1, source_target_pairs={{0,1},{1,0},{2,3},{3,2},{4,5},{5,4},{6,7},{7,6},{8,9},{9,8},{10,11... | collective-permute-start | bytes 1474568 | tf_op jit(solution)/shard_map/ppermute | solution.py:603
  64.9 24.0 %collective-permute-start.8 = (bf16[160,1536]{1,0:T(8,128)(2,1)S(1)}, bf16[160,1536]{1,0:T(8,128)(2,1)S(1)}, u32[]{:S(2)}, u32[]{:S(2)}) collective-permute-start(bf16[160,1536]{1,0:T(8,128)(2,1)S(1)} %shard_map.117), channel_id=1, source_target_pairs={{0,2},{1,3},{2,0},{3,1},{4,6},{5,7},{6,4},{7,5},{8,10},{9,11},{10,... | collective-permute-start | bytes 1474568 | tf_op jit(solution)/shard_map/ppermute | solution.py:603
  65.3 23.6 %collective-permute-start.6 = (bf16[160,1536]{1,0:T(8,128)(2,1)}, bf16[160,1536]{1,0:T(8,128)(2,1)S(1)}, u32[]{:S(2)}, u32[]{:S(2)}) collective-permute-start(bf16[160,1536]{1,0:T(8,128)(2,1)} %collective-permute-done.3.refs_1_), channel_id=1, source_target_pairs={{0,1},{1,0},{2,3},{3,2},{4,5},{5,4},{6,7},{7,6},{8,9},{9,8},{10,11... | collective-permute-start | bytes 1474568 | tf_op jit(solution)/shard_map/ppermute | solution.py:603
  65.8 26.3 %collective-permute-start.10 = (f32[160,128]{1,0:T(8,128)S(1)}, f32[160,128]{1,0:T(8,128)S(1)}, u32[]{:S(2)}, u32[]{:S(2)}) collective-permute-start(f32[160,128]{1,0:T(8,128)S(1)} %shard_map.115), channel_id=1, source_target_pairs={{0,1},{1,0},{2,3},{3,2},{4,5},{5,4},{6,7},{7,6},{8,9},{9,8},{10,11... | collective-permute-start | bytes 245768 | tf_op jit(solution)/shard_map/ppermute | solution.py:603
  67.4 24.8 %collective-permute-start.11 = (f32[160,128]{1,0:T(8,128)S(1)}, f32[160,128]{1,0:T(8,128)S(1)}, u32[]{:S(2)}, u32[]{:S(2)}) collective-permute-start(f32[160,128]{1,0:T(8,128)S(1)} %shard_map.115), channel_id=1, source_target_pairs={{0,2},{1,3},{2,0},{3,1},{4,6},{5,7},{6,4},{7,5},{8,10},{9,11},{10,... | collective-permute-start | bytes 245768 | tf_op jit(solution)/shard_map/ppermute | solution.py:603
  70.0 23.7 %collective-permute-start.12 = (f32[160,128]{1,0:T(8,128)S(1)}, f32[160,128]{1,0:T(8,128)S(1)}, u32[]{:S(2)}, u32[]{:S(2)}) collective-permute-start(f32[160,128]{1,0:T(8,128)S(1)} %shard_map.115), channel_id=1, source_target_pairs={{0,3},{1,2},{2,1},{3,0},{4,7},{5,6},{6,5},{7,4},{8,11},{9,10},{10,... | collective-permute-start | bytes 245768 | tf_op jit(solution)/shard_map/ppermute | solution.py:603
  70.2 23.5 %slice-start.2 = ((s8[6291456]{0:T(1024)(128)(4,1)}), s8[4194304]{0:T(1024)(128)(4,1)S(1)}, s32[]{:S(2)}) async-start(s8[6291456]{0:T(1024)(128)(4,1)} %bitcast.16), calls=%async_computation.2 | async-start | bytes 8388608
  70.2 23.5 %slice-start.3 = ((s8[6291456]{0:T(1024)(128)(4,1)}), s8[2097152]{0:T(1024)(128)(4,1)S(1)}, s32[]{:S(2)}) async-start(s8[6291456]{0:T(1024)(128)(4,1)} %bitcast.16), calls=%async_computation.3 | async-start | bytes 4194304
  96.3 17.8 %copy-start.7 = (s32[4,160]{1,0:T(4,128)S(1)}, s32[4,160]{1,0:T(4,128)}, u32[]{:S(2)}) copy-start(s32[4,160]{1,0:T(4,128)} %get-tuple-element.70.slot_ref) | copy-start | bytes 7684
  96.3 17.8 %collective-permute-start.17 = (bf16[160,4096]{1,0:T(8,128)(2,1)}, bf16[160,4096]{1,0:T(8,128)(2,1)S(1)}, u32[]{:S(2)}, u32[]{:S(2)}) collective-permute-start(bf16[160,4096]{1,0:T(8,128)(2,1)} %collective-permute-done.9.refs_6_), channel_id=1, source_target_pairs={{0,4},{4,0},{8,12},{12,8},{1,5},{5,1},{9,13},{13,9},{2,6},{6,2},{1... | collective-permute-start | bytes 3932168 | tf_op jit(solution)/shard_map/ppermute | solution.py:603
  96.3 17.7 %collective-permute-start.16 = (bf16[160,4096]{1,0:T(8,128)(2,1)}, bf16[160,4096]{1,0:T(8,128)(2,1)S(1)}, u32[]{:S(2)}, u32[]{:S(2)}) collective-permute-start(bf16[160,4096]{1,0:T(8,128)(2,1)} %refs_4_.1), channel_id=1, source_target_pairs={{0,4},{4,0},{8,12},{12,8},{1,5},{5,1},{9,13},{13,9},{2,6},{6,2},{1... | collective-permute-start | bytes 3932168 | tf_op jit(solution)/shard_map/ppermute | solution.py:603
  96.8 15.2 %collective-permute-start.14 = (bf16[160,1664]{1,0:T(8,128)(2,1)S(1)}, bf16[160,1664]{1,0:T(8,128)(2,1)S(1)}, u32[]{:S(2)}, u32[]{:S(2)}) collective-permute-start(bf16[160,1664]{1,0:T(8,128)(2,1)S(1)} %shard_map.119.refs_0_), channel_id=1, source_target_pairs={{0,8},{4,12},{8,0},{12,4},{1,9},{5,13},{9,1},{13,5},{2,10},{6,14},... | collective-permute-start | bytes 1597448 | tf_op jit(solution)/shard_map/ppermute | solution.py:603
  97.4 16.6 %collective-permute-start.13 = (bf16[160,1664]{1,0:T(8,128)(2,1)S(1)}, bf16[160,1664]{1,0:T(8,128)(2,1)S(1)}, u32[]{:S(2)}, u32[]{:S(2)}) collective-permute-start(bf16[160,1664]{1,0:T(8,128)(2,1)S(1)} %shard_map.119.refs_0_), channel_id=1, source_target_pairs={{0,4},{4,0},{8,12},{12,8},{1,5},{5,1},{9,13},{13,9},{2,6},{6,2},{1... | collective-permute-start | bytes 1597448 | tf_op jit(solution)/shard_map/ppermute | solution.py:603
  112.0 2.1 %collective-permute-start.15 = (bf16[160,1664]{1,0:T(8,128)(2,1)S(1)}, bf16[160,1664]{1,0:T(8,128)(2,1)S(1)}, u32[]{:S(2)}, u32[]{:S(2)}) collective-permute-start(bf16[160,1664]{1,0:T(8,128)(2,1)S(1)} %collective-permute-done.14.refs_2_), channel_id=1, source_target_pairs={{0,4},{4,0},{8,12},{12,8},{1,5},{5,1},{9,13},{13,9},{2,6},{6,2},{1... | collective-permute-start | bytes 1597448 | tf_op jit(solution)/shard_map/ppermute | solution.py:603
  112.5 13.2 %collective-permute-start.19 = (bf16[160,1536]{1,0:T(8,128)(2,1)S(1)}, bf16[160,1536]{1,0:T(8,128)(2,1)S(1)}, u32[]{:S(2)}, u32[]{:S(2)}) collective-permute-start(bf16[160,1536]{1,0:T(8,128)(2,1)S(1)} %get-tuple-element.86.part_ref.refs_4_), channel_id=1, source_target_pairs={{0,8},{4,12},{8,0},{12,4},{1,9},{5,13},{9,1},{13,5},{2,10},{6,14},... | collective-permute-start | bytes 1474568 | tf_op jit(solution)/shard_map/ppermute | solution.py:603
  114.0 11.7 %collective-permute-start.18 = (bf16[160,1536]{1,0:T(8,128)(2,1)S(1)}, bf16[160,1536]{1,0:T(8,128)(2,1)S(1)}, u32[]{:S(2)}, u32[]{:S(2)}) collective-permute-start(bf16[160,1536]{1,0:T(8,128)(2,1)S(1)} %get-tuple-element.86.part_ref.refs_4_), channel_id=1, source_target_pairs={{0,4},{4,0},{8,12},{12,8},{1,5},{5,1},{9,13},{13,9},{2,6},{6,2},{1... | collective-permute-start | bytes 1474568 | tf_op jit(solution)/shard_map/ppermute | solution.py:603
  125.7 1.9 %collective-permute-start.20 = (bf16[160,1536]{1,0:T(8,128)(2,1)S(1)}, bf16[160,1536]{1,0:T(8,128)(2,1)S(1)}, u32[]{:S(2)}, u32[]{:S(2)}) collective-permute-start(bf16[160,1536]{1,0:T(8,128)(2,1)S(1)} %collective-permute-done.19.refs_6_), channel_id=1, source_target_pairs={{0,4},{4,0},{8,12},{12,8},{1,5},{5,1},{9,13},{13,9},{2,6},{6,2},{1... | collective-permute-start | bytes 1474568 | tf_op jit(solution)/shard_map/ppermute | solution.py:603

commit v4 on v3

--- a/solution.py
+++ b/solution.py
@@ -646,20 +646,18 @@
     beside = swap(gathered, "fsdp", 1)
     pair = swap(gathered, "fsdp", 2)
     cot_x = swap(after(cotangent, *arrived, far), "dp", 2)
-    partial = rank_backward(tenant, turned, after(up, gathered, for_far), lowered, 512)
+    across = base_gradient(owner[2].reshape(1), turned, after(frozen_weight, gathered), width, 512, for_far)
+    from_pair = swap(across, "fsdp", 2)
+    partial = rank_backward(tenant, turned, after(up, across), lowered, 512)
     first, own = own_and_forward(
-        owner[0].reshape(1), gathered, turned, after(frozen_weight, partial), 512
-    )
-    late = after(partial, first, cot_x)
+        owner[0].reshape(1), gathered, turned, after(frozen_weight, partial, from_near), 512
+    )
+    late = after(partial, first, cot_x, beside)
     sums = [swap(late, "fsdp", k) for k in (1, 2, 3)]
-    across = base_gradient(
-        owner[2].reshape(1), turned, after(frozen_weight, first, from_near), width, 512, for_far
-    )
-    from_pair = swap(across, "fsdp", 2)
-    diagonal = swap(after(pair, across), "fsdp", 1)
-    gathered_x = swap(after(gathered, across, cot_x), "dp", 2)
+    diagonal = swap(after(pair, first), "fsdp", 1)
+    gathered_x = swap(after(gathered, first, cot_x), "dp", 2)
     second = forward(
-        jnp.stack([owner[1], owner[2]]), [beside, pair], after(frozen_weight, across), 512, first
+        jnp.stack([owner[1], owner[2]]), [beside, pair], after(frozen_weight, first), 512, first
     )
     scale = jnp.where(jnp.arange(2 * rank) < rank, 1.0, adapter_scale).astype(F32)
     ranks = ((after(partial, second, from_pair) + sums[0] + (sums[1] + sums[2])) * scale).astype(BF)

time: 131 us -> 129 us (0.985)
  waiting for transfers between devices: 16 us -> 13.1 us
    ppermute x21, waiting for transfers between devices: 16 us -> 13.1 us  [swap(): return lax.ppermute(values, axis, [(i, i ^ distance) for i in range(size)])]
  transfers between devices with their start and end apart: 21 -> 21, of which waited for: 7 -> 5; matrix products, arithmetic and copies ran while one was open for 0% -> 0% of each run, Pallas kernels for 64% -> 66%
where the time goes in v4:
time: 129 us; the launch traced here: 128 us
  Pallas kernels  92.9 us (72%)
  starting transfers between devices  19.4 us (15%)
  waiting for transfers between devices  13.1 us (10%)
  local copies, waits for them, and re-layouts  1.93 us (1%)
    pallas_call x2, Pallas kernels, forward(): pl.pallas_call(kernel, grid_spec=pltpu.PrefetchScalarGridSpec(num_scalar_...  28.1 us
    ppermute x21, starting transfers between devices, swap(): return lax.ppermute(values, axis, [(i, i ^ distance) for i in range(size)])  19.4 us
    pallas_call x2, Pallas kernels, base_gradient(): pl.pallas_call(kernel, grid_spec=pltpu.PrefetchScalarGridSpec(num_scalar_...  15.1 us
    ppermute x21, waiting for transfers between devices, swap(): return lax.ppermute(values, axis, [(i, i ^ distance) for i in range(size)])  13.1 us
    pallas_call x2, Pallas kernels, owned_gradient(): pl.pallas_call(kernel, grid=(width // block,), in_specs=[SMEM(), whole(sl...  11.2 us
    pallas_call x1, Pallas kernels, own_and_forward(): pl.pallas_call(kernel, grid_spec=pltpu.PrefetchScalarGridSpec(num_scalar_...  9.21 us
    pallas_call x1, Pallas kernels, turn_and_far(): pl.pallas_call(kernel, grid_spec=pltpu.PrefetchScalarGridSpec(num_scalar_...  8.77 us
    pallas_call x1, Pallas kernels, rank_backward(): pl.pallas_call(kernel, grid=(steps,), in_specs=[whole(tenant.shape), whol...  8.51 us
  transfers between devices with their start and end apart: 21, of which 5 were waited for; matrix products, arithmetic and copies ran while one was open for 0% of the time, Pallas kernels for 66%

profile of v4, /device:TPU:0, one launch (start us, length us, event | category | flops | bytes accessed | tf_op | source)
XLA Modules:
  0.0 128.2 jit_solution(17065236653577894044)
XLA Ops:
  0.6 2.8 %shard_map.111 = (bf16[80,1536]{1,0:T(8,128)(2,1)}, bf16[80,1536]{1,0:T(8,128)(2,1)}, bf16[80,1536]{1,0:T(8,128)(2,1)}, s32[4,160]{1,0:T(4,128)}, s32[4,160]{1,0:T(4,128)}) custom-call(s32[1]{0:T(128)} %bitcast.1.place_ref, s32[4,4]{1,0:T(4,128)} %handoff_ref.5, s32[32]{0:T(128)} %slots_ref.1, s32[4,32]{1,0:T(4,128)} %counts_ref.1, bf16[320,1536]{1,0:T(8,128)(2,1)} %rows_ref.3), custom_call_target="tpu_custom_call" | custom-call | flops 235929 | bytes 1966 | tf_op jit(solution)/shard_map/pallas_call | solution.py:232
  3.5 0.5 collective-permute-start
  3.9 2.5 %collective-permute-start.1 = (bf16[80,1536]{1,0:T(8,128)(2,1)}, bf16[80,1536]{1,0:T(8,128)(2,1)S(1)}, u32[]{:S(2)}, u32[]{:S(2)}) collective-permute-start(bf16[80,1536]{1,0:T(8,128)(2,1)} %get-tuple-element.48), channel_id=1, source_target_pairs={{0,8},{4,12},{8,0},{12,4},{1,9},{5,13},{9,1},{13,5},{2,10},{6,14},... | collective-permute-start | bytes 737288 | tf_op jit(solution)/shard_map/ppermute | solution.py:603
  6.4 0.1 collective-permute-start.2
  6.5 8.8 %shard_map.112 = (bf16[160,1536]{1,0:T(8,128)(2,1)}, bf16[4096,160]{1,0:T(8,128)(2,1)S(1)}) custom-call(s32[1]{0:T(128)} %bitcast.owner_ref.owners_ref, bf16[160,4096]{1,0:T(8,128)(2,1)} %refs_4_.1, bf16[6144,4096]{1,0:T(8,128)(2,1)} %refs_1_), custom_call_target="tpu_custom_call" | custom-call | flops 2013265 | bytes 12582 | tf_op jit(solution)/shard_map/pallas_call | solution.py:377
  15.3 0.0 collective-permute-done.refs_0_
  15.3 0.0 collective-permute-done.1.refs_1_
  15.3 0.0 copy-start.1
  15.3 2.9 %collective-permute-done.2.refs_2_ = bf16[80,1536]{1,0:T(8,128)(2,1)S(1)} collective-permute-done((bf16[80,1536]{1,0:T(8,128)(2,1)}, bf16[80,1536]{1,0:T(8,128)(2,1)S(1)}, u32[]{:S(2)}, u32[]{:S(2)}) %collective-permute-start.2) | collective-permute-done | bytes 245792 | tf_op jit(solution)/shard_map/ppermute | solution.py:603
  18.3 1.5 %collective-permute-start.9 = (bf16[160,4096]{1,0:T(8,128)(2,1)}, bf16[160,4096]{1,0:T(8,128)(2,1)}, u32[]{:S(2)}, u32[]{:S(2)}) collective-permute-start(bf16[160,4096]{1,0:T(8,128)(2,1)} %refs_4_.1), channel_id=1, source_target_pairs={{0,8},{4,12},{8,0},{12,4},{1,9},{5,13},{9,1},{13,5},{2,10},{6,14},... | collective-permute-start | bytes 3932168 | tf_op jit(solution)/shard_map/ppermute | solution.py:603
  19.8 1.6 %collective-permute-start.4 = (bf16[160,1536]{1,0:T(8,128)(2,1)}, bf16[160,1536]{1,0:T(8,128)(2,1)}, u32[]{:S(2)}, u32[]{:S(2)}) collective-permute-start(bf16[160,1536]{1,0:T(8,128)(2,1)} %get-tuple-element.52), channel_id=1, source_target_pairs={{0,1},{1,0},{2,3},{3,2},{4,5},{5,4},{6,7},{7,6},{8,9},{9,8},{10,11... | collective-permute-start | bytes 1474568 | tf_op jit(solution)/shard_map/ppermute | solution.py:603
  21.4 0.0 copy-start.6
  21.4 8.0 %shard_map.113 = bf16[160,1536]{1,0:T(8,128)(2,1)S(1)} custom-call(s32[1]{0:T(128)} %bitcast.4.owner_ref, bf16[4096,160]{1,0:T(8,128)(2,1)S(1)} %get-tuple-element.51.turned_ref, bf16[6144,4096]{1,0:T(8,128)(2,1)} %refs_1_), custom_call_target="tpu_custom_call" | custom-call | flops 2013265 | bytes 12582 | tf_op jit(solution)/shard_map/pallas_call | solution.py:348
  29.5 0.0 copy-done.1
  29.5 0.0 copy-done.3
  29.5 0.5 collective-permute-start.5
  30.0 0.0 slice-done.1
  30.0 0.0 copy-start.2
  30.0 0.9 copy-done.2
  31.0 0.9 copy-done.4
  31.9 3.9 %shard_map.114 = (bf16[160,1536]{1,0:T(8,128)(2,1)S(1)}, f32[64,160]{1,0:T(8,128)S(1)}) custom-call(s32[1]{0:T(128)} %bitcast.1.place_ref, s32[4,4]{1,0:T(4,128)S(1)} %copy-done.6, s32[4,160]{1,0:T(4,128)S(1)} %copy-done.5, bf16[320,1536]{1,0:T(8,128)(2,1)S(1)} %copy-done, bf16[80,1536]{1,0:T(8,128)(2,1)S(1)} %collective-permute-done.refs_0_, ...), custom_call_target="tpu_custom_call" | custom-call | flops 1006632 | bytes 7766 | tf_op jit(solution)/shard_map/pallas_call | solution.py:285
  35.8 2.6 %collective-permute-start.3 = (bf16[160,1536]{1,0:T(8,128)(2,1)S(1)}, bf16[160,1536]{1,0:T(8,128)(2,1)}, u32[]{:S(2)}, u32[]{:S(2)}) collective-permute-start(bf16[160,1536]{1,0:T(8,128)(2,1)S(1)} %get-tuple-element.86.part_ref.refs_4_), channel_id=1, source_target_pairs={{0,2},{1,3},{2,0},{3,1},{4,6},{5,7},{6,4},{7,5},{8,10},{9,11},{10,... | collective-permute-start | bytes 1474568 | tf_op jit(solution)/shard_map/ppermute | solution.py:603
  38.5 1.6 %collective-permute-start.7 = (bf16[160,1536]{1,0:T(8,128)(2,1)S(1)}, bf16[160,1536]{1,0:T(8,128)(2,1)}, u32[]{:S(2)}, u32[]{:S(2)}) collective-permute-start(bf16[160,1536]{1,0:T(8,128)(2,1)S(1)} %get-tuple-element.86.part_ref.refs_4_), channel_id=1, source_target_pairs={{0,1},{1,0},{2,3},{3,2},{4,5},{5,4},{6,7},{7,6},{8,9},{9,8},{10,11... | collective-permute-start | bytes 1474568 | tf_op jit(solution)/shard_map/ppermute | solution.py:603
  40.0 0.0 collective-permute-done.4.refs_0_
  40.0 7.1 %shard_map.115 = bf16[160,1536]{1,0:T(8,128)(2,1)S(1)} custom-call(s32[1]{0:T(128)} %bitcast.7.owner_ref, bf16[4096,160]{1,0:T(8,128)(2,1)S(1)} %get-tuple-element.51.turned_ref, bf16[6144,4096]{1,0:T(8,128)(2,1)} %refs_1_, bf16[160,1536]{1,0:T(8,128)(2,1)} %collective-permute-done.4.refs_0_), custom_call_target="tpu_custom_call" | custom-call | flops 2013265 | bytes 12582 | tf_op jit(solution)/shard_map/pallas_call | solution.py:348
  47.1 0.4 collective-permute-start.8
  47.5 8.5 %shard_map.116 = f32[160,128]{1,0:T(8,128)S(1)} custom-call(s32[4,160]{1,0:T(4,128)S(1)} %copy-done.5, bf16[4096,160]{1,0:T(8,128)(2,1)S(1)} %get-tuple-element.51.turned_ref, f32[64,160]{1,0:T(8,128)S(1)} %get-tuple-element.56.lowered_ref, bf16[2048,4096]{1,0:T(8,128)(2,1)} %bitcast.19), custom_call_target="tpu_custom_call" | custom-call | flops 2684354 | bytes 16777 | tf_op jit(solution)/shard_map/pallas_call | solution.py:322
  56.1 0.0 collective-permute-done.5.refs_1_
  56.1 9.2 %shard_map.117 = (f32[160,4096]{1,0:T(8,128)S(1)}, bf16[160,1536]{1,0:T(8,128)(2,1)S(1)}) custom-call(s32[1]{0:T(128)} %bitcast.5.owner_ref, bf16[160,1536]{1,0:T(8,128)(2,1)S(1)} %get-tuple-element.86.part_ref.refs_4_, bf16[4096,160]{1,0:T(8,128)(2,1)S(1)} %get-tuple-element.51.turned_ref, bf16[6144,4096]{1,0:T(8,128)(2,1)} %refs_1_), custom_call_target="tpu_custom_call" | custom-call | flops 4026531 | bytes 12582 | tf_op jit(solution)/shard_map/pallas_call | solution.py:427
  65.3 0.0 collective-permute-done.3.refs_1_
  65.3 0.5 collective-permute-start.6
  65.8 0.1 pad_add_fusion.owners_ref
  65.9 6.9 %collective-permute-done.7.refs_0_ = bf16[160,1536]{1,0:T(8,128)(2,1)} collective-permute-done((bf16[160,1536]{1,0:T(8,128)(2,1)S(1)}, bf16[160,1536]{1,0:T(8,128)(2,1)}, u32[]{:S(2)}, u32[]{:S(2)}) %collective-permute-start.7) | collective-permute-done | bytes 491552 | tf_op jit(solution)/shard_map/ppermute | solution.py:603
  72.8 0.0 collective-permute-done.9.refs_6_
  72.8 1.4 %collective-permute-start.12 = (f32[160,128]{1,0:T(8,128)S(1)}, f32[160,128]{1,0:T(8,128)S(1)}, u32[]{:S(2)}, u32[]{:S(2)}) collective-permute-start(f32[160,128]{1,0:T(8,128)S(1)} %shard_map.116), channel_id=1, source_target_pairs={{0,3},{1,2},{2,1},{3,0},{4,7},{5,6},{6,5},{7,4},{8,11},{9,10},{10,... | collective-permute-start | bytes 245768 | tf_op jit(solution)/shard_map/ppermute | solution.py:603
  74.1 0.0 collective-permute-start.11
  74.1 3.0 %collective-permute-start.10 = (f32[160,128]{1,0:T(8,128)S(1)}, f32[160,128]{1,0:T(8,128)S(1)}, u32[]{:S(2)}, u32[]{:S(2)}) collective-permute-start(f32[160,128]{1,0:T(8,128)S(1)} %shard_map.116), channel_id=1, source_target_pairs={{0,1},{1,0},{2,3},{3,2},{4,5},{5,4},{6,7},{7,6},{8,9},{9,8},{10,11... | collective-permute-start | bytes 245768 | tf_op jit(solution)/shard_map/ppermute | solution.py:603
  77.2 13.4 %shard_map.118.refs_2_ = f32[160,4096]{1,0:T(8,128)S(1)} custom-call(s32[2]{0:T(128)S(1)} %pad_add_fusion.owners_ref, bf16[160,1536]{1,0:T(8,128)(2,1)} %collective-permute-done.7.refs_0_, bf16[160,1536]{1,0:T(8,128)(2,1)} %collective-permute-done.3.refs_1_, bf16[6144,4096]{1,0:T(8,128)(2,1)} %refs_1_, bf16[6144,4096]{1,0:T(8,128)(2,1)} %refs_1_, ...), custom_call_target="tpu_custom_call" | custom-call | flops 4026531 | bytes 25165 | tf_op jit(solution)/shard_map/pallas_call | solution.py:485
  90.6 0.0 collective-permute-done.8.refs_2_
  90.6 0.0 collective-permute-done.6.refs_0_
  90.6 0.0 collective-permute-done.12
  90.7 0.0 collective-permute-done.11
  90.7 0.4 collective-permute-done.10
  91.1 2.5 %shard_map.119.refs_0_ = bf16[160,1664]{1,0:T(8,128)(2,1)S(1)} custom-call(s32[4,160]{1,0:T(4,128)S(1)} %copy-done.5, bf16[160,128]{1,0:T(8,128)(2,1)S(1)} %multiply_convert_fusion.ranks_ref.refs_4_, bf16[2048,1536]{1,0:T(8,128)(2,1)S(1)} %bitcast.18, bf16[160,1536]{1,0:T(8,128)(2,1)S(1)} %get-tuple-element.67.refs_0_, ...), custom_call_target="tpu_custom_call" | custom-call | flops 1006632 | bytes 6291 | tf_op jit(solution)/shard_map/pallas_call | solution.py:520
  93.7 0.1 collective-permute-start.16
  93.7 0.5 collective-permute-start.17
  94.2 0.4 collective-permute-start.14
  94.6 0.0 collective-permute-start.13
  94.6 14.6 %shard_map.120 = bf16[160,4096]{1,0:T(8,128)(2,1)} custom-call(s32[1]{0:T(128)} %bitcast.owner_ref.owners_ref, bf16[160,1536]{1,0:T(8,128)(2,1)S(1)} %collective-permute-done.6.refs_0_, bf16[6144,4096]{1,0:T(8,128)(2,1)} %refs_1_, f32[160,4096]{1,0:T(8,128)S(1)} %shard_map.118.refs_2_, s32[4,160]{1,0:T(4,128)S(1)} %copy-done.5, ...), custom_call_target="tpu_custom_call" | custom-call | flops 4697620 | bytes 29360 | tf_op jit(solution)/shard_map/pallas_call | solution.py:485
  109.2 0.0 collective-permute-done.14.refs_2_
  109.2 0.5 collective-permute-start.15
  109.7 1.6 %collective-permute-start.19 = (bf16[160,1536]{1,0:T(8,128)(2,1)S(1)}, bf16[160,1536]{1,0:T(8,128)(2,1)S(1)}, u32[]{:S(2)}, u32[]{:S(2)}) collective-permute-start(bf16[160,1536]{1,0:T(8,128)(2,1)S(1)} %get-tuple-element.86.part_ref.refs_4_), channel_id=1, source_target_pairs={{0,8},{4,12},{8,0},{12,4},{1,9},{5,13},{9,1},{13,5},{2,10},{6,14},... | collective-permute-start | bytes 1474568 | tf_op jit(solution)/shard_map/ppermute | solution.py:603
  111.4 0.0 collective-permute-done.13.refs_1_
  111.4 0.0 collective-permute-start.18
  111.4 0.0 collective-permute-done.15.refs_3_
  111.4 0.0 collective-permute-done.16.refs_5_
  111.4 0.0 collective-permute-done.17.refs_7_
  111.4 7.8 %shard_map.121 = bf16[512,4096]{1,0:T(8,128)(2,1)} custom-call(s32[1]{0:T(128)} %bitcast.1.place_ref, s32[4,160]{1,0:T(4,128)S(1)} %copy-done.7, bf16[160,1664]{1,0:T(8,128)(2,1)S(1)} %shard_map.119.refs_0_, bf16[160,1664]{1,0:T(8,128)(2,1)S(1)} %collective-permute-done.13.refs_1_, bf16[160,1664]{1,0:T(8,128)(2,1)S(1)} %collective-permute-done.14.refs_2_, ...), custom_call_target="tpu_custom_call" | custom-call | flops 2684354 | bytes 9437 | tf_op jit(solution)/shard_map/pallas_call | solution.py:558
  119.2 2.7 %shard_map.122 = bf16[320,1536]{1,0:T(8,128)(2,1)} custom-call(s32[1]{0:T(128)} %bitcast.1.place_ref, s32[4,4]{1,0:T(4,128)S(1)} %copy-done.6, bf16[160,1664]{1,0:T(8,128)(2,1)S(1)} %shard_map.119.refs_0_, bf16[160,1664]{1,0:T(8,128)(2,1)S(1)} %collective-permute-done.13.refs_1_, bf16[160,1664]{1,0:T(8,128)(2,1)S(1)} %collective-permute-done.14.refs_2_, ...), custom_call_target="tpu_custom_call" | custom-call | flops 629145 | bytes 3932 | tf_op jit(solution)/shard_map/pallas_call | solution.py:590
  122.0 1.0 collective-permute-done.19.refs_6_
  122.9 0.0 collective-permute-start.20
  122.9 0.0 collective-permute-done.18.refs_5_
  122.9 1.9 %collective-permute-done.20.refs_7_ = bf16[160,1536]{1,0:T(8,128)(2,1)S(1)} collective-permute-done((bf16[160,1536]{1,0:T(8,128)(2,1)S(1)}, bf16[160,1536]{1,0:T(8,128)(2,1)S(1)}, u32[]{:S(2)}, u32[]{:S(2)}) %collective-permute-start.20) | collective-permute-done | bytes 491552 | tf_op jit(solution)/shard_map/ppermute | solution.py:603
  124.8 3.4 %shard_map.123 = bf16[512,1536]{1,0:T(8,128)(2,1)} custom-call(s32[1]{0:T(128)} %bitcast.1.place_ref, s32[4,160]{1,0:T(4,128)S(1)} %copy-done.7, bf16[160,1664]{1,0:T(8,128)(2,1)S(1)} %shard_map.119.refs_0_, bf16[160,1664]{1,0:T(8,128)(2,1)S(1)} %collective-permute-done.13.refs_1_, bf16[160,1664]{1,0:T(8,128)(2,1)S(1)} %collective-permute-done.14.refs_2_, ...), custom_call_target="tpu_custom_call" | custom-call | flops 1006632 | bytes 3538 | tf_op jit(solution)/shard_map/pallas_call | solution.py:558
  (20 shorter events, 0.1 us)
Async XLA Ops:
  3.5 11.8 %collective-permute-start = (bf16[80,1536]{1,0:T(8,128)(2,1)}, bf16[80,1536]{1,0:T(8,128)(2,1)S(1)}, u32[]{:S(2)}, u32[]{:S(2)}) collective-permute-start(bf16[80,1536]{1,0:T(8,128)(2,1)} %get-tuple-element.47), channel_id=1, source_target_pairs={{0,4},{4,0},{8,12},{12,8},{1,5},{5,1},{9,13},{13,9},{2,6},{6,2},{1... | collective-permute-start | bytes 737288 | tf_op jit(solution)/shard_map/ppermute | solution.py:603
  3.9 11.4 %collective-permute-start.1 = (bf16[80,1536]{1,0:T(8,128)(2,1)}, bf16[80,1536]{1,0:T(8,128)(2,1)S(1)}, u32[]{:S(2)}, u32[]{:S(2)}) collective-permute-start(bf16[80,1536]{1,0:T(8,128)(2,1)} %get-tuple-element.48), channel_id=1, source_target_pairs={{0,8},{4,12},{8,0},{12,4},{1,9},{5,13},{9,1},{13,5},{2,10},{6,14},... | collective-permute-start | bytes 737288 | tf_op jit(solution)/shard_map/ppermute | solution.py:603
  6.4 11.8 %collective-permute-start.2 = (bf16[80,1536]{1,0:T(8,128)(2,1)}, bf16[80,1536]{1,0:T(8,128)(2,1)S(1)}, u32[]{:S(2)}, u32[]{:S(2)}) collective-permute-start(bf16[80,1536]{1,0:T(8,128)(2,1)} %get-tuple-element.49), channel_id=1, source_target_pairs={{0,12},{4,8},{8,4},{12,0},{1,13},{5,9},{9,5},{13,1},{2,14},{6,10},... | collective-permute-start | bytes 737288 | tf_op jit(solution)/shard_map/ppermute | solution.py:603
  15.3 14.1 %copy-start.1 = (bf16[80,1536]{1,0:T(8,128)(2,1)}, bf16[80,1536]{1,0:T(8,128)(2,1)S(1)}, u32[]{:S(2)}) copy-start(bf16[80,1536]{1,0:T(8,128)(2,1)S(1)} %collective-permute-done.1.refs_1_) | copy-start | bytes 737284
  18.3 11.2 %copy-start.3 = (bf16[80,1536]{1,0:T(8,128)(2,1)}, bf16[80,1536]{1,0:T(8,128)(2,1)S(1)}, u32[]{:S(2)}) copy-start(bf16[80,1536]{1,0:T(8,128)(2,1)S(1)} %collective-permute-done.2.refs_2_) | copy-start | bytes 737284
  18.3 54.5 %collective-permute-start.9 = (bf16[160,4096]{1,0:T(8,128)(2,1)}, bf16[160,4096]{1,0:T(8,128)(2,1)}, u32[]{:S(2)}, u32[]{:S(2)}) collective-permute-start(bf16[160,4096]{1,0:T(8,128)(2,1)} %refs_4_.1), channel_id=1, source_target_pairs={{0,8},{4,12},{8,0},{12,4},{1,9},{5,13},{9,1},{13,5},{2,10},{6,14},... | collective-permute-start | bytes 3932168 | tf_op jit(solution)/shard_map/ppermute | solution.py:603
  19.8 20.2 %collective-permute-start.4 = (bf16[160,1536]{1,0:T(8,128)(2,1)}, bf16[160,1536]{1,0:T(8,128)(2,1)}, u32[]{:S(2)}, u32[]{:S(2)}) collective-permute-start(bf16[160,1536]{1,0:T(8,128)(2,1)} %get-tuple-element.52), channel_id=1, source_target_pairs={{0,1},{1,0},{2,3},{3,2},{4,5},{5,4},{6,7},{7,6},{8,9},{9,8},{10,11... | collective-permute-start | bytes 1474568 | tf_op jit(solution)/shard_map/ppermute | solution.py:603
  21.4 8.6 %slice-start = ((s8[6291456]{0:T(1024)(128)(4,1)}), s8[4194304]{0:T(1024)(128)(4,1)S(1)}, s32[]{:S(2)}) async-start(s8[6291456]{0:T(1024)(128)(4,1)} %bitcast.13), calls=%async_computation | async-start | bytes 8388608
  21.4 8.6 %slice-start.1 = ((s8[6291456]{0:T(1024)(128)(4,1)}), s8[2097152]{0:T(1024)(128)(4,1)S(1)}, s32[]{:S(2)}) async-start(s8[6291456]{0:T(1024)(128)(4,1)} %bitcast.13), calls=%async_computation.1 | async-start | bytes 4194304
  21.4 8.6 %copy-start = (bf16[320,1536]{1,0:T(8,128)(2,1)S(1)}, bf16[320,1536]{1,0:T(8,128)(2,1)}, u32[]{:S(2)}) copy-start(bf16[320,1536]{1,0:T(8,128)(2,1)} %rows_ref.3) | copy-start | bytes 2949124
  21.4 8.6 %copy-start.5 = (s32[4,160]{1,0:T(4,128)S(1)}, s32[4,160]{1,0:T(4,128)}, u32[]{:S(2)}) copy-start(s32[4,160]{1,0:T(4,128)} %get-tuple-element.46.tenant_ref.refs_3_) | copy-start | bytes 7684
  21.4 8.6 %copy-start.6 = (s32[4,4]{1,0:T(4,128)S(1)}, s32[4,4]{1,0:T(4,128)}, u32[]{:S(2)}) copy-start(s32[4,4]{1,0:T(4,128)} %handoff_ref.5) | copy-start | bytes 196
  29.5 26.6 %collective-permute-start.5 = (bf16[160,1536]{1,0:T(8,128)(2,1)S(1)}, bf16[160,1536]{1,0:T(8,128)(2,1)}, u32[]{:S(2)}, u32[]{:S(2)}) collective-permute-start(bf16[160,1536]{1,0:T(8,128)(2,1)S(1)} %shard_map.113), channel_id=1, source_target_pairs={{0,1},{1,0},{2,3},{3,2},{4,5},{5,4},{6,7},{7,6},{8,9},{9,8},{10,11... | collective-permute-start | bytes 1474568 | tf_op jit(solution)/shard_map/ppermute | solution.py:603
  30.0 0.9 copy-start.2
  31.0 0.9 copy-start.4
  35.8 29.5 %collective-permute-start.3 = (bf16[160,1536]{1,0:T(8,128)(2,1)S(1)}, bf16[160,1536]{1,0:T(8,128)(2,1)}, u32[]{:S(2)}, u32[]{:S(2)}) collective-permute-start(bf16[160,1536]{1,0:T(8,128)(2,1)S(1)} %get-tuple-element.86.part_ref.refs_4_), channel_id=1, source_target_pairs={{0,2},{1,3},{2,0},{3,1},{4,6},{5,7},{6,4},{7,5},{8,10},{9,11},{10,... | collective-permute-start | bytes 1474568 | tf_op jit(solution)/shard_map/ppermute | solution.py:603
  38.5 34.3 %collective-permute-start.7 = (bf16[160,1536]{1,0:T(8,128)(2,1)S(1)}, bf16[160,1536]{1,0:T(8,128)(2,1)}, u32[]{:S(2)}, u32[]{:S(2)}) collective-permute-start(bf16[160,1536]{1,0:T(8,128)(2,1)S(1)} %get-tuple-element.86.part_ref.refs_4_), channel_id=1, source_target_pairs={{0,1},{1,0},{2,3},{3,2},{4,5},{5,4},{6,7},{7,6},{8,9},{9,8},{10,11... | collective-permute-start | bytes 1474568 | tf_op jit(solution)/shard_map/ppermute | solution.py:603
  47.1 43.5 %collective-permute-start.8 = (bf16[160,1536]{1,0:T(8,128)(2,1)S(1)}, bf16[160,1536]{1,0:T(8,128)(2,1)S(1)}, u32[]{:S(2)}, u32[]{:S(2)}) collective-permute-start(bf16[160,1536]{1,0:T(8,128)(2,1)S(1)} %shard_map.115), channel_id=1, source_target_pairs={{0,2},{1,3},{2,0},{3,1},{4,6},{5,7},{6,4},{7,5},{8,10},{9,11},{10,... | collective-permute-start | bytes 1474568 | tf_op jit(solution)/shard_map/ppermute | solution.py:603
  65.3 25.3 %collective-permute-start.6 = (bf16[160,1536]{1,0:T(8,128)(2,1)}, bf16[160,1536]{1,0:T(8,128)(2,1)S(1)}, u32[]{:S(2)}, u32[]{:S(2)}) collective-permute-start(bf16[160,1536]{1,0:T(8,128)(2,1)} %collective-permute-done.3.refs_1_), channel_id=1, source_target_pairs={{0,1},{1,0},{2,3},{3,2},{4,5},{5,4},{6,7},{7,6},{8,9},{9,8},{10,11... | collective-permute-start | bytes 1474568 | tf_op jit(solution)/shard_map/ppermute | solution.py:603
  72.8 17.9 %collective-permute-start.12 = (f32[160,128]{1,0:T(8,128)S(1)}, f32[160,128]{1,0:T(8,128)S(1)}, u32[]{:S(2)}, u32[]{:S(2)}) collective-permute-start(f32[160,128]{1,0:T(8,128)S(1)} %shard_map.116), channel_id=1, source_target_pairs={{0,3},{1,2},{2,1},{3,0},{4,7},{5,6},{6,5},{7,4},{8,11},{9,10},{10,... | collective-permute-start | bytes 245768 | tf_op jit(solution)/shard_map/ppermute | solution.py:603
  74.1 16.5 %collective-permute-start.11 = (f32[160,128]{1,0:T(8,128)S(1)}, f32[160,128]{1,0:T(8,128)S(1)}, u32[]{:S(2)}, u32[]{:S(2)}) collective-permute-start(f32[160,128]{1,0:T(8,128)S(1)} %shard_map.116), channel_id=1, source_target_pairs={{0,2},{1,3},{2,0},{3,1},{4,6},{5,7},{6,4},{7,5},{8,10},{9,11},{10,... | collective-permute-start | bytes 245768 | tf_op jit(solution)/shard_map/ppermute | solution.py:603
  74.1 16.9 %collective-permute-start.10 = (f32[160,128]{1,0:T(8,128)S(1)}, f32[160,128]{1,0:T(8,128)S(1)}, u32[]{:S(2)}, u32[]{:S(2)}) collective-permute-start(f32[160,128]{1,0:T(8,128)S(1)} %shard_map.116), channel_id=1, source_target_pairs={{0,1},{1,0},{2,3},{3,2},{4,5},{5,4},{6,7},{7,6},{8,9},{9,8},{10,11... | collective-permute-start | bytes 245768 | tf_op jit(solution)/shard_map/ppermute | solution.py:603
  77.2 13.9 %slice-start.2 = ((s8[6291456]{0:T(1024)(128)(4,1)}), s8[4194304]{0:T(1024)(128)(4,1)S(1)}, s32[]{:S(2)}) async-start(s8[6291456]{0:T(1024)(128)(4,1)} %bitcast.16), calls=%async_computation.2 | async-start | bytes 8388608
  77.2 13.9 %slice-start.3 = ((s8[6291456]{0:T(1024)(128)(4,1)}), s8[2097152]{0:T(1024)(128)(4,1)S(1)}, s32[]{:S(2)}) async-start(s8[6291456]{0:T(1024)(128)(4,1)} %bitcast.16), calls=%async_computation.3 | async-start | bytes 4194304
  93.6 17.8 %copy-start.7 = (s32[4,160]{1,0:T(4,128)S(1)}, s32[4,160]{1,0:T(4,128)}, u32[]{:S(2)}) copy-start(s32[4,160]{1,0:T(4,128)} %get-tuple-element.70.slot_ref) | copy-start | bytes 7684
  93.7 17.7 %collective-permute-start.16 = (bf16[160,4096]{1,0:T(8,128)(2,1)}, bf16[160,4096]{1,0:T(8,128)(2,1)S(1)}, u32[]{:S(2)}, u32[]{:S(2)}) collective-permute-start(bf16[160,4096]{1,0:T(8,128)(2,1)} %refs_4_.1), channel_id=1, source_target_pairs={{0,4},{4,0},{8,12},{12,8},{1,5},{5,1},{9,13},{13,9},{2,6},{6,2},{1... | collective-permute-start | bytes 3932168 | tf_op jit(solution)/shard_map/ppermute | solution.py:603
  93.7 17.7 %collective-permute-start.17 = (bf16[160,4096]{1,0:T(8,128)(2,1)}, bf16[160,4096]{1,0:T(8,128)(2,1)S(1)}, u32[]{:S(2)}, u32[]{:S(2)}) collective-permute-start(bf16[160,4096]{1,0:T(8,128)(2,1)} %collective-permute-done.9.refs_6_), channel_id=1, source_target_pairs={{0,4},{4,0},{8,12},{12,8},{1,5},{5,1},{9,13},{13,9},{2,6},{6,2},{1... | collective-permute-start | bytes 3932168 | tf_op jit(solution)/shard_map/ppermute | solution.py:603
  94.2 15.0 %collective-permute-start.14 = (bf16[160,1664]{1,0:T(8,128)(2,1)S(1)}, bf16[160,1664]{1,0:T(8,128)(2,1)S(1)}, u32[]{:S(2)}, u32[]{:S(2)}) collective-permute-start(bf16[160,1664]{1,0:T(8,128)(2,1)S(1)} %shard_map.119.refs_0_), channel_id=1, source_target_pairs={{0,8},{4,12},{8,0},{12,4},{1,9},{5,13},{9,1},{13,5},{2,10},{6,14},... | collective-permute-start | bytes 1597448 | tf_op jit(solution)/shard_map/ppermute | solution.py:603
  94.6 16.8 %collective-permute-start.13 = (bf16[160,1664]{1,0:T(8,128)(2,1)S(1)}, bf16[160,1664]{1,0:T(8,128)(2,1)S(1)}, u32[]{:S(2)}, u32[]{:S(2)}) collective-permute-start(bf16[160,1664]{1,0:T(8,128)(2,1)S(1)} %shard_map.119.refs_0_), channel_id=1, source_target_pairs={{0,4},{4,0},{8,12},{12,8},{1,5},{5,1},{9,13},{13,9},{2,6},{6,2},{1... | collective-permute-start | bytes 1597448 | tf_op jit(solution)/shard_map/ppermute | solution.py:603
  109.2 2.2 %collective-permute-start.15 = (bf16[160,1664]{1,0:T(8,128)(2,1)S(1)}, bf16[160,1664]{1,0:T(8,128)(2,1)S(1)}, u32[]{:S(2)}, u32[]{:S(2)}) collective-permute-start(bf16[160,1664]{1,0:T(8,128)(2,1)S(1)} %collective-permute-done.14.refs_2_), channel_id=1, source_target_pairs={{0,4},{4,0},{8,12},{12,8},{1,5},{5,1},{9,13},{13,9},{2,6},{6,2},{1... | collective-permute-start | bytes 1597448 | tf_op jit(solution)/shard_map/ppermute | solution.py:603
  109.7 13.2 %collective-permute-start.19 = (bf16[160,1536]{1,0:T(8,128)(2,1)S(1)}, bf16[160,1536]{1,0:T(8,128)(2,1)S(1)}, u32[]{:S(2)}, u32[]{:S(2)}) collective-permute-start(bf16[160,1536]{1,0:T(8,128)(2,1)S(1)} %get-tuple-element.86.part_ref.refs_4_), channel_id=1, source_target_pairs={{0,8},{4,12},{8,0},{12,4},{1,9},{5,13},{9,1},{13,5},{2,10},{6,14},... | collective-permute-start | bytes 1474568 | tf_op jit(solution)/shard_map/ppermute | solution.py:603
  111.4 11.6 %collective-permute-start.18 = (bf16[160,1536]{1,0:T(8,128)(2,1)S(1)}, bf16[160,1536]{1,0:T(8,128)(2,1)S(1)}, u32[]{:S(2)}, u32[]{:S(2)}) collective-permute-start(bf16[160,1536]{1,0:T(8,128)(2,1)S(1)} %get-tuple-element.86.part_ref.refs_4_), channel_id=1, source_target_pairs={{0,4},{4,0},{8,12},{12,8},{1,5},{5,1},{9,13},{13,9},{2,6},{6,2},{1... | collective-permute-start | bytes 1474568 | tf_op jit(solution)/shard_map/ppermute | solution.py:603
  122.9 1.9 %collective-permute-start.20 = (bf16[160,1536]{1,0:T(8,128)(2,1)S(1)}, bf16[160,1536]{1,0:T(8,128)(2,1)S(1)}, u32[]{:S(2)}, u32[]{:S(2)}) collective-permute-start(bf16[160,1536]{1,0:T(8,128)(2,1)S(1)} %collective-permute-done.19.refs_6_), channel_id=1, source_target_pairs={{0,4},{4,0},{8,12},{12,8},{1,5},{5,1},{9,13},{13,9},{2,6},{6,2},{1... | collective-permute-start | bytes 1474568 | tf_op jit(solution)/shard_map/ppermute | solution.py:603

commit v5 on v4

--- a/solution.py
+++ b/solution.py
@@ -657,7 +657,7 @@
     diagonal = swap(after(pair, first), "fsdp", 1)
     gathered_x = swap(after(gathered, first, cot_x), "dp", 2)
     second = forward(
-        jnp.stack([owner[1], owner[2]]), [beside, pair], after(frozen_weight, first), 512, first
+        jnp.stack([owner[1], owner[2]]), [beside, pair], after(frozen_weight, first), 1024, first
     )
     scale = jnp.where(jnp.arange(2 * rank) < rank, 1.0, adapter_scale).astype(F32)
     ranks = ((after(partial, second, from_pair) + sums[0] + (sums[1] + sums[2])) * scale).astype(BF)
@@ -671,11 +671,11 @@
         swap(after(cot_x, bundle), "dp", 1),
     ]
     outputs = forward(
-        owner[3].reshape(1), [diagonal], after(frozen_weight, bundle), 512, second, tenant, ranks, up
+        owner[3].reshape(1), [diagonal], after(frozen_weight, bundle), 1024, second, tenant, ranks, up
     )
     bundles = [bundle, bundle_c, bundle_x, swap(after(bundle_x, outputs), "dp", 1)]
     grad_b = owned_gradient(
-        place, slot, after(bundles, outputs), False, cot_all, share, 2 * rank, adapter_scale, 1024
+        place, slot, after(bundles, outputs), False, cot_all, share, 2 * rank, adapter_scale, 2048
     )
     row_grad = bring_home(place, handoff_counts, after(bundles, grad_b), capacity, width)
     gathered_all = [
@@ -685,7 +685,7 @@
         swap(after(gathered_x, row_grad), "dp", 1),
     ]
     grad_a = owned_gradient(
-        place, slot, after(bundles, row_grad), True, gathered_all, share, 2 * rank, 1.0, 512
+        place, slot, after(bundles, row_grad), True, gathered_all, share, 2 * rank, 1.0, 768
     )
     return (
         outputs,

time: 129 us -> 128 us (level)
  Pallas kernels: 92.9 us -> 89.3 us
  waiting for transfers between devices: 13.1 us -> 16.6 us
    ppermute x21, waiting for transfers between devices: 13.1 us -> 16.6 us  [swap(): return lax.ppermute(values, axis, [(i, i ^ distance) for i in range(size)])]
    pallas_call x2, Pallas kernels: 28.1 us -> 24.7 us  [forward(): pl.pallas_call(kernel, grid_spec=pltpu.PrefetchScalarGridSpec(num_scalar_...]
  transfers between devices with their start and end apart: 21 -> 21, of which waited for: 5 -> 9; matrix products, arithmetic and copies ran while one was open for 0% -> 0% of each run, Pallas kernels for 66% -> 63%
where the time goes in v5:
time: 128 us; the launch traced here: 127 us
  Pallas kernels  89.3 us (70%)
  starting transfers between devices  18.4 us (14%)
  waiting for transfers between devices  16.6 us (13%)
  local copies, waits for them, and re-layouts  1.93 us (2%)
    pallas_call x2, Pallas kernels, forward(): pl.pallas_call(kernel, grid_spec=pltpu.PrefetchScalarGridSpec(num_scalar_...  24.7 us
    ppermute x21, starting transfers between devices, swap(): return lax.ppermute(values, axis, [(i, i ^ distance) for i in range(size)])  18.4 us
    ppermute x21, waiting for transfers between devices, swap(): return lax.ppermute(values, axis, [(i, i ^ distance) for i in range(size)])  16.6 us
    pallas_call x2, Pallas kernels, base_gradient(): pl.pallas_call(kernel, grid_spec=pltpu.PrefetchScalarGridSpec(num_scalar_...  15.1 us
    pallas_call x2, Pallas kernels, owned_gradient(): pl.pallas_call(kernel, grid=(width // block,), in_specs=[SMEM(), whole(sl...  11 us
    pallas_call x1, Pallas kernels, own_and_forward(): pl.pallas_call(kernel, grid_spec=pltpu.PrefetchScalarGridSpec(num_scalar_...  9.21 us
    pallas_call x1, Pallas kernels, turn_and_far(): pl.pallas_call(kernel, grid_spec=pltpu.PrefetchScalarGridSpec(num_scalar_...  8.77 us
    pallas_call x1, Pallas kernels, rank_backward(): pl.pallas_call(kernel, grid=(steps,), in_specs=[whole(tenant.shape), whol...  8.51 us
  transfers between devices with their start and end apart: 21, of which 9 were waited for; matrix products, arithmetic and copies ran while one was open for 0% of the time, Pallas kernels for 63%

profile of v5, /device:TPU:0, one launch (start us, length us, event | category | flops | bytes accessed | tf_op | source)
XLA Modules:
  0.0 127.2 jit_solution(5695286743211924563)
XLA Ops:
  0.6 2.8 %shard_map.111 = (bf16[80,1536]{1,0:T(8,128)(2,1)}, bf16[80,1536]{1,0:T(8,128)(2,1)}, bf16[80,1536]{1,0:T(8,128)(2,1)}, s32[4,160]{1,0:T(4,128)}, s32[4,160]{1,0:T(4,128)}) custom-call(s32[1]{0:T(128)} %bitcast.1.place_ref, s32[4,4]{1,0:T(4,128)} %handoff_ref.5, s32[32]{0:T(128)} %slots_ref.1, s32[4,32]{1,0:T(4,128)} %counts_ref.1, bf16[320,1536]{1,0:T(8,128)(2,1)} %rows_ref.3), custom_call_target="tpu_custom_call" | custom-call | flops 235929 | bytes 1966 | tf_op jit(solution)/shard_map/pallas_call | solution.py:232
  3.5 0.5 collective-permute-start
  3.9 2.5 %collective-permute-start.1 = (bf16[80,1536]{1,0:T(8,128)(2,1)}, bf16[80,1536]{1,0:T(8,128)(2,1)S(1)}, u32[]{:S(2)}, u32[]{:S(2)}) collective-permute-start(bf16[80,1536]{1,0:T(8,128)(2,1)} %get-tuple-element.48), channel_id=1, source_target_pairs={{0,8},{4,12},{8,0},{12,4},{1,9},{5,13},{9,1},{13,5},{2,10},{6,14},... | collective-permute-start | bytes 737288 | tf_op jit(solution)/shard_map/ppermute | solution.py:603
  6.4 0.1 collective-permute-start.2
  6.5 8.8 %shard_map.112 = (bf16[160,1536]{1,0:T(8,128)(2,1)}, bf16[4096,160]{1,0:T(8,128)(2,1)S(1)}) custom-call(s32[1]{0:T(128)} %bitcast.owner_ref.owners_ref, bf16[160,4096]{1,0:T(8,128)(2,1)} %refs_4_.1, bf16[6144,4096]{1,0:T(8,128)(2,1)} %refs_1_), custom_call_target="tpu_custom_call" | custom-call | flops 2013265 | bytes 12582 | tf_op jit(solution)/shard_map/pallas_call | solution.py:377
  15.3 0.0 collective-permute-done.refs_0_
  15.3 0.0 collective-permute-done.1.refs_1_
  15.3 0.0 copy-start.1
  15.3 2.9 %collective-permute-done.2.refs_2_ = bf16[80,1536]{1,0:T(8,128)(2,1)S(1)} collective-permute-done((bf16[80,1536]{1,0:T(8,128)(2,1)}, bf16[80,1536]{1,0:T(8,128)(2,1)S(1)}, u32[]{:S(2)}, u32[]{:S(2)}) %collective-permute-start.2) | collective-permute-done | bytes 245792 | tf_op jit(solution)/shard_map/ppermute | solution.py:603
  18.3 1.5 %collective-permute-start.9 = (bf16[160,4096]{1,0:T(8,128)(2,1)}, bf16[160,4096]{1,0:T(8,128)(2,1)}, u32[]{:S(2)}, u32[]{:S(2)}) collective-permute-start(bf16[160,4096]{1,0:T(8,128)(2,1)} %refs_4_.1), channel_id=1, source_target_pairs={{0,8},{4,12},{8,0},{12,4},{1,9},{5,13},{9,1},{13,5},{2,10},{6,14},... | collective-permute-start | bytes 3932168 | tf_op jit(solution)/shard_map/ppermute | solution.py:603
  19.8 1.6 %collective-permute-start.4 = (bf16[160,1536]{1,0:T(8,128)(2,1)}, bf16[160,1536]{1,0:T(8,128)(2,1)}, u32[]{:S(2)}, u32[]{:S(2)}) collective-permute-start(bf16[160,1536]{1,0:T(8,128)(2,1)} %get-tuple-element.52), channel_id=1, source_target_pairs={{0,1},{1,0},{2,3},{3,2},{4,5},{5,4},{6,7},{7,6},{8,9},{9,8},{10,11... | collective-permute-start | bytes 1474568 | tf_op jit(solution)/shard_map/ppermute | solution.py:603
  21.4 0.0 copy-start.6
  21.4 8.0 %shard_map.113 = bf16[160,1536]{1,0:T(8,128)(2,1)S(1)} custom-call(s32[1]{0:T(128)} %bitcast.4.owner_ref, bf16[4096,160]{1,0:T(8,128)(2,1)S(1)} %get-tuple-element.51.turned_ref, bf16[6144,4096]{1,0:T(8,128)(2,1)} %refs_1_), custom_call_target="tpu_custom_call" | custom-call | flops 2013265 | bytes 12582 | tf_op jit(solution)/shard_map/pallas_call | solution.py:348
  29.5 0.5 collective-permute-start.5
  30.0 0.0 copy-done.5
  30.0 0.0 copy-done.6
  30.0 0.0 copy-start.2
  30.0 0.9 copy-done.2
  31.0 0.9 copy-done.4
  31.9 3.9 %shard_map.114 = (bf16[160,1536]{1,0:T(8,128)(2,1)S(1)}, f32[64,160]{1,0:T(8,128)S(1)}) custom-call(s32[1]{0:T(128)} %bitcast.1.place_ref, s32[4,4]{1,0:T(4,128)S(1)} %copy-done.6, s32[4,160]{1,0:T(4,128)S(1)} %copy-done.5, bf16[320,1536]{1,0:T(8,128)(2,1)S(1)} %copy-done, bf16[80,1536]{1,0:T(8,128)(2,1)S(1)} %collective-permute-done.refs_0_, ...), custom_call_target="tpu_custom_call" | custom-call | flops 1006632 | bytes 7766 | tf_op jit(solution)/shard_map/pallas_call | solution.py:285
  35.8 2.6 %collective-permute-start.3 = (bf16[160,1536]{1,0:T(8,128)(2,1)S(1)}, bf16[160,1536]{1,0:T(8,128)(2,1)}, u32[]{:S(2)}, u32[]{:S(2)}) collective-permute-start(bf16[160,1536]{1,0:T(8,128)(2,1)S(1)} %get-tuple-element.86.part_ref.refs_4_), channel_id=1, source_target_pairs={{0,2},{1,3},{2,0},{3,1},{4,6},{5,7},{6,4},{7,5},{8,10},{9,11},{10,... | collective-permute-start | bytes 1474568 | tf_op jit(solution)/shard_map/ppermute | solution.py:603
  38.5 1.6 %collective-permute-start.7 = (bf16[160,1536]{1,0:T(8,128)(2,1)S(1)}, bf16[160,1536]{1,0:T(8,128)(2,1)}, u32[]{:S(2)}, u32[]{:S(2)}) collective-permute-start(bf16[160,1536]{1,0:T(8,128)(2,1)S(1)} %get-tuple-element.86.part_ref.refs_4_), channel_id=1, source_target_pairs={{0,1},{1,0},{2,3},{3,2},{4,5},{5,4},{6,7},{7,6},{8,9},{9,8},{10,11... | collective-permute-start | bytes 1474568 | tf_op jit(solution)/shard_map/ppermute | solution.py:603
  40.0 0.0 collective-permute-done.4.refs_0_
  40.0 7.1 %shard_map.115 = bf16[160,1536]{1,0:T(8,128)(2,1)S(1)} custom-call(s32[1]{0:T(128)} %bitcast.7.owner_ref, bf16[4096,160]{1,0:T(8,128)(2,1)S(1)} %get-tuple-element.51.turned_ref, bf16[6144,4096]{1,0:T(8,128)(2,1)} %refs_1_, bf16[160,1536]{1,0:T(8,128)(2,1)} %collective-permute-done.4.refs_0_), custom_call_target="tpu_custom_call" | custom-call | flops 2013265 | bytes 12582 | tf_op jit(solution)/shard_map/pallas_call | solution.py:348
  47.1 0.4 collective-permute-start.8
  47.5 8.5 %shard_map.116 = f32[160,128]{1,0:T(8,128)S(1)} custom-call(s32[4,160]{1,0:T(4,128)S(1)} %copy-done.5, bf16[4096,160]{1,0:T(8,128)(2,1)S(1)} %get-tuple-element.51.turned_ref, f32[64,160]{1,0:T(8,128)S(1)} %get-tuple-element.56.lowered_ref, bf16[2048,4096]{1,0:T(8,128)(2,1)} %bitcast.19), custom_call_target="tpu_custom_call" | custom-call | flops 2684354 | bytes 16777 | tf_op jit(solution)/shard_map/pallas_call | solution.py:322
  56.1 0.0 collective-permute-done.5.refs_1_
  56.1 9.2 %shard_map.117 = (f32[160,4096]{1,0:T(8,128)S(1)}, bf16[160,1536]{1,0:T(8,128)(2,1)S(1)}) custom-call(s32[1]{0:T(128)} %bitcast.5.owner_ref, bf16[160,1536]{1,0:T(8,128)(2,1)S(1)} %get-tuple-element.86.part_ref.refs_4_, bf16[4096,160]{1,0:T(8,128)(2,1)S(1)} %get-tuple-element.51.turned_ref, bf16[6144,4096]{1,0:T(8,128)(2,1)} %refs_1_), custom_call_target="tpu_custom_call" | custom-call | flops 4026531 | bytes 12582 | tf_op jit(solution)/shard_map/pallas_call | solution.py:427
  65.3 0.0 collective-permute-done.3.refs_1_
  65.3 0.5 collective-permute-start.6
  65.8 0.1 pad_add_fusion.owners_ref
  65.9 6.9 %collective-permute-done.7.refs_0_ = bf16[160,1536]{1,0:T(8,128)(2,1)} collective-permute-done((bf16[160,1536]{1,0:T(8,128)(2,1)S(1)}, bf16[160,1536]{1,0:T(8,128)(2,1)}, u32[]{:S(2)}, u32[]{:S(2)}) %collective-permute-start.7) | collective-permute-done | bytes 491552 | tf_op jit(solution)/shard_map/ppermute | solution.py:603
  72.8 0.0 collective-permute-done.9.refs_6_
  72.8 1.4 %collective-permute-start.12 = (f32[160,128]{1,0:T(8,128)S(1)}, f32[160,128]{1,0:T(8,128)S(1)}, u32[]{:S(2)}, u32[]{:S(2)}) collective-permute-start(f32[160,128]{1,0:T(8,128)S(1)} %shard_map.116), channel_id=1, source_target_pairs={{0,3},{1,2},{2,1},{3,0},{4,7},{5,6},{6,5},{7,4},{8,11},{9,10},{10,... | collective-permute-start | bytes 245768 | tf_op jit(solution)/shard_map/ppermute | solution.py:603
  74.1 0.0 collective-permute-start.11
  74.1 3.0 %collective-permute-start.10 = (f32[160,128]{1,0:T(8,128)S(1)}, f32[160,128]{1,0:T(8,128)S(1)}, u32[]{:S(2)}, u32[]{:S(2)}) collective-permute-start(f32[160,128]{1,0:T(8,128)S(1)} %shard_map.116), channel_id=1, source_target_pairs={{0,1},{1,0},{2,3},{3,2},{4,5},{5,4},{6,7},{7,6},{8,9},{9,8},{10,11... | collective-permute-start | bytes 245768 | tf_op jit(solution)/shard_map/ppermute | solution.py:603
  77.2 12.0 %shard_map.118.refs_2_ = f32[160,4096]{1,0:T(8,128)S(1)} custom-call(s32[2]{0:T(128)S(1)} %pad_add_fusion.owners_ref, bf16[160,1536]{1,0:T(8,128)(2,1)} %collective-permute-done.7.refs_0_, bf16[160,1536]{1,0:T(8,128)(2,1)} %collective-permute-done.3.refs_1_, bf16[6144,4096]{1,0:T(8,128)(2,1)} %refs_1_, bf16[6144,4096]{1,0:T(8,128)(2,1)} %refs_1_, ...), custom_call_target="tpu_custom_call" | custom-call | flops 4026531 | bytes 25165 | tf_op jit(solution)/shard_map/pallas_call | solution.py:485
  89.1 0.0 collective-permute-done.8.refs_2_
  89.1 0.6 collective-permute-done.6.refs_0_
  89.7 0.9 collective-permute-done.12
  90.6 0.0 collective-permute-done.11
  90.6 0.4 collective-permute-done.10
  91.1 2.5 %shard_map.119.refs_0_ = bf16[160,1664]{1,0:T(8,128)(2,1)S(1)} custom-call(s32[4,160]{1,0:T(4,128)S(1)} %copy-done.5, bf16[160,128]{1,0:T(8,128)(2,1)S(1)} %multiply_convert_fusion.ranks_ref.refs_4_, bf16[2048,1536]{1,0:T(8,128)(2,1)S(1)} %bitcast.18, bf16[160,1536]{1,0:T(8,128)(2,1)S(1)} %get-tuple-element.67.refs_0_, ...), custom_call_target="tpu_custom_call" | custom-call | flops 1006632 | bytes 6291 | tf_op jit(solution)/shard_map/pallas_call | solution.py:520
  93.6 0.0 copy-start.7
  93.7 0.1 collective-permute-start.16
  93.7 0.5 collective-permute-start.17
  94.2 0.4 collective-permute-start.14
  94.6 0.0 collective-permute-start.13
  94.6 12.8 %shard_map.120 = bf16[160,4096]{1,0:T(8,128)(2,1)} custom-call(s32[1]{0:T(128)} %bitcast.owner_ref.owners_ref, bf16[160,1536]{1,0:T(8,128)(2,1)S(1)} %collective-permute-done.6.refs_0_, bf16[6144,4096]{1,0:T(8,128)(2,1)} %refs_1_, f32[160,4096]{1,0:T(8,128)S(1)} %shard_map.118.refs_2_, s32[4,160]{1,0:T(4,128)S(1)} %copy-done.5, ...), custom_call_target="tpu_custom_call" | custom-call | flops 4697620 | bytes 29360 | tf_op jit(solution)/shard_map/pallas_call | solution.py:485
  107.4 0.9 collective-permute-done.14.refs_2_
  108.3 0.0 collective-permute-start.15
  108.3 1.2 collective-permute-start.19
  109.5 0.0 collective-permute-done.13.refs_1_
  109.5 0.0 collective-permute-start.18
  109.5 0.7 collective-permute-done.15.refs_3_
  110.2 0.0 collective-permute-done.16.refs_5_
  110.2 0.0 collective-permute-done.17.refs_7_
  110.2 7.6 %shard_map.121 = bf16[512,4096]{1,0:T(8,128)(2,1)} custom-call(s32[1]{0:T(128)} %bitcast.1.place_ref, s32[4,160]{1,0:T(4,128)S(1)} %copy-done.7, bf16[160,1664]{1,0:T(8,128)(2,1)S(1)} %shard_map.119.refs_0_, bf16[160,1664]{1,0:T(8,128)(2,1)S(1)} %collective-permute-done.13.refs_1_, bf16[160,1664]{1,0:T(8,128)(2,1)S(1)} %collective-permute-done.14.refs_2_, ...), custom_call_target="tpu_custom_call" | custom-call | flops 2684354 | bytes 9437 | tf_op jit(solution)/shard_map/pallas_call | solution.py:558
  117.9 2.7 %shard_map.122 = bf16[320,1536]{1,0:T(8,128)(2,1)} custom-call(s32[1]{0:T(128)} %bitcast.1.place_ref, s32[4,4]{1,0:T(4,128)S(1)} %copy-done.6, bf16[160,1664]{1,0:T(8,128)(2,1)S(1)} %shard_map.119.refs_0_, bf16[160,1664]{1,0:T(8,128)(2,1)S(1)} %collective-permute-done.13.refs_1_, bf16[160,1664]{1,0:T(8,128)(2,1)S(1)} %collective-permute-done.14.refs_2_, ...), custom_call_target="tpu_custom_call" | custom-call | flops 629145 | bytes 3932 | tf_op jit(solution)/shard_map/pallas_call | solution.py:590
  120.6 1.3 %collective-permute-done.19.refs_6_ = bf16[160,1536]{1,0:T(8,128)(2,1)S(1)} collective-permute-done((bf16[160,1536]{1,0:T(8,128)(2,1)S(1)}, bf16[160,1536]{1,0:T(8,128)(2,1)S(1)}, u32[]{:S(2)}, u32[]{:S(2)}) %collective-permute-start.19) | collective-permute-done | bytes 491552 | tf_op jit(solution)/shard_map/ppermute | solution.py:603
  122.0 0.0 collective-permute-start.20
  122.0 0.0 collective-permute-done.18.refs_5_
  122.0 1.9 %collective-permute-done.20.refs_7_ = bf16[160,1536]{1,0:T(8,128)(2,1)S(1)} collective-permute-done((bf16[160,1536]{1,0:T(8,128)(2,1)S(1)}, bf16[160,1536]{1,0:T(8,128)(2,1)S(1)}, u32[]{:S(2)}, u32[]{:S(2)}) %collective-permute-start.20) | collective-permute-done | bytes 491552 | tf_op jit(solution)/shard_map/ppermute | solution.py:603
  123.8 3.4 %shard_map.123 = bf16[512,1536]{1,0:T(8,128)(2,1)} custom-call(s32[1]{0:T(128)} %bitcast.1.place_ref, s32[4,160]{1,0:T(4,128)S(1)} %copy-done.7, bf16[160,1664]{1,0:T(8,128)(2,1)S(1)} %shard_map.119.refs_0_, bf16[160,1664]{1,0:T(8,128)(2,1)S(1)} %collective-permute-done.13.refs_1_, bf16[160,1664]{1,0:T(8,128)(2,1)S(1)} %collective-permute-done.14.refs_2_, ...), custom_call_target="tpu_custom_call" | custom-call | flops 1006632 | bytes 3538 | tf_op jit(solution)/shard_map/pallas_call | solution.py:558
  (20 shorter events, 0.1 us)
Async XLA Ops:
  3.5 11.8 %collective-permute-start = (bf16[80,1536]{1,0:T(8,128)(2,1)}, bf16[80,1536]{1,0:T(8,128)(2,1)S(1)}, u32[]{:S(2)}, u32[]{:S(2)}) collective-permute-start(bf16[80,1536]{1,0:T(8,128)(2,1)} %get-tuple-element.47), channel_id=1, source_target_pairs={{0,4},{4,0},{8,12},{12,8},{1,5},{5,1},{9,13},{13,9},{2,6},{6,2},{1... | collective-permute-start | bytes 737288 | tf_op jit(solution)/shard_map/ppermute | solution.py:603
  3.9 11.4 %collective-permute-start.1 = (bf16[80,1536]{1,0:T(8,128)(2,1)}, bf16[80,1536]{1,0:T(8,128)(2,1)S(1)}, u32[]{:S(2)}, u32[]{:S(2)}) collective-permute-start(bf16[80,1536]{1,0:T(8,128)(2,1)} %get-tuple-element.48), channel_id=1, source_target_pairs={{0,8},{4,12},{8,0},{12,4},{1,9},{5,13},{9,1},{13,5},{2,10},{6,14},... | collective-permute-start | bytes 737288 | tf_op jit(solution)/shard_map/ppermute | solution.py:603
  6.4 11.8 %collective-permute-start.2 = (bf16[80,1536]{1,0:T(8,128)(2,1)}, bf16[80,1536]{1,0:T(8,128)(2,1)S(1)}, u32[]{:S(2)}, u32[]{:S(2)}) collective-permute-start(bf16[80,1536]{1,0:T(8,128)(2,1)} %get-tuple-element.49), channel_id=1, source_target_pairs={{0,12},{4,8},{8,4},{12,0},{1,13},{5,9},{9,5},{13,1},{2,14},{6,10},... | collective-permute-start | bytes 737288 | tf_op jit(solution)/shard_map/ppermute | solution.py:603
  15.3 14.1 %copy-start.1 = (bf16[80,1536]{1,0:T(8,128)(2,1)}, bf16[80,1536]{1,0:T(8,128)(2,1)S(1)}, u32[]{:S(2)}) copy-start(bf16[80,1536]{1,0:T(8,128)(2,1)S(1)} %collective-permute-done.1.refs_1_) | copy-start | bytes 737284
  18.3 11.2 %copy-start.3 = (bf16[80,1536]{1,0:T(8,128)(2,1)}, bf16[80,1536]{1,0:T(8,128)(2,1)S(1)}, u32[]{:S(2)}) copy-start(bf16[80,1536]{1,0:T(8,128)(2,1)S(1)} %collective-permute-done.2.refs_2_) | copy-start | bytes 737284
  18.3 54.5 %collective-permute-start.9 = (bf16[160,4096]{1,0:T(8,128)(2,1)}, bf16[160,4096]{1,0:T(8,128)(2,1)}, u32[]{:S(2)}, u32[]{:S(2)}) collective-permute-start(bf16[160,4096]{1,0:T(8,128)(2,1)} %refs_4_.1), channel_id=1, source_target_pairs={{0,8},{4,12},{8,0},{12,4},{1,9},{5,13},{9,1},{13,5},{2,10},{6,14},... | collective-permute-start | bytes 3932168 | tf_op jit(solution)/shard_map/ppermute | solution.py:603
  19.8 20.2 %collective-permute-start.4 = (bf16[160,1536]{1,0:T(8,128)(2,1)}, bf16[160,1536]{1,0:T(8,128)(2,1)}, u32[]{:S(2)}, u32[]{:S(2)}) collective-permute-start(bf16[160,1536]{1,0:T(8,128)(2,1)} %get-tuple-element.52), channel_id=1, source_target_pairs={{0,1},{1,0},{2,3},{3,2},{4,5},{5,4},{6,7},{7,6},{8,9},{9,8},{10,11... | collective-permute-start | bytes 1474568 | tf_op jit(solution)/shard_map/ppermute | solution.py:603
  21.4 8.6 %slice-start = ((s8[6291456]{0:T(1024)(128)(4,1)}), s8[4194304]{0:T(1024)(128)(4,1)S(1)}, s32[]{:S(2)}) async-start(s8[6291456]{0:T(1024)(128)(4,1)} %bitcast.13), calls=%async_computation | async-start | bytes 8388608
  21.4 8.6 %slice-start.1 = ((s8[6291456]{0:T(1024)(128)(4,1)}), s8[2097152]{0:T(1024)(128)(4,1)S(1)}, s32[]{:S(2)}) async-start(s8[6291456]{0:T(1024)(128)(4,1)} %bitcast.13), calls=%async_computation.1 | async-start | bytes 4194304
  21.4 8.6 %copy-start = (bf16[320,1536]{1,0:T(8,128)(2,1)S(1)}, bf16[320,1536]{1,0:T(8,128)(2,1)}, u32[]{:S(2)}) copy-start(bf16[320,1536]{1,0:T(8,128)(2,1)} %rows_ref.3) | copy-start | bytes 2949124
  21.4 8.6 %copy-start.5 = (s32[4,160]{1,0:T(4,128)S(1)}, s32[4,160]{1,0:T(4,128)}, u32[]{:S(2)}) copy-start(s32[4,160]{1,0:T(4,128)} %get-tuple-element.46.tenant_ref.refs_3_) | copy-start | bytes 7684
  21.4 8.6 %copy-start.6 = (s32[4,4]{1,0:T(4,128)S(1)}, s32[4,4]{1,0:T(4,128)}, u32[]{:S(2)}) copy-start(s32[4,4]{1,0:T(4,128)} %handoff_ref.5) | copy-start | bytes 196
  29.5 26.6 %collective-permute-start.5 = (bf16[160,1536]{1,0:T(8,128)(2,1)S(1)}, bf16[160,1536]{1,0:T(8,128)(2,1)}, u32[]{:S(2)}, u32[]{:S(2)}) collective-permute-start(bf16[160,1536]{1,0:T(8,128)(2,1)S(1)} %shard_map.113), channel_id=1, source_target_pairs={{0,1},{1,0},{2,3},{3,2},{4,5},{5,4},{6,7},{7,6},{8,9},{9,8},{10,11... | collective-permute-start | bytes 1474568 | tf_op jit(solution)/shard_map/ppermute | solution.py:603
  30.0 0.9 copy-start.2
  31.0 0.9 copy-start.4
  35.8 29.5 %collective-permute-start.3 = (bf16[160,1536]{1,0:T(8,128)(2,1)S(1)}, bf16[160,1536]{1,0:T(8,128)(2,1)}, u32[]{:S(2)}, u32[]{:S(2)}) collective-permute-start(bf16[160,1536]{1,0:T(8,128)(2,1)S(1)} %get-tuple-element.86.part_ref.refs_4_), channel_id=1, source_target_pairs={{0,2},{1,3},{2,0},{3,1},{4,6},{5,7},{6,4},{7,5},{8,10},{9,11},{10,... | collective-permute-start | bytes 1474568 | tf_op jit(solution)/shard_map/ppermute | solution.py:603
  38.5 34.3 %collective-permute-start.7 = (bf16[160,1536]{1,0:T(8,128)(2,1)S(1)}, bf16[160,1536]{1,0:T(8,128)(2,1)}, u32[]{:S(2)}, u32[]{:S(2)}) collective-permute-start(bf16[160,1536]{1,0:T(8,128)(2,1)S(1)} %get-tuple-element.86.part_ref.refs_4_), channel_id=1, source_target_pairs={{0,1},{1,0},{2,3},{3,2},{4,5},{5,4},{6,7},{7,6},{8,9},{9,8},{10,11... | collective-permute-start | bytes 1474568 | tf_op jit(solution)/shard_map/ppermute | solution.py:603
  47.1 42.0 %collective-permute-start.8 = (bf16[160,1536]{1,0:T(8,128)(2,1)S(1)}, bf16[160,1536]{1,0:T(8,128)(2,1)S(1)}, u32[]{:S(2)}, u32[]{:S(2)}) collective-permute-start(bf16[160,1536]{1,0:T(8,128)(2,1)S(1)} %shard_map.115), channel_id=1, source_target_pairs={{0,2},{1,3},{2,0},{3,1},{4,6},{5,7},{6,4},{7,5},{8,10},{9,11},{10,... | collective-permute-start | bytes 1474568 | tf_op jit(solution)/shard_map/ppermute | solution.py:603
  65.3 24.4 %collective-permute-start.6 = (bf16[160,1536]{1,0:T(8,128)(2,1)}, bf16[160,1536]{1,0:T(8,128)(2,1)S(1)}, u32[]{:S(2)}, u32[]{:S(2)}) collective-permute-start(bf16[160,1536]{1,0:T(8,128)(2,1)} %collective-permute-done.3.refs_1_), channel_id=1, source_target_pairs={{0,1},{1,0},{2,3},{3,2},{4,5},{5,4},{6,7},{7,6},{8,9},{9,8},{10,11... | collective-permute-start | bytes 1474568 | tf_op jit(solution)/shard_map/ppermute | solution.py:603
  72.8 17.9 %collective-permute-start.12 = (f32[160,128]{1,0:T(8,128)S(1)}, f32[160,128]{1,0:T(8,128)S(1)}, u32[]{:S(2)}, u32[]{:S(2)}) collective-permute-start(f32[160,128]{1,0:T(8,128)S(1)} %shard_map.116), channel_id=1, source_target_pairs={{0,3},{1,2},{2,1},{3,0},{4,7},{5,6},{6,5},{7,4},{8,11},{9,10},{10,... | collective-permute-start | bytes 245768 | tf_op jit(solution)/shard_map/ppermute | solution.py:603
  74.1 16.5 %collective-permute-start.11 = (f32[160,128]{1,0:T(8,128)S(1)}, f32[160,128]{1,0:T(8,128)S(1)}, u32[]{:S(2)}, u32[]{:S(2)}) collective-permute-start(f32[160,128]{1,0:T(8,128)S(1)} %shard_map.116), channel_id=1, source_target_pairs={{0,2},{1,3},{2,0},{3,1},{4,6},{5,7},{6,4},{7,5},{8,10},{9,11},{10,... | collective-permute-start | bytes 245768 | tf_op jit(solution)/shard_map/ppermute | solution.py:603
  74.1 16.9 %collective-permute-start.10 = (f32[160,128]{1,0:T(8,128)S(1)}, f32[160,128]{1,0:T(8,128)S(1)}, u32[]{:S(2)}, u32[]{:S(2)}) collective-permute-start(f32[160,128]{1,0:T(8,128)S(1)} %shard_map.116), channel_id=1, source_target_pairs={{0,1},{1,0},{2,3},{3,2},{4,5},{5,4},{6,7},{7,6},{8,9},{9,8},{10,11... | collective-permute-start | bytes 245768 | tf_op jit(solution)/shard_map/ppermute | solution.py:603
  77.2 13.9 %slice-start.2 = ((s8[6291456]{0:T(1024)(128)(4,1)}), s8[4194304]{0:T(1024)(128)(4,1)S(1)}, s32[]{:S(2)}) async-start(s8[6291456]{0:T(1024)(128)(4,1)} %bitcast.16), calls=%async_computation.2 | async-start | bytes 8388608
  77.2 13.9 %slice-start.3 = ((s8[6291456]{0:T(1024)(128)(4,1)}), s8[2097152]{0:T(1024)(128)(4,1)S(1)}, s32[]{:S(2)}) async-start(s8[6291456]{0:T(1024)(128)(4,1)} %bitcast.16), calls=%async_computation.3 | async-start | bytes 4194304
  93.6 16.6 %copy-start.7 = (s32[4,160]{1,0:T(4,128)S(1)}, s32[4,160]{1,0:T(4,128)}, u32[]{:S(2)}) copy-start(s32[4,160]{1,0:T(4,128)} %get-tuple-element.70.slot_ref) | copy-start | bytes 7684
  93.7 16.6 %collective-permute-start.16 = (bf16[160,4096]{1,0:T(8,128)(2,1)}, bf16[160,4096]{1,0:T(8,128)(2,1)S(1)}, u32[]{:S(2)}, u32[]{:S(2)}) collective-permute-start(bf16[160,4096]{1,0:T(8,128)(2,1)} %refs_4_.1), channel_id=1, source_target_pairs={{0,4},{4,0},{8,12},{12,8},{1,5},{5,1},{9,13},{13,9},{2,6},{6,2},{1... | collective-permute-start | bytes 3932168 | tf_op jit(solution)/shard_map/ppermute | solution.py:603
  93.7 16.5 %collective-permute-start.17 = (bf16[160,4096]{1,0:T(8,128)(2,1)}, bf16[160,4096]{1,0:T(8,128)(2,1)S(1)}, u32[]{:S(2)}, u32[]{:S(2)}) collective-permute-start(bf16[160,4096]{1,0:T(8,128)(2,1)} %collective-permute-done.9.refs_6_), channel_id=1, source_target_pairs={{0,4},{4,0},{8,12},{12,8},{1,5},{5,1},{9,13},{13,9},{2,6},{6,2},{1... | collective-permute-start | bytes 3932168 | tf_op jit(solution)/shard_map/ppermute | solution.py:603
  94.2 14.1 %collective-permute-start.14 = (bf16[160,1664]{1,0:T(8,128)(2,1)S(1)}, bf16[160,1664]{1,0:T(8,128)(2,1)S(1)}, u32[]{:S(2)}, u32[]{:S(2)}) collective-permute-start(bf16[160,1664]{1,0:T(8,128)(2,1)S(1)} %shard_map.119.refs_0_), channel_id=1, source_target_pairs={{0,8},{4,12},{8,0},{12,4},{1,9},{5,13},{9,1},{13,5},{2,10},{6,14},... | collective-permute-start | bytes 1597448 | tf_op jit(solution)/shard_map/ppermute | solution.py:603
  94.6 14.9 %collective-permute-start.13 = (bf16[160,1664]{1,0:T(8,128)(2,1)S(1)}, bf16[160,1664]{1,0:T(8,128)(2,1)S(1)}, u32[]{:S(2)}, u32[]{:S(2)}) collective-permute-start(bf16[160,1664]{1,0:T(8,128)(2,1)S(1)} %shard_map.119.refs_0_), channel_id=1, source_target_pairs={{0,4},{4,0},{8,12},{12,8},{1,5},{5,1},{9,13},{13,9},{2,6},{6,2},{1... | collective-permute-start | bytes 1597448 | tf_op jit(solution)/shard_map/ppermute | solution.py:603
  108.3 1.9 %collective-permute-start.15 = (bf16[160,1664]{1,0:T(8,128)(2,1)S(1)}, bf16[160,1664]{1,0:T(8,128)(2,1)S(1)}, u32[]{:S(2)}, u32[]{:S(2)}) collective-permute-start(bf16[160,1664]{1,0:T(8,128)(2,1)S(1)} %collective-permute-done.14.refs_2_), channel_id=1, source_target_pairs={{0,4},{4,0},{8,12},{12,8},{1,5},{5,1},{9,13},{13,9},{2,6},{6,2},{1... | collective-permute-start | bytes 1597448 | tf_op jit(solution)/shard_map/ppermute | solution.py:603
  108.3 13.6 %collective-permute-start.19 = (bf16[160,1536]{1,0:T(8,128)(2,1)S(1)}, bf16[160,1536]{1,0:T(8,128)(2,1)S(1)}, u32[]{:S(2)}, u32[]{:S(2)}) collective-permute-start(bf16[160,1536]{1,0:T(8,128)(2,1)S(1)} %get-tuple-element.86.part_ref.refs_4_), channel_id=1, source_target_pairs={{0,8},{4,12},{8,0},{12,4},{1,9},{5,13},{9,1},{13,5},{2,10},{6,14},... | collective-permute-start | bytes 1474568 | tf_op jit(solution)/shard_map/ppermute | solution.py:603
  109.5 12.4 %collective-permute-start.18 = (bf16[160,1536]{1,0:T(8,128)(2,1)S(1)}, bf16[160,1536]{1,0:T(8,128)(2,1)S(1)}, u32[]{:S(2)}, u32[]{:S(2)}) collective-permute-start(bf16[160,1536]{1,0:T(8,128)(2,1)S(1)} %get-tuple-element.86.part_ref.refs_4_), channel_id=1, source_target_pairs={{0,4},{4,0},{8,12},{12,8},{1,5},{5,1},{9,13},{13,9},{2,6},{6,2},{1... | collective-permute-start | bytes 1474568 | tf_op jit(solution)/shard_map/ppermute | solution.py:603
  122.0 1.9 %collective-permute-start.20 = (bf16[160,1536]{1,0:T(8,128)(2,1)S(1)}, bf16[160,1536]{1,0:T(8,128)(2,1)S(1)}, u32[]{:S(2)}, u32[]{:S(2)}) collective-permute-start(bf16[160,1536]{1,0:T(8,128)(2,1)S(1)} %collective-permute-done.19.refs_6_), channel_id=1, source_target_pairs={{0,4},{4,0},{8,12},{12,8},{1,5},{5,1},{9,13},{13,9},{2,6},{6,2},{1... | collective-permute-start | bytes 1474568 | tf_op jit(solution)/shard_map/ppermute | solution.py:603
